TPU v7x, 512 devices: a whole 4x8x8 slice. The times are simulated.
512 devices in a mesh: replica: 16 (over x, y_hi), space: 32 (over z, y_lo, core).
Axes of the slice: x: 4, y: 8 (y_hi: 4, y_lo: 2; y = y_hi * 2 + y_lo), z: 8, core: 2. Of those that a mesh axis runs over, the one named last changes fastest.
Arguments:
- particle_coordinates: float32 [16, 3, 8192], P('replica', None, 'space'), may hold values from 0 to 4
- particle_motions: float32 [16, 3, 8192], P('replica', None, 'space'), may hold values from -6 to 6
- particle_kinds: int32 [16, 8192], P('replica', 'space'), may hold values from 0 to 5
- filled_totals: int32 [16, 8192], P('replica', 'space'), may hold values from 1 to 32, as said below
- adjacent_particles: int32 [16, 32, 8192], P('replica', None, 'space'), may hold values from 0 to 511, as said below
- adjacent_place_kinds: int32 [16, 32, 8192], P('replica', None, 'space'), may hold values from 0 to 5
- border_particle_numbers: int32 [16, 4, 2048], P('replica', None, 'space'), may hold values from 0 to 255, as said below
- reciprocal_kind_inertia: float32 [6], replicated, may hold values from 0.1 to 1
- thermal_levels: float32 [16], P('replica'), may hold values from 250 to 600
- swap_mates: int32 [16], P('replica'), may hold values from 0 to 15, as said below
- bond_intake_coefficients: bfloat16 [256, 28], replicated, may hold values from -1 to 1
- bond_output_coefficients: float32 [256], replicated, may hold values from -0.375 to 0.375
- particle_opening_coefficients: bfloat16 [256, 8], replicated, may hold values from -2 to 2
- particle_middle_coefficients: bfloat16 [256, 256], replicated, may hold values from -0.375 to 0.375
- particle_output_coefficients: float32 [256], replicated, may hold values from -0.375 to 0.375
Outputs:
- positions_out: float32 [16, 3, 8192], P('replica', None, 'space')
- velocities_out: float32 [16, 3, 8192], P('replica', None, 'space')
Inputs may be any that keep to these rules, and one draw needn't show every extreme that they name: `filled_totals`: each atom's live slots are its first counts slots. `adjacent_particles`: indices into the domain's own 256 atoms followed by its four ghost sets of 64 in the order of offsets +1, -1, +2, -2; an atom's slots are distinct and never the atom itself. `border_particle_numbers`: for each offset and domain, 64 distinct own atoms of that domain. swap_mates[swap_mates[r]] = r and swap_mates[r] - r is -1, 0 or 1; every swapped pair (r, r + 1) of one draw has r of the same parity, and at least one pair swaps.
All inputs are finite; a program needn't handle non-finite values.
Results may differ from a plain program's by a relative error of at most 0.0003.
Values sent between devices are 32-bit elements; how exact they have to be, the bound alone decides.
No kernel may reach another device: no remote copies, remote signals or barrier semaphores. Data moves between devices by JAX's collectives and lax.ppermute only.
A program may use at most 64 MiB of HBM per device.

v0:
```python
import jax
import jax.numpy as jnp
from jax import lax
from jax.sharding import PartitionSpec as P

STEPS = 2


OFFSETS = (1, -1, 2, -2)
TIME_STEP = 0.05
CUT_SQ = 9.0
GROUP_SLOTS = 4


def passed_along(value, axis, by):
    size = lax.axis_size(axis)
    return lax.ppermute(value, axis, [(i, (i + by) % size) for i in range(size)])


def from_behind(value, axis, by):
    size = lax.axis_size(axis)
    pairs = [(i, i + by) for i in range(size) if 0 <= i + by < size]
    return lax.ppermute(value, axis, pairs)


def features(edge_vec, live_mask, centre_hot, neigh_hot, n_basis):
    dist_sq = jnp.sum(edge_vec * edge_vec, axis=0)
    inside = 1.0 - dist_sq / CUT_SQ
    cutoff = jnp.where(live_mask & (inside > 0.0), inside * inside, 0.0)
    centres = CUT_SQ * jnp.arange(n_basis).astype(jnp.float32) / (n_basis - 1)
    sharpness = (n_basis / CUT_SQ) ** 2
    radial = jnp.exp(-sharpness * (dist_sq[None] - centres[:, None, None]) ** 2) * cutoff[None]
    environ = jnp.sum(radial, axis=1)
    slot_len = edge_vec.shape[1]
    inputs = jnp.concatenate(
        [
            radial,
            jnp.broadcast_to(environ[:, None, :], radial.shape),
            jnp.broadcast_to(
                centre_hot[:, None, :], (centre_hot.shape[0], slot_len, centre_hot.shape[1])
            ),
            neigh_hot,
        ],
        axis=0,
    )
    return (inputs, cutoff, environ)


def edge_block(inputs, cutoff, bond_intake_coefficients, bond_output_coefficients):
    rounded = inputs.astype(jnp.bfloat16)
    pre_edge = jnp.dot(
        bond_intake_coefficients, rounded, preferred_element_type=jnp.float32
    ).astype(jnp.bfloat16)
    pre_edge = lax.optimization_barrier(pre_edge)
    pre_wide = pre_edge.astype(jnp.float32)
    sig_pre = jax.nn.sigmoid(pre_wide)
    output = jnp.sum(bond_output_coefficients[:, None] * (pre_wide * sig_pre), axis=0)
    slope_pre = sig_pre * (1.0 + pre_wide * (1.0 - sig_pre))
    g_pre = (cutoff[None, :] * bond_output_coefficients[:, None] * slope_pre).astype(jnp.bfloat16)
    g_in = jnp.dot(bond_intake_coefficients.T, g_pre, preferred_element_type=jnp.float32)
    return (g_in, output)


def atom_block(
    environ,
    particle_opening_coefficients,
    particle_middle_coefficients,
    particle_output_coefficients,
):
    env_low = environ.astype(jnp.bfloat16)
    first_pre = jnp.dot(particle_opening_coefficients, env_low, preferred_element_type=jnp.float32)
    sig_first = jax.nn.sigmoid(first_pre)
    hidden_one = (first_pre * sig_first).astype(jnp.bfloat16)
    second = jnp.dot(particle_middle_coefficients, hidden_one, preferred_element_type=jnp.float32)
    sig_second = jax.nn.sigmoid(second)
    g_second = (
        particle_output_coefficients[:, None] * sig_second * (1.0 + second * (1.0 - sig_second))
    ).astype(jnp.bfloat16)
    g_hidden = jnp.dot(particle_middle_coefficients.T, g_second, preferred_element_type=jnp.float32)
    g_first = (g_hidden * sig_first * (1.0 + first_pre * (1.0 - sig_first))).astype(jnp.bfloat16)
    return jnp.dot(particle_opening_coefficients.T, g_first, preferred_element_type=jnp.float32)


def domain_gradient(
    domain_coordinates_here, ghost_pos, neighbour_idx, atom_counts, centre_hot, neigh_hot, weights
):
    (
        bond_intake_coefficients,
        bond_output_coefficients,
        particle_opening_coefficients,
        particle_middle_coefficients,
        particle_output_coefficients,
    ) = weights
    n_basis = particle_opening_coefficients.shape[1]
    all_pos = jnp.concatenate([domain_coordinates_here, ghost_pos], axis=1)
    slot_len, atom_count = neighbour_idx.shape
    edge_vec = all_pos[:, neighbour_idx] - domain_coordinates_here[:, None, :]
    live_mask = jnp.arange(slot_len)[:, None] < atom_counts[None, :]
    (inputs, cutoff, environ), pullback = jax.vjp(
        lambda vecs: features(vecs, live_mask, centre_hot, neigh_hot, n_basis), edge_vec
    )
    feat_len = inputs.shape[0]
    group_count = slot_len // GROUP_SLOTS
    blocks_in = inputs.reshape(feat_len, group_count, GROUP_SLOTS * atom_count).transpose(1, 0, 2)
    blocks_cut = cutoff.reshape(group_count, GROUP_SLOTS * atom_count)
    group_start = jnp.arange(group_count, dtype=jnp.int32) * GROUP_SLOTS

    def run_group(items):
        return edge_block(items[0], items[1], bond_intake_coefficients, bond_output_coefficients)

    g_blocks, out_blocks = lax.map(run_group, (blocks_in, blocks_cut, group_start))
    g_in = g_blocks.transpose(1, 0, 2).reshape(feat_len, slot_len, atom_count)
    output = out_blocks.reshape(slot_len, atom_count)
    g_env = atom_block(
        environ,
        particle_opening_coefficients,
        particle_middle_coefficients,
        particle_output_coefficients,
    )
    (g_vec,) = pullback((g_in, output, g_env))
    g_all = jnp.zeros_like(all_pos).at[:, neighbour_idx].add(g_vec)
    return g_all.at[:, :atom_count].add(-jnp.sum(g_vec, axis=1))


def send_out(block, offset):
    return passed_along(block, "space", offset)


def send_back(block, offset):
    return passed_along(block, "space", offset)


def ladder(looped_bundle, offset):
    return from_behind((looped_bundle[0], looped_bundle[1], looped_bundle[2]), "replica", offset)


def on_device(
    particle_coordinates,
    particle_motions,
    particle_kinds,
    filled_totals,
    adjacent_particles,
    adjacent_place_kinds,
    border_particle_numbers,
    reciprocal_kind_inertia,
    thermal_levels,
    swap_mates,
    bond_intake_coefficients,
    bond_output_coefficients,
    particle_opening_coefficients,
    particle_middle_coefficients,
    particle_output_coefficients,
):
    weights = (
        bond_intake_coefficients,
        bond_output_coefficients,
        particle_opening_coefficients,
        particle_middle_coefficients,
        particle_output_coefficients,
    )
    domain_coordinates_here = particle_coordinates[0]
    particle_motion = particle_motions[0]
    own_species = particle_kinds[0]
    atom_counts = filled_totals[0]
    neighbour_idx = adjacent_particles[0]
    neigh_spec = adjacent_place_kinds[0]
    ghost_idx = border_particle_numbers[0]
    atom_count = domain_coordinates_here.shape[1]
    ghost_len = ghost_idx.shape[1]
    kinds = jnp.arange(reciprocal_kind_inertia.shape[0], dtype=jnp.int32)
    centre_hot = (own_species[None, :] == kinds[:, None]).astype(jnp.float32)
    neigh_hot = (neigh_spec[None] == kinds[:, None, None]).astype(jnp.float32)
    inverse = jnp.sum(centre_hot * reciprocal_kind_inertia[:, None], axis=0)
    for step_no in range(STEPS):
        outgoing = [domain_coordinates_here[:, ghost_idx[which]] for which in range(4)]
        arrived = [None, None, None, None]
        for which in range(4):
            arrived[which] = send_out(outgoing[which], OFFSETS[which])
        g_every = domain_gradient(
            domain_coordinates_here,
            jnp.concatenate(arrived, axis=1),
            neighbour_idx,
            atom_counts,
            centre_hot,
            neigh_hot,
            weights,
        )
        g_ghost = [
            g_every[:, atom_count + which * ghost_len : atom_count + (which + 1) * ghost_len]
            for which in range(4)
        ]
        returned = [None, None, None, None]
        for which in range(4):
            returned[which] = send_back(g_ghost[which], -OFFSETS[which])
        g_own = g_every[:, :atom_count]
        for which in range(4):
            g_own = g_own.at[:, ghost_idx[which]].add(returned[which])
        particle_motion = particle_motion - TIME_STEP * g_own * inverse[None, :]
        domain_coordinates_here = domain_coordinates_here + TIME_STEP * particle_motion
    looped_bundle = (domain_coordinates_here[None], particle_motion[None], thermal_levels)
    arrived_below_side = ladder(looped_bundle, 1)
    arrived_above_side = ladder(looped_bundle, -1)
    my_rank = lax.axis_index("replica")
    my_partner = swap_mates[0]
    take_below = my_partner == my_rank - 1
    take_above = my_partner == my_rank + 1

    def pick_swap_mate(below_val, above_val, own_val):
        return jnp.where(take_below, below_val, jnp.where(take_above, above_val, own_val))

    new_pos = pick_swap_mate(arrived_below_side[0], arrived_above_side[0], looped_bundle[0])
    new_vel = pick_swap_mate(arrived_below_side[1], arrived_above_side[1], looped_bundle[1])
    mate_thermal_level = pick_swap_mate(
        arrived_below_side[2], arrived_above_side[2], thermal_levels
    )
    motion_rescaling = jnp.sqrt(thermal_levels / mate_thermal_level)
    return (new_pos, new_vel * motion_rescaling[:, None, None])


def solution(mesh):
    return jax.shard_map(
        on_device,
        mesh=mesh,
        in_specs=(
            P("replica", None, "space"),
            P("replica", None, "space"),
            P("replica", "space"),
            P("replica", "space"),
            P("replica", None, "space"),
            P("replica", None, "space"),
            P("replica", None, "space"),
            P(),
            P("replica"),
            P("replica"),
            P(),
            P(),
            P(),
            P(),
            P(),
        ),
        out_specs=(P("replica", None, "space"), P("replica", None, "space")),
        check_vma=False,
    )
```

profile of v0, /device:TPU:7, one launch (start us, length us, event | category | flops | bytes accessed | tf_op | source)
XLA Modules:
  0.0 327.9 jit_solution(8002790383573894782)
XLA Ops:
  2.9 3.8 %collective-permute-start = (f32[3,64]{0,1:T(8,128)S(1)}, f32[3,64]{0,1:T(8,128)S(1)}, u32[]{:S(2)}, u32[]{:S(2)}) collective-permute-start(f32[3,64]{0,1:T(8,128)S(1)} %bitcast.249), channel_id=1, source_target_pairs={{0,1},{1,2},{2,3},{3,4},{4,5},{5,6},{6,7},{7,8},{8,9},{9,10},{10,1... | collective-permute-start | bytes 2312 | tf_op jit(solution)/shard_map/ppermute | solution.py:17
  7.3 1.9 collective-permute-start.1
  9.8 3.9 %collective-permute-start.2 = (f32[3,64]{0,1:T(8,128)S(1)}, f32[3,64]{0,1:T(8,128)S(1)}, u32[]{:S(2)}, u32[]{:S(2)}) collective-permute-start(f32[3,64]{0,1:T(8,128)S(1)} %bitcast.251), channel_id=1, source_target_pairs={{0,2},{1,3},{2,4},{3,5},{4,6},{5,7},{6,8},{7,9},{8,10},{9,11},{10,... | collective-permute-start | bytes 2312 | tf_op jit(solution)/shard_map/ppermute | solution.py:17
  14.3 8.5 %collective-permute-start.3 = (f32[3,64]{0,1:T(8,128)S(1)}, f32[3,64]{0,1:T(8,128)S(1)}, u32[]{:S(2)}, u32[]{:S(2)}) collective-permute-start(f32[3,64]{0,1:T(8,128)S(1)} %bitcast.250), channel_id=1, source_target_pairs={{0,30},{1,31},{2,0},{3,1},{4,2},{5,3},{6,4},{7,5},{8,6},{9,7},{10,... | collective-permute-start | bytes 2312 | tf_op jit(solution)/shard_map/ppermute | solution.py:17
  28.3 27.7 %gather_fusion.4 = f32[8192,3]{1,0:T(8,128)} fusion(f32[3,512]{0,1:T(8,128)S(1)} %constant_dynamic-update-slice_fusion, s32[8192]{0:T(1024)S(1)} %broadcast_clamp_fusion), kind=kCustom, calls=%fused_computation.4 | custom fusion | bytes 229376 | tf_op jit(solution)/shard_map/gather | solution.py:97
  56.0 3.3 %multiply_reduce_fusion.1 = f32[32,256]{1,0:T(8,128)S(1)} fusion(f32[3,32,256]{0,2,1:T(8,128)} %bitcast.217, f32[3,256]{0,1:T(8,128)S(1)} %bitcast.224), kind=kLoop, calls=%fused_computation.63 | loop fusion | flops 65536 | bytes 134144 | tf_op jit(solution)/shard_map/jvp()/reduce_sum | solution.py:27
  60.1 21.4 %while.26 = (s32[]{:T(128)}, f32[8,28,1024]{2,0,1:T(8,128)S(1)}, f32[8,1024]{1,0:T(8,128)S(1)}, f32[8,1024]{1,0:T(8,128)S(1)}, f32[256]{0:T(256)S(1)}, /*index=5...) while((s32[]{:T(128)}, f32[8,28,1024]{2,0,1:T(8,128)S(1)}, ...), condition=%wide.region_5.6_spmd, body=%wide.region_3.5_spmd.sunk | while | flops 34339840 | bytes 2373741 | solution.py:111
  61.3 1.0 dynamic_update_slice.18
  64.0 1.0 dynamic_update_slice.18
  66.6 1.0 dynamic_update_slice.18
  69.3 1.0 dynamic_update_slice.18
  72.0 1.0 dynamic_update_slice.18
  74.6 1.0 dynamic_update_slice.18
  77.3 1.0 dynamic_update_slice.18
  80.0 1.0 dynamic_update_slice.18
  82.9 4.3 %add_multiply_fusion.1 = f32[3,32,256]{0,2,1:T(8,128)} fusion(f32[32,256]{1,0:T(8,128)S(1)} %fusion.95, f32[3,256]{0,1:T(8,128)S(1)} %bitcast.225, f32[8192,3]{1,0:T(8,128)} %gather_fusion.4), kind=kLoop, calls=%fused_computation.61 | loop fusion | flops 73728 | bytes 232448 | tf_op jit(solution)/shard_map/transpose(jvp())/add_any | solution.py:27
  87.2 2.5 reduce_sum.169
  89.7 44.4 %scatter_custom_fusion = f32[3,512]{0,1:T(8,128)S(1)} fusion(s32[8192]{0:T(1024)S(1)} %bitcast.236, f32[8192,3]{1,0:T(8,128)} %bitcast.219, f32[]{:T(128)} %constant.121.clone.1), kind=kCustom, calls=%fused_computation.142 | custom fusion | flops 24576 | bytes 6656 | tf_op jit(solution)/shard_map/scatter-add | solution.py:121
  134.1 5.8 %collective-permute-start.4 = (f32[3,64]{0,1:T(8,128)S(1)}, f32[3,64]{0,1:T(8,128)S(1)}, u32[]{:S(2)}, u32[]{:S(2)}) collective-permute-start(f32[3,64]{0,1:T(8,128)S(1)} %get-tuple-element.201), channel_id=1, source_target_pairs={{0,31},{1,0},{2,1},{3,2},{4,3},{5,4},{6,5},{7,6},{8,7},{9,8},{10,9... | collective-permute-start | bytes 2312 | tf_op jit(solution)/shard_map/ppermute | solution.py:17
  139.9 1.9 collective-permute-start.5
  141.8 5.4 %collective-permute-start.6 = (f32[3,64]{0,1:T(8,128)S(1)}, f32[3,64]{0,1:T(8,128)S(1)}, u32[]{:S(2)}, u32[]{:S(2)}) collective-permute-start(f32[3,64]{0,1:T(8,128)S(1)} %get-tuple-element.199), channel_id=1, source_target_pairs={{0,30},{1,31},{2,0},{3,1},{4,2},{5,3},{6,4},{7,5},{8,6},{9,7},{10,... | collective-permute-start | bytes 2312 | tf_op jit(solution)/shard_map/ppermute | solution.py:17
  147.2 1.9 collective-permute-start.7
  152.8 1.2 collective-permute-done.7
  155.6 1.9 collective-permute-start.8
  159.3 2.4 collective-permute-start.9
  161.7 1.9 collective-permute-start.10
  163.7 5.7 %collective-permute-start.11 = (f32[3,64]{0,1:T(8,128)S(1)}, f32[3,64]{0,1:T(8,128)S(1)}, u32[]{:S(2)}, u32[]{:S(2)}) collective-permute-start(f32[3,64]{0,1:T(8,128)S(1)} %bitcast.252), channel_id=1, source_target_pairs={{0,30},{1,31},{2,0},{3,1},{4,2},{5,3},{6,4},{7,5},{8,6},{9,7},{10,... | collective-permute-start | bytes 2312 | tf_op jit(solution)/shard_map/ppermute | solution.py:17
  170.2 27.7 %gather_fusion.9 = f32[8192,3]{1,0:T(8,128)} fusion(f32[3,512]{0,1:T(8,128)S(1)} %constant_dynamic-update-slice_fusion.5, s32[8192]{0:T(1024)S(1)} %broadcast_clamp_fusion), kind=kCustom, calls=%fused_computation.9 | custom fusion | bytes 229376 | tf_op jit(solution)/shard_map/gather | solution.py:97
  197.8 3.3 %multiply_reduce_fusion = f32[32,256]{1,0:T(8,128)S(1)} fusion(f32[3,32,256]{0,2,1:T(8,128)} %bitcast.216, f32[3,256]{0,1:T(8,128)S(1)} %get-tuple-element.191), kind=kLoop, calls=%fused_computation.62 | loop fusion | flops 65536 | bytes 134144 | tf_op jit(solution)/shard_map/jvp()/reduce_sum | solution.py:27
  202.1 21.3 %while.27 = (s32[]{:T(128)}, f32[8,28,1024]{2,0,1:T(8,128)S(1)}, f32[8,1024]{1,0:T(8,128)S(1)}, f32[8,1024]{1,0:T(8,128)S(1)}, f32[256]{0:T(256)S(1)}, /*index=5...) while((s32[]{:T(128)}, f32[8,28,1024]{2,0,1:T(8,128)S(1)}, ...), condition=%wide.region_20.21_spmd, body=%wide.region_18.20_spmd.sunk | while | flops 34339840 | bytes 2373741 | solution.py:111
  211.3 1.0 dynamic_update_slice.20
  216.6 1.0 dynamic_update_slice.20
  224.6 4.3 %add_multiply_fusion = f32[3,32,256]{0,2,1:T(8,128)} fusion(f32[32,256]{1,0:T(8,128)S(1)} %fusion.93, f32[3,256]{0,1:T(8,128)S(1)} %get-tuple-element.191, f32[8192,3]{1,0:T(8,128)} %gather_fusion.9), kind=kLoop, calls=%fused_computation.60 | loop fusion | flops 73728 | bytes 232448 | tf_op jit(solution)/shard_map/transpose(jvp())/add_any | solution.py:27
  228.9 2.5 reduce_sum.177
  231.4 44.4 %scatter_custom_fusion.5 = f32[3,512]{0,1:T(8,128)S(1)} fusion(s32[8192]{0:T(1024)S(1)} %bitcast.237, f32[8192,3]{1,0:T(8,128)} %bitcast.218, f32[]{:T(128)} %constant.121.clone.1), kind=kCustom, calls=%fused_computation.140 | custom fusion | flops 24576 | bytes 6656 | tf_op jit(solution)/shard_map/scatter-add | solution.py:121
  275.8 5.4 %collective-permute-start.12 = (f32[3,64]{0,1:T(8,128)S(1)}, f32[3,64]{0,1:T(8,128)S(1)}, u32[]{:S(2)}, u32[]{:S(2)}) collective-permute-start(f32[3,64]{0,1:T(8,128)S(1)} %get-tuple-element.197), channel_id=1, source_target_pairs={{0,31},{1,0},{2,1},{3,2},{4,3},{5,4},{6,5},{7,6},{8,7},{9,8},{10,9... | collective-permute-start | bytes 2312 | tf_op jit(solution)/shard_map/ppermute | solution.py:17
  281.2 1.9 collective-permute-start.13
  283.1 6.1 %collective-permute-start.14 = (f32[3,64]{0,1:T(8,128)S(1)}, f32[3,64]{0,1:T(8,128)S(1)}, u32[]{:S(2)}, u32[]{:S(2)}) collective-permute-start(f32[3,64]{0,1:T(8,128)S(1)} %get-tuple-element.195), channel_id=1, source_target_pairs={{0,30},{1,31},{2,0},{3,1},{4,2},{5,3},{6,4},{7,5},{8,6},{9,7},{10,... | collective-permute-start | bytes 2312 | tf_op jit(solution)/shard_map/ppermute | solution.py:17
  289.3 1.9 collective-permute-start.15
  294.9 1.2 collective-permute-done.15
  297.1 4.2 %collective-permute-start.18 = (f32[1,3,256]{1,2,0:T(8,128)S(1)}, f32[1,3,256]{1,2,0:T(8,128)S(1)}, u32[]{:S(2)}, u32[]{:S(2)}) collective-permute-start(f32[1,3,256]{1,2,0:T(8,128)S(1)} %bitcast.230), channel_id=1, source_target_pairs={{0,32},{32,64},{64,96},{96,128},{128,160},{160,192},{192,224},{224... | collective-permute-start | bytes 9224 | tf_op jit(solution)/shard_map/ppermute | solution.py:23
  301.3 4.1 %collective-permute-start.19 = (f32[1,3,256]{1,2,0:T(8,128)S(1)}, f32[1,3,256]{1,2,0:T(8,128)S(1)}, u32[]{:S(2)}, u32[]{:S(2)}) collective-permute-start(f32[1,3,256]{1,2,0:T(8,128)S(1)} %bitcast.231), channel_id=1, source_target_pairs={{32,0},{64,32},{96,64},{128,96},{160,128},{192,160},{224,192},{256... | collective-permute-start | bytes 9224 | tf_op jit(solution)/shard_map/ppermute | solution.py:23
  305.4 3.1 collective-permute-start.21
  308.6 3.1 collective-permute-start.20
  313.6 2.4 collective-permute-done.20
  316.6 1.9 collective-permute-start.16
  318.5 6.4 %collective-permute-start.17 = (f32[1,3,256]{1,2,0:T(8,128)S(1)}, f32[1,3,256]{1,2,0:T(8,128)S(1)}, u32[]{:S(2)}, u32[]{:S(2)}) collective-permute-start(f32[1,3,256]{1,2,0:T(8,128)S(1)} %get-tuple-element.188), channel_id=1, source_target_pairs={{32,0},{64,32},{96,64},{128,96},{160,128},{192,160},{224,192},{256... | collective-permute-start | bytes 9224 | tf_op jit(solution)/shard_map/ppermute | solution.py:23
  325.6 1.2 collective-permute-done.16
  (250 shorter events, 59.2 us)
Async XLA Ops:
  0.6 81.2 %copy-start = (bf16[256,256]{1,0:T(8,128)(2,1)S(1)}, bf16[256,256]{1,0:T(8,128)(2,1)}, u32[]{:S(2)}) copy-start(bf16[256,256]{1,0:T(8,128)(2,1)} %param.36) | copy-start | bytes 393220
  0.6 58.7 %copy-start.3 = (s32[1,256]{1,0:T(1,128)S(1)}, s32[1,256]{1,0:T(1,128)}, u32[]{:S(2)}) copy-start(s32[1,256]{1,0:T(1,128)} %param.26) | copy-start | bytes 3076
  2.9 25.3 %collective-permute-start = (f32[3,64]{0,1:T(8,128)S(1)}, f32[3,64]{0,1:T(8,128)S(1)}, u32[]{:S(2)}, u32[]{:S(2)}) collective-permute-start(f32[3,64]{0,1:T(8,128)S(1)} %bitcast.249), channel_id=1, source_target_pairs={{0,1},{1,2},{2,3},{3,4},{4,5},{5,6},{6,7},{7,8},{8,9},{9,10},{10,1... | collective-permute-start | bytes 2312 | tf_op jit(solution)/shard_map/ppermute | solution.py:17
  7.3 20.9 %collective-permute-start.1 = (f32[3,64]{0,1:T(8,128)S(1)}, f32[3,64]{0,1:T(8,128)S(1)}, u32[]{:S(2)}, u32[]{:S(2)}) collective-permute-start(f32[3,64]{0,1:T(8,128)S(1)} %bitcast.248), channel_id=1, source_target_pairs={{0,31},{1,0},{2,1},{3,2},{4,3},{5,4},{6,5},{7,6},{8,7},{9,8},{10,9... | collective-permute-start | bytes 2312 | tf_op jit(solution)/shard_map/ppermute | solution.py:17
  9.8 18.4 %collective-permute-start.2 = (f32[3,64]{0,1:T(8,128)S(1)}, f32[3,64]{0,1:T(8,128)S(1)}, u32[]{:S(2)}, u32[]{:S(2)}) collective-permute-start(f32[3,64]{0,1:T(8,128)S(1)} %bitcast.251), channel_id=1, source_target_pairs={{0,2},{1,3},{2,4},{3,5},{4,6},{5,7},{6,8},{7,9},{8,10},{9,11},{10,... | collective-permute-start | bytes 2312 | tf_op jit(solution)/shard_map/ppermute | solution.py:17
  14.3 14.0 %collective-permute-start.3 = (f32[3,64]{0,1:T(8,128)S(1)}, f32[3,64]{0,1:T(8,128)S(1)}, u32[]{:S(2)}, u32[]{:S(2)}) collective-permute-start(f32[3,64]{0,1:T(8,128)S(1)} %bitcast.250), channel_id=1, source_target_pairs={{0,30},{1,31},{2,0},{3,1},{4,2},{5,3},{6,4},{7,5},{8,6},{9,7},{10,... | collective-permute-start | bytes 2312 | tf_op jit(solution)/shard_map/ppermute | solution.py:17
  28.2 31.9 %copy-start.1 = (bf16[256,28]{0,1:T(8,128)(2,1)S(1)}, bf16[256,28]{0,1:T(8,128)(2,1)}, u32[]{:S(2)}) copy-start(bf16[256,28]{0,1:T(8,128)(2,1)} %param.33) | copy-start | bytes 43012
  28.2 31.9 %copy-start.2 = (f32[256]{0:T(256)S(1)}, f32[256]{0:T(256)}, u32[]{:S(2)}) copy-start(f32[256]{0:T(256)} %param.34) | copy-start | bytes 3076
  60.1 21.5 %copy-start.4 = (bf16[256,8]{0,1:T(8,128)(2,1)S(1)}, bf16[256,8]{0,1:T(8,128)(2,1)}, u32[]{:S(2)}) copy-start(bf16[256,8]{0,1:T(8,128)(2,1)} %param.35) | copy-start | bytes 12292
  60.1 21.8 %copy-start.5 = (f32[256]{0:T(256)S(1)}, f32[256]{0:T(256)}, u32[]{:S(2)}) copy-start(f32[256]{0:T(256)} %param.37) | copy-start | bytes 3076
  134.1 15.7 %collective-permute-start.4 = (f32[3,64]{0,1:T(8,128)S(1)}, f32[3,64]{0,1:T(8,128)S(1)}, u32[]{:S(2)}, u32[]{:S(2)}) collective-permute-start(f32[3,64]{0,1:T(8,128)S(1)} %get-tuple-element.201), channel_id=1, source_target_pairs={{0,31},{1,0},{2,1},{3,2},{4,3},{5,4},{6,5},{7,6},{8,7},{9,8},{10,9... | collective-permute-start | bytes 2312 | tf_op jit(solution)/shard_map/ppermute | solution.py:17
  139.9 10.9 %collective-permute-start.5 = (f32[3,64]{0,1:T(8,128)S(1)}, f32[3,64]{0,1:T(8,128)S(1)}, u32[]{:S(2)}, u32[]{:S(2)}) collective-permute-start(f32[3,64]{0,1:T(8,128)S(1)} %get-tuple-element.200), channel_id=1, source_target_pairs={{0,1},{1,2},{2,3},{3,4},{4,5},{5,6},{6,7},{7,8},{8,9},{9,10},{10,1... | collective-permute-start | bytes 2312 | tf_op jit(solution)/shard_map/ppermute | solution.py:17
  141.8 10.0 %collective-permute-start.6 = (f32[3,64]{0,1:T(8,128)S(1)}, f32[3,64]{0,1:T(8,128)S(1)}, u32[]{:S(2)}, u32[]{:S(2)}) collective-permute-start(f32[3,64]{0,1:T(8,128)S(1)} %get-tuple-element.199), channel_id=1, source_target_pairs={{0,30},{1,31},{2,0},{3,1},{4,2},{5,3},{6,4},{7,5},{8,6},{9,7},{10,... | collective-permute-start | bytes 2312 | tf_op jit(solution)/shard_map/ppermute | solution.py:17
  147.2 6.8 %collective-permute-start.7 = (f32[3,64]{0,1:T(8,128)S(1)}, f32[3,64]{0,1:T(8,128)S(1)}, u32[]{:S(2)}, u32[]{:S(2)}) collective-permute-start(f32[3,64]{0,1:T(8,128)S(1)} %get-tuple-element.198), channel_id=1, source_target_pairs={{0,2},{1,3},{2,4},{3,5},{4,6},{5,7},{6,8},{7,9},{8,10},{9,11},{10,... | collective-permute-start | bytes 2312 | tf_op jit(solution)/shard_map/ppermute | solution.py:17
  155.6 13.7 %collective-permute-start.8 = (f32[3,64]{0,1:T(8,128)S(1)}, f32[3,64]{0,1:T(8,128)S(1)}, u32[]{:S(2)}, u32[]{:S(2)}) collective-permute-start(f32[3,64]{0,1:T(8,128)S(1)} %bitcast.255), channel_id=1, source_target_pairs={{0,1},{1,2},{2,3},{3,4},{4,5},{5,6},{6,7},{7,8},{8,9},{9,10},{10,1... | collective-permute-start | bytes 2312 | tf_op jit(solution)/shard_map/ppermute | solution.py:17
  159.3 10.0 %collective-permute-start.9 = (f32[3,64]{0,1:T(8,128)S(1)}, f32[3,64]{0,1:T(8,128)S(1)}, u32[]{:S(2)}, u32[]{:S(2)}) collective-permute-start(f32[3,64]{0,1:T(8,128)S(1)} %bitcast.254), channel_id=1, source_target_pairs={{0,31},{1,0},{2,1},{3,2},{4,3},{5,4},{6,5},{7,6},{8,7},{9,8},{10,9... | collective-permute-start | bytes 2312 | tf_op jit(solution)/shard_map/ppermute | solution.py:17
  161.7 7.6 %collective-permute-start.10 = (f32[3,64]{0,1:T(8,128)S(1)}, f32[3,64]{0,1:T(8,128)S(1)}, u32[]{:S(2)}, u32[]{:S(2)}) collective-permute-start(f32[3,64]{0,1:T(8,128)S(1)} %bitcast.253), channel_id=1, source_target_pairs={{0,2},{1,3},{2,4},{3,5},{4,6},{5,7},{6,8},{7,9},{8,10},{9,11},{10,... | collective-permute-start | bytes 2312 | tf_op jit(solution)/shard_map/ppermute | solution.py:17
  163.7 6.5 %collective-permute-start.11 = (f32[3,64]{0,1:T(8,128)S(1)}, f32[3,64]{0,1:T(8,128)S(1)}, u32[]{:S(2)}, u32[]{:S(2)}) collective-permute-start(f32[3,64]{0,1:T(8,128)S(1)} %bitcast.252), channel_id=1, source_target_pairs={{0,30},{1,31},{2,0},{3,1},{4,2},{5,3},{6,4},{7,5},{8,6},{9,7},{10,... | collective-permute-start | bytes 2312 | tf_op jit(solution)/shard_map/ppermute | solution.py:17
  275.8 16.1 %collective-permute-start.12 = (f32[3,64]{0,1:T(8,128)S(1)}, f32[3,64]{0,1:T(8,128)S(1)}, u32[]{:S(2)}, u32[]{:S(2)}) collective-permute-start(f32[3,64]{0,1:T(8,128)S(1)} %get-tuple-element.197), channel_id=1, source_target_pairs={{0,31},{1,0},{2,1},{3,2},{4,3},{5,4},{6,5},{7,6},{8,7},{9,8},{10,9... | collective-permute-start | bytes 2312 | tf_op jit(solution)/shard_map/ppermute | solution.py:17
  281.2 11.7 %collective-permute-start.13 = (f32[3,64]{0,1:T(8,128)S(1)}, f32[3,64]{0,1:T(8,128)S(1)}, u32[]{:S(2)}, u32[]{:S(2)}) collective-permute-start(f32[3,64]{0,1:T(8,128)S(1)} %get-tuple-element.196), channel_id=1, source_target_pairs={{0,1},{1,2},{2,3},{3,4},{4,5},{5,6},{6,7},{7,8},{8,9},{9,10},{10,1... | collective-permute-start | bytes 2312 | tf_op jit(solution)/shard_map/ppermute | solution.py:17
  283.1 10.8 %collective-permute-start.14 = (f32[3,64]{0,1:T(8,128)S(1)}, f32[3,64]{0,1:T(8,128)S(1)}, u32[]{:S(2)}, u32[]{:S(2)}) collective-permute-start(f32[3,64]{0,1:T(8,128)S(1)} %get-tuple-element.195), channel_id=1, source_target_pairs={{0,30},{1,31},{2,0},{3,1},{4,2},{5,3},{6,4},{7,5},{8,6},{9,7},{10,... | collective-permute-start | bytes 2312 | tf_op jit(solution)/shard_map/ppermute | solution.py:17
  289.3 6.8 %collective-permute-start.15 = (f32[3,64]{0,1:T(8,128)S(1)}, f32[3,64]{0,1:T(8,128)S(1)}, u32[]{:S(2)}, u32[]{:S(2)}) collective-permute-start(f32[3,64]{0,1:T(8,128)S(1)} %get-tuple-element.194), channel_id=1, source_target_pairs={{0,2},{1,3},{2,4},{3,5},{4,6},{5,7},{6,8},{7,9},{8,10},{9,11},{10,... | collective-permute-start | bytes 2312 | tf_op jit(solution)/shard_map/ppermute | solution.py:17
  297.1 27.8 %collective-permute-start.18 = (f32[1,3,256]{1,2,0:T(8,128)S(1)}, f32[1,3,256]{1,2,0:T(8,128)S(1)}, u32[]{:S(2)}, u32[]{:S(2)}) collective-permute-start(f32[1,3,256]{1,2,0:T(8,128)S(1)} %bitcast.230), channel_id=1, source_target_pairs={{0,32},{32,64},{64,96},{96,128},{128,160},{160,192},{192,224},{224... | collective-permute-start | bytes 9224 | tf_op jit(solution)/shard_map/ppermute | solution.py:23
  301.3 23.6 %collective-permute-start.19 = (f32[1,3,256]{1,2,0:T(8,128)S(1)}, f32[1,3,256]{1,2,0:T(8,128)S(1)}, u32[]{:S(2)}, u32[]{:S(2)}) collective-permute-start(f32[1,3,256]{1,2,0:T(8,128)S(1)} %bitcast.231), channel_id=1, source_target_pairs={{32,0},{64,32},{96,64},{128,96},{160,128},{192,160},{224,192},{256... | collective-permute-start | bytes 9224 | tf_op jit(solution)/shard_map/ppermute | solution.py:23
  305.4 7.5 %collective-permute-start.21 = (f32[1]{0:T(128)}, f32[1]{0:T(128)}, u32[]{:S(2)}, u32[]{:S(2)}) collective-permute-start(f32[1]{0:T(128)} %param.31), channel_id=1, source_target_pairs={{32,0},{64,32},{96,64},{128,96},{160,128},{192,160},{224,192},{256... | collective-permute-start | bytes 20 | tf_op jit(solution)/shard_map/ppermute | solution.py:23
  308.6 7.4 %collective-permute-start.20 = (f32[1]{0:T(128)}, f32[1]{0:T(128)}, u32[]{:S(2)}, u32[]{:S(2)}) collective-permute-start(f32[1]{0:T(128)} %param.31), channel_id=1, source_target_pairs={{0,32},{32,64},{64,96},{96,128},{128,160},{160,192},{192,224},{224... | collective-permute-start | bytes 20 | tf_op jit(solution)/shard_map/ppermute | solution.py:23
  316.6 10.2 %collective-permute-start.16 = (f32[1,3,256]{1,2,0:T(8,128)S(1)}, f32[1,3,256]{1,2,0:T(8,128)S(1)}, u32[]{:S(2)}, u32[]{:S(2)}) collective-permute-start(f32[1,3,256]{1,2,0:T(8,128)S(1)} %get-tuple-element.188), channel_id=1, source_target_pairs={{0,32},{32,64},{64,96},{96,128},{128,160},{160,192},{192,224},{224... | collective-permute-start | bytes 9224 | tf_op jit(solution)/shard_map/ppermute | solution.py:23
  318.5 8.7 %collective-permute-start.17 = (f32[1,3,256]{1,2,0:T(8,128)S(1)}, f32[1,3,256]{1,2,0:T(8,128)S(1)}, u32[]{:S(2)}, u32[]{:S(2)}) collective-permute-start(f32[1,3,256]{1,2,0:T(8,128)S(1)} %get-tuple-element.188), channel_id=1, source_target_pairs={{32,0},{64,32},{96,64},{128,96},{160,128},{192,160},{224,192},{256... | collective-permute-start | bytes 9224 | tf_op jit(solution)/shard_map/ppermute | solution.py:23
where the time goes:
time: 334 us; the launch traced here: 328 us
  other arithmetic  129 us (39%)
  local copies, waits for them, and re-layouts  87.7 us (26%)
  starting transfers between devices  83.1 us (25%)
  matrix products  15.5 us (5%)
  waiting for transfers between devices  7.07 us (2%)
  between operations  4.22 us (1%)
    scatter-add x2, other arithmetic, domain_gradient(): g_all = jnp.zeros_like(all_pos).at[:, neighbour_idx].add(g_vec)  88.8 us
    ppermute x16, starting transfers between devices, passed_along(): lax.ppermute(value, axis, [(i, (i + by) % size) for i in range(size)])  60.3 us
    gather x2, local copies, waits for them, and re-layouts, domain_gradient(): edge_vec = all_pos[:, neighbour_idx] - domain_coordinates_here[:, None, :]  55.4 us
    ppermute x6, starting transfers between devices, from_behind(): return lax.ppermute(value, axis, pairs)  22.8 us
    dynamic_update_slice x48, local copies, waits for them, and re-layouts, domain_gradient(): lax.map(run_group, (blocks_in, blocks_cut, group_start))  19.8 us
    dot_general x16, matrix products, edge_block(): jnp.dot(bond_intake_coefficients.T, g_pre, preferred_element_type=jnp.flo...  8.67 us
    add_any x2, other arithmetic, features(): dist_sq = jnp.sum(edge_vec * edge_vec, axis=0)  8.55 us
    scatter-add x8, other arithmetic, on_device(): g_own = g_own.at[:, ghost_idx[which]].add(returned[which])  7.86 us
  transfers between devices with their start and end apart: 22, of which 6 were waited for; matrix products, arithmetic and copies ran while one was open for 5% of the time, Pallas kernels for 0%

commit v1 on v0

v1 whole, which is shorter than its diff:
```python
import functools

import jax
import jax.numpy as jnp
from jax import lax
from jax.experimental import pallas as pl
from jax.experimental.pallas import tpu as pltpu
from jax.sharding import PartitionSpec as P

STEPS = 2
TIME_STEP = 0.05
CUT_SQ = 9.0
N_BASIS = 8
N_KIND = 6
LANES = 128
SLOTS = 32
GROUPS = SLOTS // 8
HIDDEN = 256
SHARP = (N_BASIS / CUT_SQ) ** 2
CENTRES = [CUT_SQ * c / (N_BASIS - 1) for c in range(N_BASIS)]
F32 = jnp.float32
BF16 = jnp.bfloat16


def nt_dot(a, b):
    return lax.dot_general(a, b, (((1,), (1,)), ((), ())), preferred_element_type=F32)


def tn_dot(a, b):
    return lax.dot_general(a, b, (((0,), (0,)), ((), ())), preferred_element_type=F32)


def nn_dot(a, b):
    return lax.dot_general(a, b, (((1,), (0,)), ((), ())), preferred_element_type=F32)


def as_tile(wide):
    pad = jnp.zeros((2, LANES), wide.dtype)
    return jnp.concatenate([wide[:, :LANES], wide[:, LANES:], pad], axis=0)


def rows_of_two(first, second, pad_with=None):
    shape = (3, LANES)
    pad = jnp.zeros((2, LANES), first.dtype)
    return jnp.concatenate(
        [jnp.broadcast_to(first, shape), jnp.broadcast_to(second, shape), pad], axis=0
    )


def take_lanes(table, lane):
    return jnp.take_along_axis(table, lane, axis=1, mode="promise_in_bounds")


def border_positions(tile, border0, border1):
    index = rows_of_two(border0, border1)
    pad = jnp.zeros((2, LANES), F32)
    low = jnp.concatenate([tile[0:3], tile[0:3], pad], axis=0)
    high = jnp.concatenate([tile[3:6], tile[3:6], pad], axis=0)
    lane = index & (LANES - 1)
    return jnp.where(index < LANES, take_lanes(low, lane), take_lanes(high, lane))


def four_sets(set0, set1, set2, set3):
    row = lax.broadcasted_iota(jnp.int32, (8, LANES), 0)
    col = lax.broadcasted_iota(jnp.int32, (8, LANES), 1)
    left = col < LANES // 2
    return jnp.where(row < 3, jnp.where(left, set0, set1), jnp.where(left, set2, set3))


def split_parts(value, count):
    parts = []
    for _ in range(count):
        part = value.astype(BF16).astype(F32)
        parts.append(part)
        value = value - part
    return parts


def start_kernel(x_ref, v_ref, kind_ref, border_ref, inertia_ref, out_ref):
    x_tile = as_tile(x_ref[0])
    border = border_ref[0]
    border0 = jnp.concatenate([border[0:1], border[1:2]], axis=1)
    border1 = jnp.concatenate([border[2:3], border[3:4]], axis=1)
    kind = kind_ref[...]
    inverse = jnp.zeros(kind.shape, F32)
    for k in range(N_KIND):
        inverse = jnp.where(kind == k, inertia_ref[k], inverse)
    out_ref[0:8] = border_positions(x_tile, border0, border1)
    out_ref[8:14] = x_tile[0:6]
    out_ref[14:15] = inverse[:, :LANES]
    out_ref[15:16] = inverse[:, LANES:]
    out_ref[16:22] = as_tile(v_ref[0])[0:6]
    out_ref[22:23] = border0.astype(F32)
    out_ref[23:24] = border1.astype(F32)


def chosen_columns(slot, count):
    feature = lax.broadcasted_iota(jnp.int32, (28, count), 0)
    col = lax.broadcasted_iota(jnp.int32, (28, count), 1)
    block, which = col // 8, col % 8
    radial = (block < 8) & (which == slot) & (feature == block)
    environ = (block == 8) & (feature == 8 + which)
    centre = (block == 9) & (which < N_KIND) & (feature == 16 + which)
    neigh = (block >= 10) & (which == slot) & (feature == 22 + block - 10)
    return (radial | environ | centre | neigh).astype(F32)


def force_kernel(
    core_ref,
    state_ref,
    near_ref,
    far_ref,
    index_ref,
    place_kind_ref,
    total_ref,
    kind_ref,
    intake_ref,
    edge_out_ref,
    opening_ref,
    middle_ref,
    atom_out_ref,
    out_ref,
    feat_ref,
    gauss_ref,
    geo_ref,
    intake_up,
    intake_down,
    edge_w,
    energy_ref,
    gin_ref,
    scat0_ref,
    scat1_ref,
):
    core = core_ref[0]
    first_core = core == 0
    own = state_ref[core]
    minus2, minus1 = far_ref[0, 0, 0], far_ref[0, 0, 1]
    plus2, plus3 = far_ref[1, 1, 0], far_ref[1, 1, 1]
    near0, near1 = near_ref[0], near_ref[1]

    def pick(a, b):
        return jnp.where(first_core, a, b)

    ghost = four_sets(
        pick(minus1, near0), pick(near1, plus2), pick(minus2, minus1), pick(plus2, plus3)
    )

    intake = intake_ref[...]
    for j in range(8):
        up = (0.5 * chosen_columns(j, 128)).astype(BF16)
        intake_up[j * HIDDEN : (j + 1) * HIDDEN, :] = nn_dot(intake, up).astype(BF16)
        down = chosen_columns(j, 128).astype(BF16)
        intake_down[:, j * HIDDEN : (j + 1) * HIDDEN] = lax.dot_general(
            down, intake, (((0,), (1,)), ((), ())), preferred_element_type=F32
        )[0:80].astype(BF16)
    edge_w[...] = jnp.transpose(jnp.broadcast_to(0.5 * edge_out_ref[...], (LANES, HIDDEN)))

    kind = kind_ref[...]
    kind_rows = lax.broadcasted_iota(jnp.int32, (8, 2 * LANES), 0)
    centre_hot = (kind_rows == kind).astype(F32)
    slot_row = lax.broadcasted_iota(jnp.int32, (8, LANES), 0)
    environ_sum = [[None] * N_BASIS for _ in range(2)]
    for s in range(GROUPS):
        for h in range(2):
            cols = slice(h * LANES, (h + 1) * LANES)
            index = index_ref[0, s * 8 : s * 8 + 8, cols]
            lane = index & (LANES - 1)
            chunk = index // LANES
            dist_sq = None
            for comp in range(3):
                found = None
                for which in range(4):
                    table = own if which < 2 else ghost
                    row = (which % 2) * 3 + comp
                    values = take_lanes(
                        jnp.broadcast_to(table[row : row + 1], (8, LANES)), lane
                    )
                    found = values if which == 0 else jnp.where(chunk == which, values, found)
                vec = found - own[h * 3 + comp : h * 3 + comp + 1]
                geo_ref[comp, s, :, cols] = vec
                dist_sq = vec * vec if comp == 0 else dist_sq + vec * vec
            live = slot_row + s * 8 < total_ref[:, cols]
            inside = 1.0 - dist_sq / CUT_SQ
            used = live & (inside > 0.0)
            cutoff = jnp.where(used, inside * inside, 0.0)
            geo_ref[3, s, :, cols] = dist_sq
            geo_ref[4, s, :, cols] = cutoff
            geo_ref[5, s, :, cols] = jnp.where(used, inside * (-2.0 / CUT_SQ), 0.0)
            for c in range(N_BASIS):
                gap = dist_sq - CENTRES[c]
                gauss = jnp.exp(-SHARP * (gap * gap))
                gauss_ref[s, c * 8 : c * 8 + 8, cols] = gauss
                radial = gauss * cutoff
                sofar = environ_sum[h][c]
                environ_sum[h][c] = radial if sofar is None else sofar + radial
    environ = jnp.concatenate(
        [
            jnp.concatenate(
                [jnp.sum(environ_sum[h][c], axis=0, keepdims=True) for c in range(N_BASIS)], axis=0
            )
            for h in range(2)
        ],
        axis=1,
    )
    for s in range(GROUPS):
        place_kind = place_kind_ref[0, s * 8 : s * 8 + 8, :]
        cutoff = geo_ref[4, s]
        parts = [gauss_ref[s, c * 8 : c * 8 + 8, :] * cutoff for c in range(N_BASIS)]
        parts += [environ, centre_hot]
        parts += [(place_kind == k).astype(F32) for k in range(N_KIND)]
        feat_ref[s] = jnp.concatenate(parts, axis=0).astype(BF16)

    env_low = environ.astype(BF16)
    opening = opening_ref[...]
    middle = middle_ref[...]
    atom_w = jnp.transpose(jnp.broadcast_to(atom_out_ref[...], (LANES, HIDDEN)))
    atom_w = jnp.concatenate([atom_w, atom_w], axis=1)
    first = nn_dot(opening, env_low)
    sig_first = jax.nn.sigmoid(first)
    hidden_one = (first * sig_first).astype(BF16)
    second = nn_dot(middle, hidden_one)
    sig_second = jax.nn.sigmoid(second)
    g_second = (atom_w * sig_second * (1.0 + second * (1.0 - sig_second))).astype(BF16)
    g_hidden = tn_dot(middle, g_second)
    g_first = (g_hidden * sig_first * (1.0 + first * (1.0 - sig_first))).astype(BF16)
    g_env = tn_dot(opening, g_first)

    def group(s, g_env):
        feat = feat_ref[s]
        g_group = None
        for j in range(8):
            pre = nn_dot(intake_up[j * HIDDEN : (j + 1) * HIDDEN, :], feat)
            cut = geo_ref[4, s, j : j + 1, :]
            energy = None
            g_parts = []
            for b in range(HIDDEN // 16):
                rows = slice(b * 16, b * 16 + 16)
                half = pre[rows].astype(BF16).astype(F32)
                w = edge_w[rows, :]
                w = jnp.concatenate([w, w], axis=1)
                th = jnp.tanh(half)
                p = w * (th + 1.0)
                e = half * p
                g = (p + e) - e * th
                energy = e if energy is None else energy + e
                g_parts.append((g * cut).astype(BF16))
            energy_ref[s, j : j + 1, :] = 2.0 * jnp.sum(energy, axis=0, keepdims=True)
            g_pre = jnp.concatenate(g_parts, axis=0)
            part = nn_dot(intake_down[:, j * HIDDEN : (j + 1) * HIDDEN], g_pre)
            g_group = part if g_group is None else g_group + part
        gin_ref[s] = g_group[0:64]
        return g_env + g_group[64:72]

    g_env = lax.fori_loop(0, GROUPS, group, g_env)

    own_sum = [[None] * 3 for _ in range(2)]
    for s in range(GROUPS):
        for h in range(2):
            cols = slice(h * LANES, (h + 1) * LANES)
            dist_sq, cutoff, slope = (geo_ref[k, s, :, cols] for k in (3, 4, 5))
            g_cut = energy_ref[s, :, cols]
            g_gap = None
            for c in range(N_BASIS):
                g_radial = gin_ref[s, c * 8 : c * 8 + 8, cols] + g_env[c : c + 1, cols]
                q = g_radial * gauss_ref[s, c * 8 : c * 8 + 8, cols]
                g_cut = g_cut + q
                moment = q * (dist_sq - CENTRES[c])
                g_gap = moment if g_gap is None else g_gap + moment
            g_dist = (-4.0 * SHARP) * (cutoff * g_gap) + 2.0 * (g_cut * slope)
            chunk = index_ref[0, s * 8 : s * 8 + 8, cols] // LANES
            scat = (scat0_ref, scat1_ref)[h]
            for comp in range(3):
                g_vec = g_dist * geo_ref[comp, s, :, cols]
                sofar = own_sum[h][comp]
                own_sum[h][comp] = g_vec if sofar is None else sofar + g_vec
                for part, value in enumerate(split_parts(g_vec, 2)):
                    for which in range(4):
                        row = s * 8 * 24 + part * 12 + which * 3 + comp
                        scat[pl.ds(row, 8, stride=24), :] = jnp.where(chunk == which, value, 0.0)
    place = lax.broadcasted_iota(jnp.int32, (LANES, 2 * LANES), 0)
    total = None
    for s in range(GROUPS):
        lhs, rhs = [], []
        for j in range(8):
            slot = s * 8 + j
            block = jnp.concatenate(
                [scat0_ref[slot * 24 : slot * 24 + 24, :], scat1_ref[slot * 24 : slot * 24 + 24, :]],
                axis=1,
            )
            lhs.append(block.astype(BF16))
            lane = index_ref[0, slot : slot + 1, :] & (LANES - 1)
            rhs.append((place == lane).astype(F32).astype(BF16))
        part = nt_dot(jnp.concatenate(lhs, axis=1), jnp.concatenate(rhs, axis=1))
        total = part if total is None else total + part
    total = total[0:12] + total[12:24]
    centre = jnp.concatenate(
        [jnp.sum(own_sum[h][comp], axis=0, keepdims=True) for h in range(2) for comp in range(3)],
        axis=0,
    )
    pad = jnp.zeros((2, LANES), F32)
    out_ref[0:8] = jnp.concatenate([total[6:12], pad], axis=0)
    out_ref[8:16] = jnp.concatenate([total[0:6] - centre, pad], axis=0)


def returned_sum(returned, border0, border1):
    row = lax.broadcasted_iota(jnp.int32, (8, LANES), 0)
    place = lax.broadcasted_iota(jnp.int32, (LANES, LANES), 0)
    lhs, rhs = [], []
    for which, border in enumerate((border0, border1)):
        three = returned[which * 3 : which * 3 + 3]
        twice = jnp.concatenate([three, three, jnp.zeros((2, LANES), F32)], axis=0)
        meant = (border // LANES == 1) == (row >= 3)
        kept = jnp.where(meant, twice, 0.0)
        lhs.append(jnp.concatenate(split_parts(kept, 3), axis=0).astype(BF16))
        rhs.append((place == (border & (LANES - 1))).astype(F32).astype(BF16))
    total = nt_dot(jnp.concatenate(lhs, axis=1), jnp.concatenate(rhs, axis=1))
    return total[0:8] + total[8:16] + total[16:24]


def moved(state_ref, near_ref, far_ref):
    minus2, minus1 = far_ref[0, 0, 0], far_ref[0, 0, 1]
    plus2, plus3 = far_ref[1, 1, 0], far_ref[1, 1, 1]
    near0, near1 = near_ref[0, 0:8], near_ref[1, 0:8]
    sets = ((near1, minus1, plus2, minus2), (plus2, near0, plus3, minus1))
    result = []
    for domain in range(2):
        state = state_ref[domain]
        border0 = state[14:15].astype(jnp.int32)
        border1 = state[15:16].astype(jnp.int32)
        inverse = rows_of_two(state[6:7], state[7:8])
        grad = near_ref[domain, 8:16] + returned_sum(four_sets(*sets[domain]), border0, border1)
        speed = state[8:16] - TIME_STEP * grad * inverse
        place = state[0:8] + TIME_STEP * speed
        result.append((place, speed, border0, border1))
    return result


def step_kernel(state_ref, near_ref, far_ref, send_ref, next_ref):
    for domain, (place, speed, border0, border1) in enumerate(moved(state_ref, near_ref, far_ref)):
        send_ref[domain] = border_positions(place, border0, border1)
        next_ref[domain, 0:6] = place[0:6]
        next_ref[domain, 6:8] = state_ref[domain, 6:8]
        next_ref[domain, 8:14] = speed[0:6]
        next_ref[domain, 14:16] = state_ref[domain, 14:16]


def last_kernel(level_ref, state_ref, near_ref, far_ref, next_ref):
    for domain, (place, speed, _, _) in enumerate(moved(state_ref, near_ref, far_ref)):
        next_ref[domain, 0:6] = place[0:6]
        next_ref[domain, 6:8] = jnp.full((2, LANES), level_ref[0], F32)
        next_ref[domain, 8:16] = speed


def swap_kernel(where_ref, level_ref, own_ref, mate_ref, x_ref, v_ref):
    core, swaps, side, position = (where_ref[k] for k in range(4))
    mine = own_ref[core]
    theirs = mate_ref[side, position, core]
    chosen = jnp.where(swaps == 1, theirs, mine)
    scale = jnp.sqrt(level_ref[0] / chosen[6:7])
    scale = jnp.concatenate([scale, scale], axis=1)
    x_ref[0] = jnp.concatenate([chosen[0:3], chosen[3:6]], axis=1)
    v_ref[0] = jnp.concatenate([chosen[8:11], chosen[11:14]], axis=1) * scale


def vmem():
    return pl.BlockSpec(memory_space=pltpu.VMEM)


def smem():
    return pl.BlockSpec(memory_space=pltpu.SMEM)


def tiles(*shape):
    return jax.ShapeDtypeStruct(shape + (LANES,), F32)


def call(kernel, scalars, arrays, out_shape, scratch=(), limit=48 * 2**20):
    out_specs = [vmem() for _ in out_shape] if isinstance(out_shape, list) else vmem()
    return pl.pallas_call(
        kernel,
        out_shape=out_shape,
        in_specs=[smem()] * len(scalars) + [vmem()] * len(arrays),
        out_specs=out_specs,
        scratch_shapes=list(scratch),
        compiler_params=pltpu.CompilerParams(vmem_limit_bytes=limit),
    )(*scalars, *arrays)


def force_scratch():
    return [
        pltpu.VMEM((GROUPS, 128, 2 * LANES), BF16),
        pltpu.VMEM((GROUPS, 64, 2 * LANES), F32),
        pltpu.VMEM((6, GROUPS, 8, 2 * LANES), F32),
        pltpu.VMEM((8 * HIDDEN, 128), BF16),
        pltpu.VMEM((80, 8 * HIDDEN), BF16),
        pltpu.VMEM((HIDDEN, LANES), F32),
        pltpu.VMEM((GROUPS, 8, 2 * LANES), F32),
        pltpu.VMEM((GROUPS, 64, 2 * LANES), F32),
        pltpu.VMEM((SLOTS * 24, LANES), F32),
        pltpu.VMEM((SLOTS * 24, LANES), F32),
    ]


def on_chip(value, domains):
    groups = [[2 * i, 2 * i + 1] for i in range(domains // 2)]
    return lax.all_gather(value, "space", axis_index_groups=groups)


def across_chips(value, domains):
    groups = [[(2 * i - 1) % domains, 2 * i] for i in range(domains // 2)]
    return lax.all_gather(value, "space", axis_index_groups=groups)


def along_ladder(value, rungs, domains):
    groups = []
    for domain in range(domains):
        shift = domain % 2
        for low in range(shift, rungs, 2):
            high = (low + 1) % rungs
            groups.append([low * domains + domain, high * domains + domain])
    return lax.all_gather(value, ("replica", "space"), axis_index_groups=groups)


def on_device(
    particle_coordinates,
    particle_motions,
    particle_kinds,
    filled_totals,
    adjacent_particles,
    adjacent_place_kinds,
    border_particle_numbers,
    reciprocal_kind_inertia,
    thermal_levels,
    swap_mates,
    bond_intake_coefficients,
    bond_output_coefficients,
    particle_opening_coefficients,
    particle_middle_coefficients,
    particle_output_coefficients,
):
    domains, rungs = lax.axis_size("space"), lax.axis_size("replica")
    core = lax.axis_index("space") % 2
    rank = lax.axis_index("replica")
    mate = swap_mates[0]
    odd = rank % 2
    side = jnp.where((mate > rank) == (odd == 0), 0, 1)
    position = jnp.where(side == 0, 1 - odd, odd)
    where_to = jnp.stack([core, (mate != rank).astype(jnp.int32), side, position]).astype(jnp.int32)

    begin = pl.pallas_call(
        start_kernel,
        out_shape=tiles(24),
        in_specs=[vmem()] * 4 + [smem()],
        out_specs=vmem(),
    )(
        particle_coordinates,
        particle_motions,
        particle_kinds,
        border_particle_numbers,
        reciprocal_kind_inertia,
    )
    both = on_chip(begin, domains)
    send, state = both[:, 0:8], both[:, 8:24]
    for step in range(STEPS):
        far = on_chip(across_chips(send, domains), domains)
        partial = call(
            force_kernel,
            (where_to,),
            (
                state,
                send,
                far,
                adjacent_particles,
                adjacent_place_kinds,
                filled_totals,
                particle_kinds,
                bond_intake_coefficients,
                bond_output_coefficients[None],
                particle_opening_coefficients,
                particle_middle_coefficients,
                particle_output_coefficients[None],
            ),
            tiles(16),
            force_scratch(),
        )
        near = on_chip(partial, domains)
        far = on_chip(across_chips(near[:, 0:8], domains), domains)
        if step < STEPS - 1:
            send, state = call(
                step_kernel, (), (state, near, far), [tiles(2, 8), tiles(2, 16)]
            )
        else:
            state = call(last_kernel, (thermal_levels,), (state, near, far), tiles(2, 16))
    mates = on_chip(along_ladder(state, rungs, domains), domains)
    out = jax.ShapeDtypeStruct(particle_coordinates.shape, F32)
    new_x, new_v = call(
        swap_kernel, (where_to, thermal_levels), (state, mates), [out, out]
    )
    return new_x, new_v


def solution(mesh):
    return jax.shard_map(
        on_device,
        mesh=mesh,
        in_specs=(
            P("replica", None, "space"),
            P("replica", None, "space"),
            P("replica", "space"),
            P("replica", "space"),
            P("replica", None, "space"),
            P("replica", None, "space"),
            P("replica", None, "space"),
            P(),
            P("replica"),
            P("replica"),
            P(),
            P(),
            P(),
            P(),
            P(),
        ),
        out_specs=(P("replica", None, "space"), P("replica", None, "space")),
        check_vma=False,
    )
```

time: 334 us -> 77.4 us (0.23)
  the two profiles are of different devices: /device:TPU:7 before, /device:TPU:1 now
where the time goes in v1:
time: 77.4 us; the launch traced here: 77 us
  blocking collectives  53.1 us (69%)
  Pallas kernels  17.2 us (22%)
  local copies, waits for them, and re-layouts  4.55 us (6%)
  between operations  2.03 us (3%)
    all_gather x8, blocking collectives, on_chip(): return lax.all_gather(value, 'space', axis_index_groups=groups)  30.4 us
    pallas_call x5, Pallas kernels, call(): pl.pallas_call(kernel, out_shape=out_shape, in_specs=[smem()] * len(scala...  15.7 us
    all_gather x4, blocking collectives, across_chips(): return lax.all_gather(value, 'space', axis_index_groups=groups)  15.2 us
    all_gather x1, blocking collectives, along_ladder(): return lax.all_gather(value, ('replica', 'space'), axis_index_groups=groups)  7.48 us
    unnamed x26, local copies, waits for them, and re-layouts  3.38 us

profile of v1, /device:TPU:1, one launch (start us, length us, event | category | flops | bytes accessed | tf_op | source)
XLA Modules:
  0.0 77.0 jit_solution(5224988298329628844)
XLA Ops:
  1.3 0.0 copy-start.9
  1.3 0.1 pad_add_fusion.core_ref.where_ref
  1.4 0.6 copy-done.9
  2.0 0.0 copy-start.10
  2.0 0.6 copy.25.x_ref
  2.6 0.1 copy-done.10
  2.7 0.6 copy.26.v_ref
  3.3 1.5 %shard_map.158 = f32[24,128]{1,0:T(8,128)} custom-call(f32[1,3,256]{2,1,0:T(4,128)} %copy.25.x_ref, f32[1,3,256]{2,1,0:T(4,128)} %copy.26.v_ref, s32[1,256]{1,0:T(1,128)} %kind_ref.5, s32[1,4,64]{2,1,0:T(4,128)} %border_ref.1, f32[6]{0:T(128)} %inertia_ref.1), custom_call_target="tpu_custom_call" | custom-call | tf_op jit(solution)/shard_map/pallas_call | solution.py:450
  4.8 8.6 %all-gather = f32[48,128]{1,0:T(8,128)S(1)} all-gather(f32[24,128]{1,0:T(8,128)} %shard_map.158), channel_id=2, replica_groups={{0,1},{2,3},{4,5},{6,7},{8,9},{10,11},{12,13},{14,15},{16,17},{18,19},{..., dimensions={0}, use_global_device_ids=true | all-gather | bytes 36864 | tf_op jit(solution)/shard_map/all_gather | solution.py:406
  13.4 0.0 copy-start.7
  13.4 0.0 copy-start
  13.4 3.9 %all-gather.1 = f32[4,8,128]{2,1,0:T(8,128)S(1)} all-gather(f32[2,8,128]{2,1,0:T(8,128)S(1)} %slice.17.near_ref), channel_id=3, replica_groups={{31,0},{1,2},{3,4},{5,6},{7,8},{9,10},{11,12},{13,14},{15,16},{17,18},{..., dimensions={0}, use_global_device_ids=true | all-gather | bytes 24576 | tf_op jit(solution)/shard_map/all_gather | solution.py:411
  17.3 4.5 %all-gather.2 = f32[4,2,8,128]{3,2,1,0:T(8,128)S(1)} all-gather(f32[2,2,8,128]{3,2,1,0:T(8,128)S(1)} %bitcast.40), channel_id=4, replica_groups={{0,1},{2,3},{4,5},{6,7},{8,9},{10,11},{12,13},{14,15},{16,17},{18,19},{..., dimensions={0}, use_global_device_ids=true | all-gather | bytes 49152 | tf_op jit(solution)/shard_map/all_gather | solution.py:406
  21.8 0.0 copy-done.7
  21.8 0.0 copy-start.8
  21.8 0.1 copy.27.intake_ref
  22.0 0.6 copy-done.8
  22.5 0.0 copy-start.1
  22.5 0.0 copy-start.2
  22.5 0.0 copy-start.4
  22.5 0.0 copy-start.5
  22.5 0.0 copy-start.6
  22.6 0.1 copy.28.opening_ref
  22.7 0.0 copy-start.3
  22.7 0.0 copy-done
  22.7 0.6 copy-done.1
  23.3 0.0 copy-done.2
  23.3 0.0 copy-done.4
  23.3 0.0 copy-done.5
  23.3 0.0 copy-done.6
  23.3 0.1 copy-done.3
  23.4 7.4 %shard_map.159 = f32[16,128]{1,0:T(8,128)S(1)} custom-call(s32[4]{0:T(128)S(1)} %pad_add_fusion.core_ref.where_ref, f32[2,16,128]{2,1,0:T(8,128)S(1)} %slice.16.state_ref, f32[2,8,128]{2,1,0:T(8,128)S(1)} %slice.17.near_ref, f32[2,2,2,8,128]{4,3,2,1,0:T(8,128)S(1)} %bitcast.23, s32[1,32,256]{2,1,0:T(8,128)S(1)} %copy-done.1, s32[1,32,256]{2,1,0:T(8,128)S(1)} %copy-done.2, ...), custom_call_target="tpu_custom_call" | custom-call | tf_op jit(solution)/shard_map/pallas_call | solution.py:379
  30.7 1.8 %all-gather.3 = f32[32,128]{1,0:T(8,128)S(1)} all-gather(f32[16,128]{1,0:T(8,128)S(1)} %shard_map.159), channel_id=5, replica_groups={{0,1},{2,3},{4,5},{6,7},{8,9},{10,11},{12,13},{14,15},{16,17},{18,19},{..., dimensions={0}, use_global_device_ids=true | all-gather | bytes 24576 | tf_op jit(solution)/shard_map/all_gather | solution.py:406
  32.6 3.8 %all-gather.4 = f32[4,8,128]{2,1,0:T(8,128)S(1)} all-gather(f32[2,8,128]{2,1,0:T(8,128)S(1)} %slice.18), channel_id=6, replica_groups={{31,0},{1,2},{3,4},{5,6},{7,8},{9,10},{11,12},{13,14},{15,16},{17,18},{..., dimensions={0}, use_global_device_ids=true | all-gather | bytes 24576 | tf_op jit(solution)/shard_map/all_gather | solution.py:411
  36.3 3.9 %all-gather.5 = f32[4,2,8,128]{3,2,1,0:T(8,128)S(1)} all-gather(f32[2,2,8,128]{3,2,1,0:T(8,128)S(1)} %bitcast.38), channel_id=7, replica_groups={{0,1},{2,3},{4,5},{6,7},{8,9},{10,11},{12,13},{14,15},{16,17},{18,19},{..., dimensions={0}, use_global_device_ids=true | all-gather | bytes 49152 | tf_op jit(solution)/shard_map/all_gather | solution.py:406
  40.3 0.2 shard_map.160
  40.5 3.8 %all-gather.6 = f32[4,8,128]{2,1,0:T(8,128)S(1)} all-gather(f32[2,8,128]{2,1,0:T(8,128)S(1)} %get-tuple-element.5.near_ref), channel_id=8, replica_groups={{31,0},{1,2},{3,4},{5,6},{7,8},{9,10},{11,12},{13,14},{15,16},{17,18},{..., dimensions={0}, use_global_device_ids=true | all-gather | bytes 24576 | tf_op jit(solution)/shard_map/all_gather | solution.py:411
  44.3 3.9 %all-gather.7 = f32[4,2,8,128]{3,2,1,0:T(8,128)S(1)} all-gather(f32[2,2,8,128]{3,2,1,0:T(8,128)S(1)} %bitcast.41), channel_id=9, replica_groups={{0,1},{2,3},{4,5},{6,7},{8,9},{10,11},{12,13},{14,15},{16,17},{18,19},{..., dimensions={0}, use_global_device_ids=true | all-gather | bytes 49152 | tf_op jit(solution)/shard_map/all_gather | solution.py:406
  48.2 7.4 %shard_map.161 = f32[16,128]{1,0:T(8,128)S(1)} custom-call(s32[4]{0:T(128)S(1)} %pad_add_fusion.core_ref.where_ref, f32[2,16,128]{2,1,0:T(8,128)S(1)} %get-tuple-element.4.state_ref, f32[2,8,128]{2,1,0:T(8,128)S(1)} %get-tuple-element.5.near_ref, f32[2,2,2,8,128]{4,3,2,1,0:T(8,128)S(1)} %bitcast.24, s32[1,32,256]{2,1,0:T(8,128)S(1)} %copy-done.1, ...), custom_call_target="tpu_custom_call" | custom-call | tf_op jit(solution)/shard_map/pallas_call | solution.py:379
  55.6 1.8 %all-gather.8 = f32[32,128]{1,0:T(8,128)S(1)} all-gather(f32[16,128]{1,0:T(8,128)S(1)} %shard_map.161), channel_id=10, replica_groups={{0,1},{2,3},{4,5},{6,7},{8,9},{10,11},{12,13},{14,15},{16,17},{18,19},{..., dimensions={0}, use_global_device_ids=true | all-gather | bytes 24576 | tf_op jit(solution)/shard_map/all_gather | solution.py:406
  57.4 3.8 %all-gather.9 = f32[4,8,128]{2,1,0:T(8,128)S(1)} all-gather(f32[2,8,128]{2,1,0:T(8,128)S(1)} %slice.19), channel_id=11, replica_groups={{31,0},{1,2},{3,4},{5,6},{7,8},{9,10},{11,12},{13,14},{15,16},{17,18},{..., dimensions={0}, use_global_device_ids=true | all-gather | bytes 24576 | tf_op jit(solution)/shard_map/all_gather | solution.py:411
  61.2 3.9 %all-gather.10 = f32[4,2,8,128]{3,2,1,0:T(8,128)S(1)} all-gather(f32[2,2,8,128]{3,2,1,0:T(8,128)S(1)} %bitcast.39), channel_id=12, replica_groups={{0,1},{2,3},{4,5},{6,7},{8,9},{10,11},{12,13},{14,15},{16,17},{18,19},{..., dimensions={0}, use_global_device_ids=true | all-gather | bytes 49152 | tf_op jit(solution)/shard_map/all_gather | solution.py:406
  65.7 0.2 shard_map.162.own_ref
  65.9 7.5 %all-gather.11 = f32[4,16,128]{2,1,0:T(8,128)S(1)} all-gather(f32[2,16,128]{2,1,0:T(8,128)S(1)} %shard_map.162.own_ref), channel_id=13, replica_groups={{0,32},{64,96},{128,160},{192,224},{256,288},{320,352},{384,416},{448,4..., dimensions={0}, use_global_device_ids=true | all-gather | bytes 49152 | tf_op jit(solution)/shard_map/all_gather | solution.py:421
  73.4 1.8 %all-gather.12 = f32[4,2,16,128]{3,2,1,0:T(8,128)S(1)} all-gather(f32[2,2,16,128]{3,2,1,0:T(8,128)S(1)} %bitcast.35), channel_id=14, replica_groups={{0,1},{2,3},{4,5},{6,7},{8,9},{10,11},{12,13},{14,15},{16,17},{18,19},{..., dimensions={0}, use_global_device_ids=true | all-gather | bytes 98304 | tf_op jit(solution)/shard_map/all_gather | solution.py:406
  75.2 0.6 shard_map.163
  75.8 0.6 copy.31
  76.4 0.6 copy.32
  (4 shorter events, 0.0 us)
Async XLA Ops:
  1.3 0.7 copy-start.9
  2.0 0.7 copy-start.10
  13.4 8.5 %copy-start.7 = (bf16[256,28]{0,1:T(8,128)(2,1)S(1)}, bf16[256,28]{0,1:T(8,128)(2,1)}, u32[]{:S(2)}) copy-start(bf16[256,28]{0,1:T(8,128)(2,1)} %param.25) | copy-start | bytes 43012
  13.4 9.3 %copy-start = (bf16[256,256]{1,0:T(8,128)(2,1)S(1)}, bf16[256,256]{1,0:T(8,128)(2,1)}, u32[]{:S(2)}) copy-start(bf16[256,256]{1,0:T(8,128)(2,1)} %middle_ref.3) | copy-start | bytes 393220
  21.8 0.7 copy-start.8
  22.5 0.8 copy-start.1
  22.5 0.8 %copy-start.2 = (s32[1,32,256]{2,1,0:T(8,128)S(1)}, s32[1,32,256]{2,1,0:T(8,128)}, u32[]{:S(2)}) copy-start(s32[1,32,256]{2,1,0:T(8,128)} %place_kind_ref.3) | copy-start | bytes 98308
  22.5 0.8 %copy-start.4 = (s32[1,256]{1,0:T(1,128)S(1)}, s32[1,256]{1,0:T(1,128)}, u32[]{:S(2)}) copy-start(s32[1,256]{1,0:T(1,128)} %total_ref.3) | copy-start | bytes 3076
  22.5 0.8 %copy-start.5 = (f32[256]{0:T(256)S(1)}, f32[256]{0:T(256)}, u32[]{:S(2)}) copy-start(f32[256]{0:T(256)} %param.26) | copy-start | bytes 3076
  22.5 0.8 %copy-start.6 = (f32[256]{0:T(256)S(1)}, f32[256]{0:T(256)}, u32[]{:S(2)}) copy-start(f32[256]{0:T(256)} %param.29) | copy-start | bytes 3076
  22.7 0.7 copy-start.3

commit v2 on v1

v2 whole, which is shorter than its diff:
```python
import functools

import jax
import jax.numpy as jnp
from jax import lax
from jax.experimental import pallas as pl
from jax.experimental.pallas import tpu as pltpu
from jax.sharding import PartitionSpec as P

STEPS = 2
TIME_STEP = 0.05
CUT_SQ = 9.0
N_BASIS = 8
N_KIND = 6
LANES = 128
SLOTS = 32
GROUPS = SLOTS // 8
HIDDEN = 256
AHEAD = 3
SHARP = (N_BASIS / CUT_SQ) ** 2
CENTRES = [CUT_SQ * c / (N_BASIS - 1) for c in range(N_BASIS)]
F32 = jnp.float32
BF16 = jnp.bfloat16


def nt_dot(a, b):
    return lax.dot_general(a, b, (((1,), (1,)), ((), ())), preferred_element_type=F32)


def tn_dot(a, b):
    return lax.dot_general(a, b, (((0,), (0,)), ((), ())), preferred_element_type=F32)


def nn_dot(a, b):
    return lax.dot_general(a, b, (((1,), (0,)), ((), ())), preferred_element_type=F32)


def tile_of(flat_ref):
    rows = [
        flat_ref[:, (comp * 2 + chunk) * LANES : (comp * 2 + chunk + 1) * LANES]
        for chunk in range(2)
        for comp in range(3)
    ]
    return jnp.concatenate(rows, axis=0)


def put_flat(flat_ref, tile):
    for chunk in range(2):
        for comp in range(3):
            start = (comp * 2 + chunk) * LANES
            row = chunk * 3 + comp
            flat_ref[:, start : start + LANES] = tile[row : row + 1]


def rows_of_two(first, second, pad_with=None):
    shape = (3, LANES)
    pad = jnp.zeros((2, LANES), first.dtype)
    return jnp.concatenate(
        [jnp.broadcast_to(first, shape), jnp.broadcast_to(second, shape), pad], axis=0
    )


def take_lanes(table, lane):
    return jnp.take_along_axis(table, lane, axis=1, mode="promise_in_bounds")


def border_positions(tile, border0, border1):
    index = rows_of_two(border0, border1)
    pad = jnp.zeros((2, LANES), F32)
    low = jnp.concatenate([tile[0:3], tile[0:3], pad], axis=0)
    high = jnp.concatenate([tile[3:6], tile[3:6], pad], axis=0)
    lane = index & (LANES - 1)
    return jnp.where(index < LANES, take_lanes(low, lane), take_lanes(high, lane))


def four_sets(set0, set1, set2, set3):
    row = lax.broadcasted_iota(jnp.int32, (8, LANES), 0)
    col = lax.broadcasted_iota(jnp.int32, (8, LANES), 1)
    left = col < LANES // 2
    return jnp.where(row < 3, jnp.where(left, set0, set1), jnp.where(left, set2, set3))


def split_parts(value, count):
    parts = []
    for _ in range(count):
        part = value.astype(BF16).astype(F32)
        parts.append(part)
        value = value - part
    return parts


def start_kernel(x_ref, v_ref, kind_ref, border_ref, inertia_ref, out_ref):
    x_tile = tile_of(x_ref)
    border = border_ref[0]
    border0 = jnp.concatenate([border[0:1], border[1:2]], axis=1)
    border1 = jnp.concatenate([border[2:3], border[3:4]], axis=1)
    kind = kind_ref[...]
    inverse = jnp.zeros(kind.shape, F32)
    for k in range(N_KIND):
        inverse = jnp.where(kind == k, inertia_ref[k], inverse)
    out_ref[0:8] = border_positions(x_tile, border0, border1)
    out_ref[8:14] = x_tile
    out_ref[14:15] = inverse[:, :LANES]
    out_ref[15:16] = inverse[:, LANES:]
    out_ref[16:22] = tile_of(v_ref)
    out_ref[22:23] = border0.astype(F32)
    out_ref[23:24] = border1.astype(F32)


def fed_columns():
    feature = lax.broadcasted_iota(jnp.int32, (28, LANES), 0)
    col = lax.broadcasted_iota(jnp.int32, (28, LANES), 1)
    block, which = col // 8, col % 8
    radial = (block < 8) & (feature == block)
    environ = (block == 8) & (feature == 8 + which)
    centre = (block == 9) & (which < N_KIND) & (feature == 16 + which)
    neigh = (block >= 10) & (feature == 22 + block - 10)
    return (radial | environ | centre | neigh).astype(F32)


def own_columns(slot, rows):
    col = lax.broadcasted_iota(jnp.int32, (rows, LANES), 1)
    return (col // 8 == 8) | (col // 8 == 9) | (col % 8 == slot)


def two_parts(value):
    high, low = split_parts(value, 2)
    return jnp.concatenate([high, low], axis=0).astype(BF16)


def weight_kernel(
    index_ref, intake_ref, edge_out_ref, opening_ref, middle_ref, atom_out_ref,
    up_ref, down_ref, line_ref, flat_ref, sum_ref, hot_ref, atom_ref, first_ref, second_ref, back_ref,
):
    intake = intake_ref[...]
    fed = fed_columns()
    for j in range(8):
        up = jnp.where(own_columns(j, 28), 0.5 * fed, 0.0).astype(BF16)
        up_ref[j * HIDDEN : (j + 1) * HIDDEN, :] = tn_dot(intake, up).astype(BF16)
    edge_w = edge_out_ref[...]
    weighted = intake.astype(F32) * (0.5 * edge_w)
    down_ref[...] = two_parts(weighted[0:16])
    line = jnp.sum(weighted, axis=1, keepdims=True)
    flat_ref[...] = jnp.broadcast_to(line[0:16], (16, LANES))
    line = jnp.sum(fed * line, axis=0, keepdims=True)
    slot = lax.broadcasted_iota(jnp.int32, (8, LANES), 0)
    line_ref[...] = two_parts(jnp.where(own_columns(slot, 8), line, 0.0))
    wide = jnp.transpose(jnp.broadcast_to(edge_w, (LANES, HIDDEN)))
    sum_ref[...] = jnp.concatenate([wide, wide], axis=1).astype(BF16)
    atom_ref[...] = jnp.transpose(jnp.broadcast_to(0.5 * atom_out_ref[...], (LANES, HIDDEN)))
    first_ref[...] = jnp.transpose((0.5 * opening_ref[...]).astype(F32)).astype(BF16)
    second_ref[...] = 0.5 * middle_ref[...]
    back_ref[...] = jnp.transpose(middle_ref[...].astype(F32)).astype(BF16)
    place = lax.broadcasted_iota(jnp.int32, (LANES, 2 * LANES), 0)

    def group(s, carry):
        for j in range(8):
            lane = index_ref[0, pl.ds(s * 8 + j, 1), :] & (LANES - 1)
            hot_ref[:, pl.ds(pl.multiple_of((s * 8 + j) * 256, 256), 256)] = (place == lane).astype(F32).astype(BF16)
        return carry

    lax.fori_loop(0, GROUPS, group, 0)


def far_tiles(far_ref):
    if len(far_ref.shape) == 5:
        return far_ref[0, 0, 0], far_ref[0, 0, 1], far_ref[1, 1, 0], far_ref[1, 1, 1]
    return far_ref[0, 0], far_ref[0, 1], far_ref[1, 0], far_ref[1, 1]


def force_kernel(
    core_ref,
    state_ref,
    near_ref,
    far_ref,
    index_ref,
    place_kind_ref,
    total_ref,
    kind_ref,
    up_ref,
    down_ref,
    line_ref,
    flat_ref,
    sum_ref,
    hot_ref,
    atom_ref,
    first_ref,
    second_ref,
    back_ref,
    opening_ref,
    out_ref,
    feat_ref,
    gauss_ref,
    geo_ref,
    energy_ref,
    gin0_ref,
    gin1_ref,
    scat0_ref,
    scat1_ref,
):
    core = core_ref[0]
    first_core = core == 0
    own = state_ref[core]
    minus2, minus1, plus2, plus3 = far_tiles(far_ref)
    near0, near1 = near_ref[0], near_ref[1]

    def pick(a, b):
        return jnp.where(first_core, a, b)

    ghost = four_sets(
        pick(minus1, near0), pick(near1, plus2), pick(minus2, minus1), pick(plus2, plus3)
    )

    kind_rows = lax.broadcasted_iota(jnp.int32, (8, 2 * LANES), 0)
    centre_hot = (kind_rows == kind_ref[...]).astype(F32)
    slot_row = lax.broadcasted_iota(jnp.int32, (8, LANES), 0)
    tables = [
        [jnp.broadcast_to(t[r * 3 + c : r * 3 + c + 1], (8, LANES)) for c in range(3)]
        for t in (own, ghost)
        for r in range(2)
    ]

    def geometry(s, sums):
        sums = list(sums)
        slots = pl.ds(pl.multiple_of(s * 8, 8), 8)
        radials = [[], []]
        for h in range(2):
            cols = slice(h * LANES, (h + 1) * LANES)
            index = index_ref[0, slots, cols]
            lane = index & (LANES - 1)
            chunk = index // LANES
            dist_sq = None
            for comp in range(3):
                found = take_lanes(tables[0][comp], lane)
                for which in range(1, 4):
                    found = jnp.where(chunk == which, take_lanes(tables[which][comp], lane), found)
                vec = found - tables[h][comp]
                geo_ref[comp, s, :, cols] = vec
                dist_sq = vec * vec if comp == 0 else dist_sq + vec * vec
            live = slot_row + s * 8 < total_ref[:, cols]
            inside = 1.0 - dist_sq * (1.0 / CUT_SQ)
            used = live & (inside > 0.0)
            cutoff = jnp.where(used, inside * inside, 0.0)
            geo_ref[3, s, :, cols] = dist_sq
            geo_ref[4, s, :, cols] = cutoff
            geo_ref[5, s, :, cols] = jnp.where(used, inside * (-2.0 / CUT_SQ), 0.0)
            for c in range(N_BASIS):
                gap = dist_sq - CENTRES[c]
                gauss = jnp.exp(-SHARP * (gap * gap))
                gauss_ref[s, c * 8 : c * 8 + 8, cols] = gauss
                radial = gauss * cutoff
                radials[h].append(radial)
                sums[h * N_BASIS + c] = sums[h * N_BASIS + c] + radial
        place_kind = place_kind_ref[0, slots, :]
        rows = [jnp.concatenate([a, b], axis=1) for a, b in zip(*radials)]
        feat_ref[s, 0:64] = jnp.concatenate(rows, axis=0).astype(BF16)
        rows = [(place_kind == k).astype(F32) for k in range(N_KIND)]
        feat_ref[s, 80:128] = jnp.concatenate(rows, axis=0).astype(BF16)
        return tuple(sums)

    nothing = jnp.zeros((8, LANES), F32)
    sums = lax.fori_loop(0, GROUPS, geometry, (nothing,) * (2 * N_BASIS))
    rows = [jnp.sum(value, axis=0, keepdims=True) for value in sums]
    environ = jnp.concatenate(
        [jnp.concatenate(rows[:N_BASIS], axis=0), jnp.concatenate(rows[N_BASIS:], axis=0)], axis=1
    )
    shared = jnp.concatenate([environ, centre_hot], axis=0).astype(BF16)
    for s in range(GROUPS):
        feat_ref[s, 64:80] = shared

    atom_w = jnp.concatenate([atom_ref[...], atom_ref[...]], axis=1)
    half = nn_dot(first_ref[...], environ.astype(BF16))
    th = jnp.tanh(half)
    hidden_one = (half + half * th).astype(BF16)
    slope_one = 0.5 * (1.0 + th + half * (1.0 - th * th))
    half = nn_dot(second_ref[...], hidden_one)
    th = jnp.tanh(half)
    g_second = (atom_w * (1.0 + th + half * (1.0 - th * th))).astype(BF16)
    g_hidden = nn_dot(back_ref[...], g_second)
    g_first = (g_hidden * slope_one).astype(BF16)
    g_env = nn_dot(opening_ref[...], g_first)

    flat = jnp.concatenate([flat_ref[...], flat_ref[...]], axis=1)
    slot = lax.broadcasted_iota(jnp.int32, (16, HIDDEN), 0)
    quarter = lax.broadcasted_iota(jnp.int32, (16, HIDDEN), 1) // (HIDDEN // 4)
    members = [(slot == quarter + 4 * k).astype(F32).astype(BF16) for k in range(2)]

    def group(s, g_env):
        feat = feat_ref[s]
        line = nn_dot(line_ref[...], feat)
        energy = line[0:8] + line[8:16]
        folded = []

        def forward(j):
            return nn_dot(up_ref[j * HIDDEN : (j + 1) * HIDDEN, :], feat).astype(BF16)

        ahead = [forward(j) for j in range(AHEAD)]
        for j in range(8):
            half = ahead.pop(0)
            if j + AHEAD < 8:
                ahead.append(forward(j + AHEAD))
            th = jnp.tanh(half)
            rest = sum_ref[...] * (half * th)
            rest = rest[: HIDDEN // 2] + rest[HIDDEN // 2 :]
            folded.append(rest[: HIDDEN // 4] + rest[HIDDEN // 4 :])
            slope = th + half * (jnp.asarray(1.0, BF16) - th * th)
            g_in = nn_dot(down_ref[...], slope)
            cut = geo_ref[4, s, j : j + 1, :]
            g_in = (g_in[0:16] + g_in[16:32] + flat) * cut
            rows = pl.ds(s * 64 + j, 8, stride=8)
            gin0_ref[rows, :] = g_in[0:8, :LANES]
            gin1_ref[rows, :] = g_in[0:8, LANES:]
            g_env = g_env + g_in[8:16]
        for k in range(2):
            rest = jnp.concatenate(folded[k * 4 : k * 4 + 4], axis=0)
            energy = energy + nn_dot(members[k], rest)[0:8]
        energy_ref[s] = energy
        return g_env

    g_env = lax.fori_loop(0, GROUPS, group, g_env)

    def backward(s, sums):
        sums = list(sums)
        slots = slice(s * 8, s * 8 + 8)
        for h in range(2):
            cols = slice(h * LANES, (h + 1) * LANES)
            dist_sq, cutoff, slope = (geo_ref[k, s, :, cols] for k in (3, 4, 5))
            g_cut = energy_ref[s, :, cols]
            g_gap = None
            gin = (gin0_ref, gin1_ref)[h]
            for c in range(N_BASIS):
                rows = slice(s * 64 + c * 8, s * 64 + c * 8 + 8)
                g_radial = gin[rows, :] + g_env[c : c + 1, cols]
                q = g_radial * gauss_ref[s, c * 8 : c * 8 + 8, cols]
                g_cut = g_cut + q
                moment = q * (dist_sq - CENTRES[c])
                g_gap = moment if g_gap is None else g_gap + moment
            g_dist = (-4.0 * SHARP) * (cutoff * g_gap) + 2.0 * (g_cut * slope)
            chunk = index_ref[0, slots, cols] // LANES
            scat = (scat0_ref, scat1_ref)[h]
            for comp in range(3):
                g_vec = g_dist * geo_ref[comp, s, :, cols]
                sums[h * 3 + comp] = sums[h * 3 + comp] + g_vec
                for part, value in enumerate(split_parts(g_vec, 2)):
                    for which in range(4):
                        row = s * 8 * 24 + part * 12 + which * 3 + comp
                        scat[pl.ds(row, 8, stride=24), :] = jnp.where(chunk == which, value, 0.0)
        return tuple(sums)

    sums = (nothing,) * 6
    for s in range(GROUPS):
        sums = backward(s, sums)

    lhs = []
    for slot in range(SLOTS):
        rows = slice(slot * 24, slot * 24 + 24)
        lhs.append(jnp.concatenate([scat0_ref[rows, :], scat1_ref[rows, :]], axis=1).astype(BF16))
    total = nt_dot(jnp.concatenate(lhs, axis=1), hot_ref[...])
    total = total[0:12] + total[12:24]
    centre = jnp.concatenate([jnp.sum(value, axis=0, keepdims=True) for value in sums], axis=0)
    pad = jnp.zeros((2, LANES), F32)
    out_ref[0:8] = jnp.concatenate([total[6:12], pad], axis=0)
    out_ref[8:16] = jnp.concatenate([total[0:6] - centre, pad], axis=0)


def returned_sum(returned, border0, border1):
    row = lax.broadcasted_iota(jnp.int32, (8, LANES), 0)
    place = lax.broadcasted_iota(jnp.int32, (LANES, LANES), 0)
    lhs, rhs = [], []
    for which, border in enumerate((border0, border1)):
        three = returned[which * 3 : which * 3 + 3]
        twice = jnp.concatenate([three, three, jnp.zeros((2, LANES), F32)], axis=0)
        meant = (border // LANES == 1) == (row >= 3)
        kept = jnp.where(meant, twice, 0.0)
        lhs.append(jnp.concatenate(split_parts(kept, 3), axis=0).astype(BF16))
        rhs.append((place == (border & (LANES - 1))).astype(F32).astype(BF16))
    total = nt_dot(jnp.concatenate(lhs, axis=1), jnp.concatenate(rhs, axis=1))
    return total[0:8] + total[8:16] + total[16:24]


def moved(state_ref, near_ref, far_ref):
    minus2, minus1, plus2, plus3 = far_tiles(far_ref)
    near0, near1 = near_ref[0, 0:8], near_ref[1, 0:8]
    sets = ((near1, minus1, plus2, minus2), (plus2, near0, plus3, minus1))
    result = []
    for domain in range(2):
        state = state_ref[domain]
        border0 = state[14:15].astype(jnp.int32)
        border1 = state[15:16].astype(jnp.int32)
        inverse = rows_of_two(state[6:7], state[7:8])
        grad = near_ref[domain, 8:16] + returned_sum(four_sets(*sets[domain]), border0, border1)
        speed = state[8:16] - TIME_STEP * grad * inverse
        place = state[0:8] + TIME_STEP * speed
        result.append((place, speed, border0, border1))
    return result


def step_kernel(state_ref, near_ref, far_ref, send_ref, next_ref):
    for domain, (place, speed, border0, border1) in enumerate(moved(state_ref, near_ref, far_ref)):
        send_ref[domain] = border_positions(place, border0, border1)
        next_ref[domain, 0:6] = place[0:6]
        next_ref[domain, 6:8] = state_ref[domain, 6:8]
        next_ref[domain, 8:14] = speed[0:6]
        next_ref[domain, 14:16] = state_ref[domain, 14:16]


def last_kernel(level_ref, state_ref, near_ref, far_ref, next_ref):
    for domain, (place, speed, _, _) in enumerate(moved(state_ref, near_ref, far_ref)):
        next_ref[domain, 0:6] = place[0:6]
        next_ref[domain, 6:8] = jnp.full((2, LANES), level_ref[0], F32)
        next_ref[domain, 8:16] = speed


def swap_kernel(where_ref, level_ref, own_ref, mate_ref, x_ref, v_ref):
    core, swaps, side, position = (where_ref[k] for k in range(4))
    mine = own_ref[core]
    theirs = mate_ref[side, position, core]
    chosen = jnp.where(swaps == 1, theirs, mine)
    scale = jnp.sqrt(level_ref[0] / chosen[6:7])
    put_flat(x_ref, chosen[0:6])
    put_flat(v_ref, chosen[8:14] * scale)


def vmem():
    return pl.BlockSpec(memory_space=pltpu.VMEM)


def smem():
    return pl.BlockSpec(memory_space=pltpu.SMEM)


def tiles(*shape):
    return jax.ShapeDtypeStruct(shape + (LANES,), F32)


def call(kernel, scalars, arrays, out_shape, scratch=(), flops=10**6, limit=24 * 2**20):
    out_specs = [vmem() for _ in out_shape] if isinstance(out_shape, list) else vmem()
    return pl.pallas_call(
        kernel,
        out_shape=out_shape,
        in_specs=[smem()] * len(scalars) + [vmem()] * len(arrays),
        out_specs=out_specs,
        scratch_shapes=list(scratch),
        cost_estimate=pl.CostEstimate(flops=flops, bytes_accessed=10**6, transcendentals=0),
        compiler_params=pltpu.CompilerParams(vmem_limit_bytes=limit),
    )(*scalars, *arrays)


def weight_shapes():
    return [
        jax.ShapeDtypeStruct((8 * HIDDEN, LANES), BF16),
        jax.ShapeDtypeStruct((32, HIDDEN), BF16),
        jax.ShapeDtypeStruct((16, LANES), BF16),
        tiles(16),
        jax.ShapeDtypeStruct((HIDDEN, 2 * LANES), BF16),
        jax.ShapeDtypeStruct((LANES, SLOTS * 2 * LANES), BF16),
        tiles(HIDDEN),
        jax.ShapeDtypeStruct((HIDDEN, N_BASIS), BF16),
        jax.ShapeDtypeStruct((HIDDEN, HIDDEN), BF16),
        jax.ShapeDtypeStruct((HIDDEN, HIDDEN), BF16),
    ]


def force_scratch():
    return [
        pltpu.VMEM((GROUPS, 128, 2 * LANES), BF16),
        pltpu.VMEM((GROUPS, 64, 2 * LANES), F32),
        pltpu.VMEM((6, GROUPS, 8, 2 * LANES), F32),
        pltpu.VMEM((GROUPS, 8, 2 * LANES), F32),
        pltpu.VMEM((GROUPS * 64, LANES), F32),
        pltpu.VMEM((GROUPS * 64, LANES), F32),
        pltpu.VMEM((SLOTS * 24, LANES), F32),
        pltpu.VMEM((SLOTS * 24, LANES), F32),
    ]


def on_chip(value, domains):
    groups = [[2 * i, 2 * i + 1] for i in range(domains // 2)]
    return lax.all_gather(value, "space", axis_index_groups=groups)


def across_chips(value, domains):
    groups = [[(2 * i - 1) % domains, 2 * i] for i in range(domains // 2)]
    return lax.all_gather(value, "space", axis_index_groups=groups)


def partner_across(value, domains):
    pairs = []
    for i in range(domains // 2):
        odd, even = (2 * i - 1) % domains, 2 * i
        pairs += [(odd, even), (even, odd)]
    return lax.ppermute(value, "space", pairs)


def along_ladder(value, rungs, domains):
    groups = []
    for domain in range(domains):
        shift = domain % 2
        for low in range(shift, rungs, 2):
            high = (low + 1) % rungs
            groups.append([low * domains + domain, high * domains + domain])
    return lax.all_gather(value, ("replica", "space"), axis_index_groups=groups)


def on_device(
    particle_coordinates,
    particle_motions,
    particle_kinds,
    filled_totals,
    adjacent_particles,
    adjacent_place_kinds,
    border_particle_numbers,
    reciprocal_kind_inertia,
    thermal_levels,
    swap_mates,
    bond_intake_coefficients,
    bond_output_coefficients,
    particle_opening_coefficients,
    particle_middle_coefficients,
    particle_output_coefficients,
):
    domains, rungs = lax.axis_size("space"), lax.axis_size("replica")
    core = lax.axis_index("space") % 2
    rank = lax.axis_index("replica")
    mate = swap_mates[0]
    odd = rank % 2
    side = jnp.where((mate > rank) == (odd == 0), 0, 1)
    position = jnp.where(side == 0, 1 - odd, odd)
    where_to = jnp.stack([core, (mate != rank).astype(jnp.int32), side, position]).astype(jnp.int32)

    begin = pl.pallas_call(
        start_kernel,
        out_shape=tiles(24),
        in_specs=[vmem()] * 4 + [smem()],
        out_specs=vmem(),
        compiler_params=pltpu.CompilerParams(vmem_limit_bytes=16 * 2**20),
    )(
        particle_coordinates.reshape(1, -1),
        particle_motions.reshape(1, -1),
        particle_kinds,
        border_particle_numbers,
        reciprocal_kind_inertia,
    )
    weights = call(
        weight_kernel,
        (),
        (
            adjacent_particles,
            bond_intake_coefficients.T,
            bond_output_coefficients[None],
            particle_opening_coefficients.T,
            particle_middle_coefficients,
            particle_output_coefficients[None],
        ),
        weight_shapes(),
        flops=10**9,
    )
    both = on_chip(begin, domains)
    send, state = both[:, 0:8], both[:, 8:24]
    for step in range(STEPS):
        if step == 0:
            far = on_chip(partner_across(send, domains), domains)
        else:
            far = on_chip(across_chips(send, domains), domains)
        partial = call(
            force_kernel,
            (where_to,),
            (
                state,
                send,
                far,
                adjacent_particles,
                adjacent_place_kinds,
                filled_totals,
                particle_kinds,
                *weights,
                particle_opening_coefficients.T,
            ),
            tiles(16),
            force_scratch(),
        )
        near = on_chip(partial, domains)
        far = on_chip(across_chips(near[:, 0:8], domains), domains)
        if step < STEPS - 1:
            send, state = call(step_kernel, (), (state, near, far), [tiles(2, 8), tiles(2, 16)])
        else:
            state = call(last_kernel, (thermal_levels,), (state, near, far), tiles(2, 16))
    mates = on_chip(along_ladder(state, rungs, domains), domains)
    shape = particle_coordinates.shape
    out = jax.ShapeDtypeStruct((1, particle_coordinates.size), F32)
    new_x, new_v = call(swap_kernel, (where_to, thermal_levels), (state, mates), [out, out])
    return new_x.reshape(shape), new_v.reshape(shape)


def solution(mesh):
    return jax.shard_map(
        on_device,
        mesh=mesh,
        in_specs=(
            P("replica", None, "space"),
            P("replica", None, "space"),
            P("replica", "space"),
            P("replica", "space"),
            P("replica", None, "space"),
            P("replica", None, "space"),
            P("replica", None, "space"),
            P(),
            P("replica"),
            P("replica"),
            P(),
            P(),
            P(),
            P(),
            P(),
        ),
        out_specs=(P("replica", None, "space"), P("replica", None, "space")),
        check_vma=False,
    )
```

time: 77.4 us -> 78.3 us (1.012)
  local copies, waits for them, and re-layouts: 4.55 us -> 7.84 us
  blocking collectives: 53.1 us -> 50.7 us
  Pallas kernels: 17.2 us -> 15.1 us
  starting transfers between devices: 0 us -> 1.91 us
    unnamed x26 -> x32, local copies, waits for them, and re-layouts: 3.38 us -> 7.83 us
    all_gather x4 -> x3, blocking collectives: 15.2 us -> 11.3 us  [across_chips(): return lax.all_gather(value, 'space', axis_index_groups=groups)]
    ppermute x0 -> x1, starting transfers between devices: none -> 1.91 us  [partner_across(): return lax.ppermute(value, 'space', pairs)]
    all_gather x8, blocking collectives: 30.4 us -> 31.9 us  [on_chip(): return lax.all_gather(value, 'space', axis_index_groups=groups)]
    pallas_call x5 -> x6, Pallas kernels: 15.7 us -> 14.4 us  [call(): pl.pallas_call(kernel, out_shape=out_shape, in_specs=[smem()] * len(scala...]
    pallas_call x2 -> x0, local copies, waits for them, and re-layouts: 1.17 us -> none  [call(): pl.pallas_call(kernel, out_shape=out_shape, in_specs=[smem()] * len(scala...]
    pallas_call x1, Pallas kernels: 1.54 us -> 0.68 us  [on_device(): pl.pallas_call(start_kernel, out_shape=tiles(24), in_specs=[vmem()] * 4 +...]
  transfers between devices with their start and end apart: 0 -> 1, of which waited for: 0 -> 0; matrix products, arithmetic and copies ran while one was open for 0% -> 0% of each run, Pallas kernels for 0% -> 1%
where the time goes in v2:
time: 78.3 us; the launch traced here: 77.6 us
  blocking collectives  50.7 us (65%)
  Pallas kernels  15.1 us (19%)
  local copies, waits for them, and re-layouts  7.84 us (10%)
  between operations  2.05 us (3%)
  starting transfers between devices  1.91 us (2%)
    all_gather x8, blocking collectives, on_chip(): return lax.all_gather(value, 'space', axis_index_groups=groups)  31.9 us
    pallas_call x6, Pallas kernels, call(): pl.pallas_call(kernel, out_shape=out_shape, in_specs=[smem()] * len(scala...  14.4 us
    all_gather x3, blocking collectives, across_chips(): return lax.all_gather(value, 'space', axis_index_groups=groups)  11.3 us
    unnamed x32, local copies, waits for them, and re-layouts  7.83 us
    all_gather x1, blocking collectives, along_ladder(): return lax.all_gather(value, ('replica', 'space'), axis_index_groups=groups)  7.48 us
    ppermute x1, starting transfers between devices, partner_across(): return lax.ppermute(value, 'space', pairs)  1.91 us
  transfers between devices with their start and end apart: 1, of which 0 were waited for; matrix products, arithmetic and copies ran while one was open for 0% of the time, Pallas kernels for 1%

profile of v2, /device:TPU:1, one launch (start us, length us, event | category | flops | bytes accessed | tf_op | source)
XLA Modules:
  0.0 77.6 jit_solution(12824501607619009761)
XLA Ops:
  0.6 0.0 copy-start.1
  0.6 0.0 copy-start.2
  0.7 0.0 copy-start.5
  0.7 0.7 copy-done.5
  1.3 0.0 copy-start.8
  1.3 0.7 copy-done.8
  2.0 0.0 copy-start.9
  2.0 0.7 copy-done.9
  2.7 0.0 copy-start.10
  2.7 0.7 copy-done.10
  3.4 0.0 copy-start.11
  3.4 0.7 copy-done.11
  4.1 0.0 copy-start.6
  4.1 0.0 copy-start.7
  4.1 0.7 shard_map.158
  4.7 8.4 %all-gather = f32[48,128]{1,0:T(8,128)S(1)} all-gather(f32[24,128]{1,0:T(8,128)S(1)} %shard_map.158), channel_id=2, replica_groups={{0,1},{2,3},{4,5},{6,7},{8,9},{10,11},{12,13},{14,15},{16,17},{18,19},{..., dimensions={0}, use_global_device_ids=true | all-gather | bytes 36864 | tf_op jit(solution)/shard_map/all_gather | solution.py:479
  13.1 1.9 %collective-permute-start = (f32[2,8,128]{2,1,0:T(8,128)S(1)}, f32[2,8,128]{2,1,0:T(8,128)S(1)}, u32[]{:S(2)}, u32[]{:S(2)}) collective-permute-start(f32[2,8,128]{2,1,0:T(8,128)S(1)} %slice.17.near_ref), channel_id=1, source_target_pairs={{31,0},{0,31},{1,2},{2,1},{3,4},{4,3},{5,6},{6,5},{7,8},{8,7},{9,1... | collective-permute-start | bytes 24584 | tf_op jit(solution)/shard_map/ppermute | solution.py:492
  15.7 0.1 pad_add_fusion.core_ref.where_ref
  15.8 0.8 copy-done
  16.5 0.7 copy-done.3
  17.2 0.9 %copy-done.12 = bf16[256,256]{1,0:T(8,128)(2,1)S(1)} copy-done((bf16[256,256]{1,0:T(8,128)(2,1)S(1)}, bf16[256,256]{1,0:T(8,128)(2,1)}, u32[]{:S(2)}) %copy-start.12) | copy-done | bytes 131096
  18.1 0.7 copy-done.13
  18.8 0.7 copy-done.14
  19.5 0.7 copy-done.15
  20.2 1.1 %shard_map.159 = (bf16[2048,128]{1,0:T(8,128)(2,1)S(1)}, bf16[32,256]{1,0:T(8,128)(2,1)S(1)}, bf16[16,128]{1,0:T(8,128)(2,1)S(1)}, f32[16,128]{1,0:T(8,128)S(1)}...) custom-call(s32[1,32,256]{2,1,0:T(8,128)S(1)} %copy-done, ...), custom_call_target="tpu_custom_call" | custom-call | flops 1000000000 | bytes 1000000 | tf_op jit(solution)/shard_map/pallas_call | solution.py:438
  21.3 0.0 copy-start.4
  22.0 0.0 collective-permute-done
  22.0 6.3 %all-gather.1 = f32[4,8,128]{2,1,0:T(8,128)S(1)} all-gather(f32[2,8,128]{2,1,0:T(8,128)S(1)} %collective-permute-done), channel_id=3, replica_groups={{0,1},{2,3},{4,5},{6,7},{8,9},{10,11},{12,13},{14,15},{16,17},{18,19},{..., dimensions={0}, use_global_device_ids=true | all-gather | bytes 24576 | tf_op jit(solution)/shard_map/all_gather | solution.py:479
  28.3 0.0 copy-done.1
  28.3 0.0 copy-done.2
  28.3 0.0 copy-done.6
  28.3 0.0 copy-done.7
  28.3 5.9 %shard_map.160 = f32[16,128]{1,0:T(8,128)S(1)} custom-call(s32[4]{0:T(128)S(1)} %pad_add_fusion.core_ref.where_ref, f32[2,16,128]{2,1,0:T(8,128)S(1)} %slice.16.state_ref, f32[2,8,128]{2,1,0:T(8,128)S(1)} %slice.17.near_ref, f32[2,2,8,128]{3,2,1,0:T(8,128)S(1)} %bitcast.35, s32[1,32,256]{2,1,0:T(8,128)S(1)} %copy-done.1, s32[1,32,256]{2,1,0:T(8,128)S(1)} %copy-done.2, ...), custom_call_target="tpu_custom_call" | custom-call | flops 1000000 | bytes 1000000 | tf_op jit(solution)/shard_map/pallas_call | solution.py:438
  34.1 1.8 %all-gather.2 = f32[32,128]{1,0:T(8,128)S(1)} all-gather(f32[16,128]{1,0:T(8,128)S(1)} %shard_map.160), channel_id=4, replica_groups={{0,1},{2,3},{4,5},{6,7},{8,9},{10,11},{12,13},{14,15},{16,17},{18,19},{..., dimensions={0}, use_global_device_ids=true | all-gather | bytes 24576 | tf_op jit(solution)/shard_map/all_gather | solution.py:479
  36.0 3.8 %all-gather.3 = f32[4,8,128]{2,1,0:T(8,128)S(1)} all-gather(f32[2,8,128]{2,1,0:T(8,128)S(1)} %slice.18), channel_id=5, replica_groups={{31,0},{1,2},{3,4},{5,6},{7,8},{9,10},{11,12},{13,14},{15,16},{17,18},{..., dimensions={0}, use_global_device_ids=true | all-gather | bytes 24576 | tf_op jit(solution)/shard_map/all_gather | solution.py:484
  39.7 3.9 %all-gather.4 = f32[4,2,8,128]{3,2,1,0:T(8,128)S(1)} all-gather(f32[2,2,8,128]{3,2,1,0:T(8,128)S(1)} %bitcast.47), channel_id=6, replica_groups={{0,1},{2,3},{4,5},{6,7},{8,9},{10,11},{12,13},{14,15},{16,17},{18,19},{..., dimensions={0}, use_global_device_ids=true | all-gather | bytes 49152 | tf_op jit(solution)/shard_map/all_gather | solution.py:479
  43.7 0.2 shard_map.161
  43.9 3.8 %all-gather.5 = f32[4,8,128]{2,1,0:T(8,128)S(1)} all-gather(f32[2,8,128]{2,1,0:T(8,128)S(1)} %get-tuple-element.27.near_ref), channel_id=7, replica_groups={{31,0},{1,2},{3,4},{5,6},{7,8},{9,10},{11,12},{13,14},{15,16},{17,18},{..., dimensions={0}, use_global_device_ids=true | all-gather | bytes 24576 | tf_op jit(solution)/shard_map/all_gather | solution.py:484
  47.7 3.9 %all-gather.6 = f32[4,2,8,128]{3,2,1,0:T(8,128)S(1)} all-gather(f32[2,2,8,128]{3,2,1,0:T(8,128)S(1)} %bitcast.49), channel_id=8, replica_groups={{0,1},{2,3},{4,5},{6,7},{8,9},{10,11},{12,13},{14,15},{16,17},{18,19},{..., dimensions={0}, use_global_device_ids=true | all-gather | bytes 49152 | tf_op jit(solution)/shard_map/all_gather | solution.py:479
  51.6 0.0 copy-done.4
  51.6 5.9 %shard_map.162 = f32[16,128]{1,0:T(8,128)S(1)} custom-call(s32[4]{0:T(128)S(1)} %pad_add_fusion.core_ref.where_ref, f32[2,16,128]{2,1,0:T(8,128)S(1)} %get-tuple-element.26.state_ref, f32[2,8,128]{2,1,0:T(8,128)S(1)} %get-tuple-element.27.near_ref, f32[2,2,2,8,128]{4,3,2,1,0:T(8,128)S(1)} %bitcast.28, s32[1,32,256]{2,1,0:T(8,128)S(1)} %copy-done.1, ...), custom_call_target="tpu_custom_call" | custom-call | flops 1000000 | bytes 1000000 | tf_op jit(solution)/shard_map/pallas_call | solution.py:438
  57.5 1.8 %all-gather.7 = f32[32,128]{1,0:T(8,128)S(1)} all-gather(f32[16,128]{1,0:T(8,128)S(1)} %shard_map.162), channel_id=9, replica_groups={{0,1},{2,3},{4,5},{6,7},{8,9},{10,11},{12,13},{14,15},{16,17},{18,19},{..., dimensions={0}, use_global_device_ids=true | all-gather | bytes 24576 | tf_op jit(solution)/shard_map/all_gather | solution.py:479
  59.3 3.8 %all-gather.8 = f32[4,8,128]{2,1,0:T(8,128)S(1)} all-gather(f32[2,8,128]{2,1,0:T(8,128)S(1)} %slice.19), channel_id=10, replica_groups={{31,0},{1,2},{3,4},{5,6},{7,8},{9,10},{11,12},{13,14},{15,16},{17,18},{..., dimensions={0}, use_global_device_ids=true | all-gather | bytes 24576 | tf_op jit(solution)/shard_map/all_gather | solution.py:484
  63.1 3.9 %all-gather.9 = f32[4,2,8,128]{3,2,1,0:T(8,128)S(1)} all-gather(f32[2,2,8,128]{3,2,1,0:T(8,128)S(1)} %bitcast.48), channel_id=11, replica_groups={{0,1},{2,3},{4,5},{6,7},{8,9},{10,11},{12,13},{14,15},{16,17},{18,19},{..., dimensions={0}, use_global_device_ids=true | all-gather | bytes 49152 | tf_op jit(solution)/shard_map/all_gather | solution.py:479
  67.0 0.2 shard_map.163.own_ref
  67.2 7.5 %all-gather.10 = f32[4,16,128]{2,1,0:T(8,128)S(1)} all-gather(f32[2,16,128]{2,1,0:T(8,128)S(1)} %shard_map.163.own_ref), channel_id=12, replica_groups={{0,32},{64,96},{128,160},{192,224},{256,288},{320,352},{384,416},{448,4..., dimensions={0}, use_global_device_ids=true | all-gather | bytes 49152 | tf_op jit(solution)/shard_map/all_gather | solution.py:502
  74.6 1.8 %all-gather.11 = f32[4,2,16,128]{3,2,1,0:T(8,128)S(1)} all-gather(f32[2,2,16,128]{3,2,1,0:T(8,128)S(1)} %bitcast.44), channel_id=13, replica_groups={{0,1},{2,3},{4,5},{6,7},{8,9},{10,11},{12,13},{14,15},{16,17},{18,19},{..., dimensions={0}, use_global_device_ids=true | all-gather | bytes 98304 | tf_op jit(solution)/shard_map/all_gather | solution.py:479
  76.5 1.1 %shard_map.164 = (f32[1,768]{1,0:T(1,128)}, f32[1,768]{1,0:T(1,128)}) custom-call(s32[4]{0:T(128)S(1)} %pad_add_fusion.core_ref.where_ref, f32[1]{0:T(128)S(6)} %copy.23.level_ref, f32[2,16,128]{2,1,0:T(8,128)S(1)} %shard_map.163.own_ref, f32[2,2,2,16,128]{4,3,2,1,0:T(8,128)S(1)} %bitcast.27), custom_call_target="tpu_custom_call" | custom-call | flops 1000000 | bytes 1000000 | tf_op jit(solution)/shard_map/pallas_call | solution.py:438
  (10 shorter events, 0.0 us)
Async XLA Ops:
  0.6 27.6 %copy-start.1 = (s32[1,32,256]{2,1,0:T(8,128)S(1)}, s32[1,32,256]{2,1,0:T(8,128)}, u32[]{:S(2)}) copy-start(s32[1,32,256]{2,1,0:T(8,128)} %index_ref.5) | copy-start | bytes 98308
  0.6 27.6 %copy-start.2 = (s32[1,32,256]{2,1,0:T(8,128)S(1)}, s32[1,32,256]{2,1,0:T(8,128)}, u32[]{:S(2)}) copy-start(s32[1,32,256]{2,1,0:T(8,128)} %place_kind_ref.3) | copy-start | bytes 98308
  0.7 0.7 copy-start.5
  1.3 0.7 copy-start.8
  2.0 0.7 copy-start.9
  2.7 0.7 copy-start.10
  3.4 0.7 copy-start.11
  4.1 24.2 %copy-start.6 = (s32[1,256]{1,0:T(1,128)S(1)}, s32[1,256]{1,0:T(1,128)}, u32[]{:S(2)}) copy-start(s32[1,256]{1,0:T(1,128)} %kind_ref.5) | copy-start | bytes 3076
  4.1 24.2 %copy-start.7 = (s32[1,256]{1,0:T(1,128)S(1)}, s32[1,256]{1,0:T(1,128)}, u32[]{:S(2)}) copy-start(s32[1,256]{1,0:T(1,128)} %total_ref.3) | copy-start | bytes 3076
  13.1 8.9 %collective-permute-start = (f32[2,8,128]{2,1,0:T(8,128)S(1)}, f32[2,8,128]{2,1,0:T(8,128)S(1)}, u32[]{:S(2)}, u32[]{:S(2)}) collective-permute-start(f32[2,8,128]{2,1,0:T(8,128)S(1)} %slice.17.near_ref), channel_id=1, source_target_pairs={{31,0},{0,31},{1,2},{2,1},{3,4},{4,3},{5,6},{6,5},{7,8},{8,7},{9,1... | collective-permute-start | bytes 24584 | tf_op jit(solution)/shard_map/ppermute | solution.py:492
  15.8 0.8 copy-start
  16.5 0.7 copy-start.3
  17.2 0.9 %copy-start.12 = (bf16[256,256]{1,0:T(8,128)(2,1)S(1)}, bf16[256,256]{1,0:T(8,128)(2,1)}, u32[]{:S(2)}) copy-start(bf16[256,256]{1,0:T(8,128)(2,1)} %middle_ref.1) | copy-start | bytes 393220
  18.1 0.7 copy-start.13
  18.8 0.7 copy-start.14
  19.5 0.7 copy-start.15
  21.3 30.3 %copy-start.4 = (bf16[256,8]{0,1:T(8,128)(2,1)S(1)}, bf16[256,8]{0,1:T(8,128)(2,1)}, u32[]{:S(2)}) copy-start(bf16[256,8]{0,1:T(8,128)(2,1)} %param.27) | copy-start | bytes 12292

commit v3 on v2

--- a/solution.py
+++ b/solution.py
@@ -35,15 +35,6 @@
     return lax.dot_general(a, b, (((1,), (0,)), ((), ())), preferred_element_type=F32)
 
 
-def tile_of(flat_ref):
-    rows = [
-        flat_ref[:, (comp * 2 + chunk) * LANES : (comp * 2 + chunk + 1) * LANES]
-        for chunk in range(2)
-        for comp in range(3)
-    ]
-    return jnp.concatenate(rows, axis=0)
-
-
 def put_flat(flat_ref, tile):
     for chunk in range(2):
         for comp in range(3):
@@ -89,22 +80,34 @@
     return parts
 
 
-def start_kernel(x_ref, v_ref, kind_ref, border_ref, inertia_ref, out_ref):
-    x_tile = tile_of(x_ref)
-    border = border_ref[0]
-    border0 = jnp.concatenate([border[0:1], border[1:2]], axis=1)
-    border1 = jnp.concatenate([border[2:3], border[3:4]], axis=1)
-    kind = kind_ref[...]
+def bring(sources, targets, sems):
+    copies = [
+        pltpu.make_async_copy(source, target, sems.at[k])
+        for k, (source, target) in enumerate(zip(sources, targets))
+    ]
+    for copy in copies:
+        copy.start()
+    for copy in copies:
+        copy.wait()
+
+
+def start_kernel(given_ref, out_ref):
+    def tile(first):
+        rows = [first + comp * 2 + chunk for chunk in range(2) for comp in range(3)]
+        return jnp.concatenate([given_ref[row : row + 1] for row in rows], axis=0)
+
+    place = tile(0)
+    border = given_ref[14:16]
+    kind = given_ref[12:14]
     inverse = jnp.zeros(kind.shape, F32)
     for k in range(N_KIND):
-        inverse = jnp.where(kind == k, inertia_ref[k], inverse)
-    out_ref[0:8] = border_positions(x_tile, border0, border1)
-    out_ref[8:14] = x_tile
-    out_ref[14:15] = inverse[:, :LANES]
-    out_ref[15:16] = inverse[:, LANES:]
-    out_ref[16:22] = tile_of(v_ref)
-    out_ref[22:23] = border0.astype(F32)
-    out_ref[23:24] = border1.astype(F32)
+        inverse = jnp.where(kind == k, given_ref[16:17, k : k + 1], inverse)
+    index = border.astype(jnp.int32)
+    out_ref[0:8] = border_positions(place, index[0:1], index[1:2])
+    out_ref[8:14] = place
+    out_ref[14:16] = inverse
+    out_ref[16:22] = tile(6)
+    out_ref[22:24] = border
 
 
 def fed_columns():
@@ -129,15 +132,18 @@
 
 
 def weight_kernel(
-    index_ref, intake_ref, edge_out_ref, opening_ref, middle_ref, atom_out_ref,
+    index_ref, given_ref,
     up_ref, down_ref, line_ref, flat_ref, sum_ref, hot_ref, atom_ref, first_ref, second_ref, back_ref,
 ):
-    intake = intake_ref[...]
+    middle = given_ref[0:HIDDEN]
+    opening = given_ref[HIDDEN : HIDDEN + 8]
+    edge_w = given_ref[HIDDEN + 8 : HIDDEN + 9]
+    atom_w = given_ref[HIDDEN + 9 : HIDDEN + 10]
+    intake = given_ref[HIDDEN + 16 : HIDDEN + 44].astype(BF16)
     fed = fed_columns()
     for j in range(8):
         up = jnp.where(own_columns(j, 28), 0.5 * fed, 0.0).astype(BF16)
         up_ref[j * HIDDEN : (j + 1) * HIDDEN, :] = tn_dot(intake, up).astype(BF16)
-    edge_w = edge_out_ref[...]
     weighted = intake.astype(F32) * (0.5 * edge_w)
     down_ref[...] = two_parts(weighted[0:16])
     line = jnp.sum(weighted, axis=1, keepdims=True)
@@ -147,10 +153,10 @@
     line_ref[...] = two_parts(jnp.where(own_columns(slot, 8), line, 0.0))
     wide = jnp.transpose(jnp.broadcast_to(edge_w, (LANES, HIDDEN)))
     sum_ref[...] = jnp.concatenate([wide, wide], axis=1).astype(BF16)
-    atom_ref[...] = jnp.transpose(jnp.broadcast_to(0.5 * atom_out_ref[...], (LANES, HIDDEN)))
-    first_ref[...] = jnp.transpose((0.5 * opening_ref[...]).astype(F32)).astype(BF16)
-    second_ref[...] = 0.5 * middle_ref[...]
-    back_ref[...] = jnp.transpose(middle_ref[...].astype(F32)).astype(BF16)
+    atom_ref[...] = jnp.transpose(jnp.broadcast_to(0.5 * atom_w, (LANES, HIDDEN)))
+    first_ref[...] = jnp.transpose(0.5 * opening).astype(BF16)
+    second_ref[...] = (0.5 * middle).astype(BF16)
+    back_ref[...] = jnp.transpose(middle).astype(BF16)
     place = lax.broadcasted_iota(jnp.int32, (LANES, 2 * LANES), 0)
 
     def group(s, carry):
@@ -411,7 +417,7 @@
         next_ref[domain, 8:16] = speed
 
 
-def swap_kernel(where_ref, level_ref, own_ref, mate_ref, x_ref, v_ref):
+def swap_kernel(where_ref, level_ref, own_ref, mate_ref, x_out, v_out, x_ref, v_ref, sems):
     core, swaps, side, position = (where_ref[k] for k in range(4))
     mine = own_ref[core]
     theirs = mate_ref[side, position, core]
@@ -419,6 +425,7 @@
     scale = jnp.sqrt(level_ref[0] / chosen[6:7])
     put_flat(x_ref, chosen[0:6])
     put_flat(v_ref, chosen[8:14] * scale)
+    bring((x_ref, v_ref), (x_out, v_out), sems)
 
 
 def vmem():
@@ -433,8 +440,9 @@
     return jax.ShapeDtypeStruct(shape + (LANES,), F32)
 
 
-def call(kernel, scalars, arrays, out_shape, scratch=(), flops=10**6, limit=24 * 2**20):
-    out_specs = [vmem() for _ in out_shape] if isinstance(out_shape, list) else vmem()
+def call(kernel, scalars, arrays, out_shape, scratch=(), flops=10**6, outputs=None):
+    outputs = outputs or vmem
+    out_specs = [outputs() for _ in out_shape] if isinstance(out_shape, list) else outputs()
     return pl.pallas_call(
         kernel,
         out_shape=out_shape,
@@ -442,8 +450,16 @@
         out_specs=out_specs,
         scratch_shapes=list(scratch),
         cost_estimate=pl.CostEstimate(flops=flops, bytes_accessed=10**6, transcendentals=0),
-        compiler_params=pltpu.CompilerParams(vmem_limit_bytes=limit),
+        compiler_params=pltpu.CompilerParams(vmem_limit_bytes=24 * 2**20),
     )(*scalars, *arrays)
+
+
+def anywhere():
+    return pl.BlockSpec(memory_space=pltpu.HBM)
+
+
+def landing(arrays):
+    return [pltpu.VMEM(a.shape, a.dtype) for a in arrays] + [pltpu.SemaphoreType.DMA((len(arrays),))]
 
 
 def weight_shapes():
@@ -528,33 +544,20 @@
     position = jnp.where(side == 0, 1 - odd, odd)
     where_to = jnp.stack([core, (mate != rank).astype(jnp.int32), side, position]).astype(jnp.int32)
 
-    begin = pl.pallas_call(
-        start_kernel,
-        out_shape=tiles(24),
-        in_specs=[vmem()] * 4 + [smem()],
-        out_specs=vmem(),
-        compiler_params=pltpu.CompilerParams(vmem_limit_bytes=16 * 2**20),
-    )(
-        particle_coordinates.reshape(1, -1),
-        particle_motions.reshape(1, -1),
-        particle_kinds,
-        border_particle_numbers,
-        reciprocal_kind_inertia,
-    )
-    weights = call(
-        weight_kernel,
-        (),
-        (
-            adjacent_particles,
-            bond_intake_coefficients.T,
-            bond_output_coefficients[None],
-            particle_opening_coefficients.T,
-            particle_middle_coefficients,
-            particle_output_coefficients[None],
-        ),
-        weight_shapes(),
-        flops=10**9,
-    )
+    rows = [particle_coordinates, particle_motions, particle_kinds, border_particle_numbers]
+    rows = [value.reshape(-1, LANES).astype(F32) for value in rows]
+    rows += [jnp.pad(reciprocal_kind_inertia[None], ((0, 7), (0, LANES - N_KIND)))]
+    begin = call(start_kernel, (), (jnp.concatenate(rows, axis=0),), tiles(24))
+    rows = [
+        particle_middle_coefficients,
+        particle_opening_coefficients.T,
+        bond_output_coefficients[None],
+        particle_output_coefficients[None],
+        jnp.zeros((6, HIDDEN), F32),
+        bond_intake_coefficients.T,
+    ]
+    rows = jnp.concatenate([value.astype(F32) for value in rows], axis=0)
+    weights = call(weight_kernel, (), (adjacent_particles, rows), weight_shapes(), (), 10**9)
     both = on_chip(begin, domains)
     send, state = both[:, 0:8], both[:, 8:24]
     for step in range(STEPS):
@@ -588,7 +591,10 @@
     mates = on_chip(along_ladder(state, rungs, domains), domains)
     shape = particle_coordinates.shape
     out = jax.ShapeDtypeStruct((1, particle_coordinates.size), F32)
-    new_x, new_v = call(swap_kernel, (where_to, thermal_levels), (state, mates), [out, out])
+    scratch = landing((out, out))
+    new_x, new_v = call(
+        swap_kernel, (where_to, thermal_levels), (state, mates), [out, out], scratch, outputs=anywhere
+    )
     return new_x.reshape(shape), new_v.reshape(shape)
 
 

time: 78.3 us -> 77.2 us (0.986)
  local copies, waits for them, and re-layouts: 7.84 us -> 3.31 us
  other arithmetic: 0.08 us -> 4.26 us
    unnamed x32 -> x12, local copies, waits for them, and re-layouts: 7.83 us -> 0.78 us
    convert_element_type x0 -> x4, other arithmetic: none -> 2.78 us  [the longest x2 1.41 us: on_device(): rows = jnp.concatenate([value.astype(F32) for value in rows], axis=0)]
    concatenate x0 -> x2, local copies, waits for them, and re-layouts: none -> 1.76 us  [the longest x1 1.68 us: on_device(): rows = jnp.concatenate([value.astype(F32) for value in rows], axis=0)]
    unnamed x0 -> x2, other arithmetic: none -> 1.41 us
    pallas_call x6 -> x7, Pallas kernels: 14.4 us -> 14.4 us  [call(): pl.pallas_call(kernel, out_shape=out_shape, in_specs=[smem()] * len(scala...]
  transfers between devices with their start and end apart: 1 -> 1, of which waited for: 0 -> 0; matrix products, arithmetic and copies ran while one was open for 0% -> 4% of each run, Pallas kernels for 1% -> 1%
where the time goes in v3:
time: 77.2 us; the launch traced here: 76.7 us
  blocking collectives  50.7 us (66%)
  Pallas kernels  14.4 us (19%)
  other arithmetic  4.26 us (6%)
  local copies, waits for them, and re-layouts  3.31 us (4%)
  between operations  2.05 us (3%)
  starting transfers between devices  1.91 us (2%)
    all_gather x8, blocking collectives, on_chip(): return lax.all_gather(value, 'space', axis_index_groups=groups)  31.9 us
    pallas_call x7, Pallas kernels, call(): pl.pallas_call(kernel, out_shape=out_shape, in_specs=[smem()] * len(scala...  14.4 us
    all_gather x3, blocking collectives, across_chips(): return lax.all_gather(value, 'space', axis_index_groups=groups)  11.3 us
    all_gather x1, blocking collectives, along_ladder(): return lax.all_gather(value, ('replica', 'space'), axis_index_groups=groups)  7.48 us
    ppermute x1, starting transfers between devices, partner_across(): return lax.ppermute(value, 'space', pairs)  1.91 us
    concatenate x1, local copies, waits for them, and re-layouts, on_device(): rows = jnp.concatenate([value.astype(F32) for value in rows], axis=0)  1.68 us
  transfers between devices with their start and end apart: 1, of which 0 were waited for; matrix products, arithmetic and copies ran while one was open for 4% of the time, Pallas kernels for 1%

profile of v3, /device:TPU:1, one launch (start us, length us, event | category | flops | bytes accessed | tf_op | source)
XLA Modules:
  0.0 76.7 jit_solution(4376115647126726387)
XLA Ops:
  0.6 0.7 reduce
  1.3 0.7 reduce.1
  2.1 0.7 convert_element_type.29
  2.7 0.1 convert_element_type.30
  2.8 0.7 convert_element_type.27
  3.5 0.7 pad.4
  4.2 0.1 concatenate.6.given_ref
  4.2 0.1 shard_map.158
  4.4 8.4 %all-gather = f32[48,128]{1,0:T(8,128)S(1)} all-gather(f32[24,128]{1,0:T(8,128)S(1)} %shard_map.158), channel_id=2, replica_groups={{0,1},{2,3},{4,5},{6,7},{8,9},{10,11},{12,13},{14,15},{16,17},{18,19},{..., dimensions={0}, use_global_device_ids=true | all-gather | bytes 36864 | tf_op jit(solution)/shard_map/all_gather | solution.py:495
  12.7 1.9 %collective-permute-start = (f32[2,8,128]{2,1,0:T(8,128)S(1)}, f32[2,8,128]{2,1,0:T(8,128)S(1)}, u32[]{:S(2)}, u32[]{:S(2)}) collective-permute-start(f32[2,8,128]{2,1,0:T(8,128)S(1)} %slice.17.near_ref), channel_id=1, source_target_pairs={{31,0},{0,31},{1,2},{2,1},{3,4},{4,3},{5,6},{6,5},{7,8},{8,7},{9,1... | collective-permute-start | bytes 24584 | tf_op jit(solution)/shard_map/ppermute | solution.py:508
  15.3 0.7 convert_bitcast_fusion
  16.1 0.7 bitcast_convert_fusion
  16.7 0.1 pad_add_fusion.core_ref.where_ref
  16.8 0.0 copy-start.1
  16.8 0.0 copy-start.2
  16.8 0.0 copy-start.3
  16.8 0.0 copy-start.4
  16.8 0.0 copy-start.5
  16.9 1.7 %concatenate.7.given_ref = f32[300,256]{1,0:T(8,128)S(1)} concatenate(bf16[256,256]{1,0:T(8,128)(2,1)} %param.28, f32[8,256]{1,0:T(8,128)S(1)} %bitcast_convert_fusion, f32[1,256]{1,0:T(1,128)} %bitcast.47, f32[1,256]{1,0:T(1,128)} %bitcast.48, f32[6,256]{1,0:T(8,128)S(1)} %broadcast_in_dim.15, f32[28,256]{1,0:T(8,128)S(1)} %convert_bitcast_fusion), dimensions={0} | concatenate | bytes 483328 | tf_op jit(solution)/shard_map/concatenate | solution.py:559
  18.5 0.0 copy-start
  18.5 0.8 copy-done
  19.3 1.1 %shard_map.159 = (bf16[2048,128]{1,0:T(8,128)(2,1)S(1)}, bf16[32,256]{1,0:T(8,128)(2,1)S(1)}, bf16[16,128]{1,0:T(8,128)(2,1)S(1)}, f32[16,128]{1,0:T(8,128)S(1)}...) custom-call(s32[1,32,256]{2,1,0:T(8,128)S(1)} %copy-done, ...), custom_call_target="tpu_custom_call" | custom-call | flops 1000000000 | bytes 1000000 | tf_op jit(solution)/shard_map/pallas_call | solution.py:446
  21.0 0.0 collective-permute-done
  21.1 6.3 %all-gather.1 = f32[4,8,128]{2,1,0:T(8,128)S(1)} all-gather(f32[2,8,128]{2,1,0:T(8,128)S(1)} %collective-permute-done), channel_id=3, replica_groups={{0,1},{2,3},{4,5},{6,7},{8,9},{10,11},{12,13},{14,15},{16,17},{18,19},{..., dimensions={0}, use_global_device_ids=true | all-gather | bytes 24576 | tf_op jit(solution)/shard_map/all_gather | solution.py:495
  27.3 0.0 copy-done.1
  27.3 0.0 copy-done.2
  27.3 0.0 copy-done.3
  27.3 0.0 copy-done.4
  27.3 0.0 copy-done.5
  27.3 5.8 %shard_map.160 = f32[16,128]{1,0:T(8,128)S(1)} custom-call(s32[4]{0:T(128)S(1)} %pad_add_fusion.core_ref.where_ref, f32[2,16,128]{2,1,0:T(8,128)S(1)} %slice.16.state_ref, f32[2,8,128]{2,1,0:T(8,128)S(1)} %slice.17.near_ref, f32[2,2,8,128]{3,2,1,0:T(8,128)S(1)} %bitcast.37, s32[1,32,256]{2,1,0:T(8,128)S(1)} %copy-done.1, s32[1,32,256]{2,1,0:T(8,128)S(1)} %copy-done.2, ...), custom_call_target="tpu_custom_call" | custom-call | flops 1000000 | bytes 1000000 | tf_op jit(solution)/shard_map/pallas_call | solution.py:446
  33.2 1.8 %all-gather.2 = f32[32,128]{1,0:T(8,128)S(1)} all-gather(f32[16,128]{1,0:T(8,128)S(1)} %shard_map.160), channel_id=4, replica_groups={{0,1},{2,3},{4,5},{6,7},{8,9},{10,11},{12,13},{14,15},{16,17},{18,19},{..., dimensions={0}, use_global_device_ids=true | all-gather | bytes 24576 | tf_op jit(solution)/shard_map/all_gather | solution.py:495
  35.0 3.8 %all-gather.3 = f32[4,8,128]{2,1,0:T(8,128)S(1)} all-gather(f32[2,8,128]{2,1,0:T(8,128)S(1)} %slice.18), channel_id=5, replica_groups={{31,0},{1,2},{3,4},{5,6},{7,8},{9,10},{11,12},{13,14},{15,16},{17,18},{..., dimensions={0}, use_global_device_ids=true | all-gather | bytes 24576 | tf_op jit(solution)/shard_map/all_gather | solution.py:500
  38.8 3.9 %all-gather.4 = f32[4,2,8,128]{3,2,1,0:T(8,128)S(1)} all-gather(f32[2,2,8,128]{3,2,1,0:T(8,128)S(1)} %bitcast.43), channel_id=6, replica_groups={{0,1},{2,3},{4,5},{6,7},{8,9},{10,11},{12,13},{14,15},{16,17},{18,19},{..., dimensions={0}, use_global_device_ids=true | all-gather | bytes 49152 | tf_op jit(solution)/shard_map/all_gather | solution.py:495
  42.7 0.2 shard_map.161
  43.0 3.8 %all-gather.5 = f32[4,8,128]{2,1,0:T(8,128)S(1)} all-gather(f32[2,8,128]{2,1,0:T(8,128)S(1)} %get-tuple-element.27.near_ref), channel_id=7, replica_groups={{31,0},{1,2},{3,4},{5,6},{7,8},{9,10},{11,12},{13,14},{15,16},{17,18},{..., dimensions={0}, use_global_device_ids=true | all-gather | bytes 24576 | tf_op jit(solution)/shard_map/all_gather | solution.py:500
  46.7 3.9 %all-gather.6 = f32[4,2,8,128]{3,2,1,0:T(8,128)S(1)} all-gather(f32[2,2,8,128]{3,2,1,0:T(8,128)S(1)} %bitcast.45), channel_id=8, replica_groups={{0,1},{2,3},{4,5},{6,7},{8,9},{10,11},{12,13},{14,15},{16,17},{18,19},{..., dimensions={0}, use_global_device_ids=true | all-gather | bytes 49152 | tf_op jit(solution)/shard_map/all_gather | solution.py:495
  50.7 5.8 %shard_map.162 = f32[16,128]{1,0:T(8,128)S(1)} custom-call(s32[4]{0:T(128)S(1)} %pad_add_fusion.core_ref.where_ref, f32[2,16,128]{2,1,0:T(8,128)S(1)} %get-tuple-element.26.state_ref, f32[2,8,128]{2,1,0:T(8,128)S(1)} %get-tuple-element.27.near_ref, f32[2,2,2,8,128]{4,3,2,1,0:T(8,128)S(1)} %bitcast.30, s32[1,32,256]{2,1,0:T(8,128)S(1)} %copy-done.1, ...), custom_call_target="tpu_custom_call" | custom-call | flops 1000000 | bytes 1000000 | tf_op jit(solution)/shard_map/pallas_call | solution.py:446
  56.5 1.8 %all-gather.7 = f32[32,128]{1,0:T(8,128)S(1)} all-gather(f32[16,128]{1,0:T(8,128)S(1)} %shard_map.162), channel_id=9, replica_groups={{0,1},{2,3},{4,5},{6,7},{8,9},{10,11},{12,13},{14,15},{16,17},{18,19},{..., dimensions={0}, use_global_device_ids=true | all-gather | bytes 24576 | tf_op jit(solution)/shard_map/all_gather | solution.py:495
  58.3 3.8 %all-gather.8 = f32[4,8,128]{2,1,0:T(8,128)S(1)} all-gather(f32[2,8,128]{2,1,0:T(8,128)S(1)} %slice.19), channel_id=10, replica_groups={{31,0},{1,2},{3,4},{5,6},{7,8},{9,10},{11,12},{13,14},{15,16},{17,18},{..., dimensions={0}, use_global_device_ids=true | all-gather | bytes 24576 | tf_op jit(solution)/shard_map/all_gather | solution.py:500
  62.1 3.9 %all-gather.9 = f32[4,2,8,128]{3,2,1,0:T(8,128)S(1)} all-gather(f32[2,2,8,128]{3,2,1,0:T(8,128)S(1)} %bitcast.44), channel_id=11, replica_groups={{0,1},{2,3},{4,5},{6,7},{8,9},{10,11},{12,13},{14,15},{16,17},{18,19},{..., dimensions={0}, use_global_device_ids=true | all-gather | bytes 49152 | tf_op jit(solution)/shard_map/all_gather | solution.py:495
  66.0 0.2 shard_map.163.own_ref
  66.2 7.5 %all-gather.10 = f32[4,16,128]{2,1,0:T(8,128)S(1)} all-gather(f32[2,16,128]{2,1,0:T(8,128)S(1)} %shard_map.163.own_ref), channel_id=12, replica_groups={{0,32},{64,96},{128,160},{192,224},{256,288},{320,352},{384,416},{448,4..., dimensions={0}, use_global_device_ids=true | all-gather | bytes 49152 | tf_op jit(solution)/shard_map/all_gather | solution.py:518
  73.7 1.8 %all-gather.11 = f32[4,2,16,128]{3,2,1,0:T(8,128)S(1)} all-gather(f32[2,2,16,128]{3,2,1,0:T(8,128)S(1)} %bitcast.40), channel_id=13, replica_groups={{0,1},{2,3},{4,5},{6,7},{8,9},{10,11},{12,13},{14,15},{16,17},{18,19},{..., dimensions={0}, use_global_device_ids=true | all-gather | bytes 98304 | tf_op jit(solution)/shard_map/all_gather | solution.py:495
  75.5 1.2 %shard_map.164 = (f32[1,768]{1,0:T(1,128)}, f32[1,768]{1,0:T(1,128)}) custom-call(s32[4]{0:T(128)S(1)} %pad_add_fusion.core_ref.where_ref, f32[1]{0:T(128)S(6)} %copy.23.level_ref, f32[2,16,128]{2,1,0:T(8,128)S(1)} %shard_map.163.own_ref, f32[2,2,2,16,128]{4,3,2,1,0:T(8,128)S(1)} %bitcast.29), custom_call_target="tpu_custom_call" | custom-call | flops 1000000 | bytes 1000000 | tf_op jit(solution)/shard_map/pallas_call | solution.py:446
  (7 shorter events, 0.0 us)
Async XLA Ops:
  12.7 8.3 %collective-permute-start = (f32[2,8,128]{2,1,0:T(8,128)S(1)}, f32[2,8,128]{2,1,0:T(8,128)S(1)}, u32[]{:S(2)}, u32[]{:S(2)}) collective-permute-start(f32[2,8,128]{2,1,0:T(8,128)S(1)} %slice.17.near_ref), channel_id=1, source_target_pairs={{31,0},{0,31},{1,2},{2,1},{3,4},{4,3},{5,6},{6,5},{7,8},{8,7},{9,1... | collective-permute-start | bytes 24584 | tf_op jit(solution)/shard_map/ppermute | solution.py:508
  16.8 10.5 %copy-start.1 = (s32[1,32,256]{2,1,0:T(8,128)S(1)}, s32[1,32,256]{2,1,0:T(8,128)}, u32[]{:S(2)}) copy-start(s32[1,32,256]{2,1,0:T(8,128)} %index_ref.5) | copy-start | bytes 98308
  16.8 10.5 %copy-start.2 = (s32[1,32,256]{2,1,0:T(8,128)S(1)}, s32[1,32,256]{2,1,0:T(8,128)}, u32[]{:S(2)}) copy-start(s32[1,32,256]{2,1,0:T(8,128)} %place_kind_ref.3) | copy-start | bytes 98308
  16.8 10.5 %copy-start.3 = (bf16[256,8]{0,1:T(8,128)(2,1)S(1)}, bf16[256,8]{0,1:T(8,128)(2,1)}, u32[]{:S(2)}) copy-start(bf16[256,8]{0,1:T(8,128)(2,1)} %param.27) | copy-start | bytes 12292
  16.8 10.5 %copy-start.4 = (s32[1,256]{1,0:T(1,128)S(1)}, s32[1,256]{1,0:T(1,128)}, u32[]{:S(2)}) copy-start(s32[1,256]{1,0:T(1,128)} %kind_ref.3) | copy-start | bytes 3076
  16.8 10.5 %copy-start.5 = (s32[1,256]{1,0:T(1,128)S(1)}, s32[1,256]{1,0:T(1,128)}, u32[]{:S(2)}) copy-start(s32[1,256]{1,0:T(1,128)} %total_ref.3) | copy-start | bytes 3076
  18.5 0.8 copy-start

commit v4 on v3

--- a/solution.py
+++ b/solution.py
@@ -16,7 +16,7 @@
 SLOTS = 32
 GROUPS = SLOTS // 8
 HIDDEN = 256
-AHEAD = 3
+AHEAD = 4
 SHARP = (N_BASIS / CUT_SQ) ** 2
 CENTRES = [CUT_SQ * c / (N_BASIS - 1) for c in range(N_BASIS)]
 F32 = jnp.float32
@@ -33,6 +33,15 @@
 
 def nn_dot(a, b):
     return lax.dot_general(a, b, (((1,), (0,)), ((), ())), preferred_element_type=F32)
+
+
+def tile_of(flat_ref):
+    rows = [
+        flat_ref[:, (comp * 2 + chunk) * LANES : (comp * 2 + chunk + 1) * LANES]
+        for chunk in range(2)
+        for comp in range(3)
+    ]
+    return jnp.concatenate(rows, axis=0)
 
 
 def put_flat(flat_ref, tile):
@@ -91,25 +100,6 @@
         copy.wait()
 
 
-def start_kernel(given_ref, out_ref):
-    def tile(first):
-        rows = [first + comp * 2 + chunk for chunk in range(2) for comp in range(3)]
-        return jnp.concatenate([given_ref[row : row + 1] for row in rows], axis=0)
-
-    place = tile(0)
-    border = given_ref[14:16]
-    kind = given_ref[12:14]
-    inverse = jnp.zeros(kind.shape, F32)
-    for k in range(N_KIND):
-        inverse = jnp.where(kind == k, given_ref[16:17, k : k + 1], inverse)
-    index = border.astype(jnp.int32)
-    out_ref[0:8] = border_positions(place, index[0:1], index[1:2])
-    out_ref[8:14] = place
-    out_ref[14:16] = inverse
-    out_ref[16:22] = tile(6)
-    out_ref[22:24] = border
-
-
 def fed_columns():
     feature = lax.broadcasted_iota(jnp.int32, (28, LANES), 0)
     col = lax.broadcasted_iota(jnp.int32, (28, LANES), 1)
@@ -131,19 +121,56 @@
     return jnp.concatenate([high, low], axis=0).astype(BF16)
 
 
-def weight_kernel(
-    index_ref, given_ref,
-    up_ref, down_ref, line_ref, flat_ref, sum_ref, hot_ref, atom_ref, first_ref, second_ref, back_ref,
-):
-    middle = given_ref[0:HIDDEN]
-    opening = given_ref[HIDDEN : HIDDEN + 8]
-    edge_w = given_ref[HIDDEN + 8 : HIDDEN + 9]
-    atom_w = given_ref[HIDDEN + 9 : HIDDEN + 10]
-    intake = given_ref[HIDDEN + 16 : HIDDEN + 44].astype(BF16)
+def begin_kernel(*refs):
+    inputs, refs = refs[:13], refs[13:]
+    (out_ref, up_ref, down_ref, line_ref, flat_ref, sum_ref, hot_ref, atom_ref, first_ref,
+     second_ref, back_ref, index_ref, place_ref, total_ref, kind_ref, opening_ref), refs = (
+        refs[:16], refs[16:]
+    )
+    x_ref, v_ref, border_ref, inertia_ref, intake_ref, edge_out_ref, middle_ref, atom_out_ref = (
+        refs[:8]
+    )
+    landed = (
+        x_ref, v_ref, kind_ref, border_ref, inertia_ref, index_ref, place_ref, total_ref,
+        intake_ref, edge_out_ref, opening_ref, middle_ref, atom_out_ref,
+    )
+    bring(inputs, landed, refs[8])
+
+    x_tile = tile_of(x_ref)
+    border = border_ref[0]
+    border0 = jnp.concatenate([border[0:1], border[1:2]], axis=1)
+    border1 = jnp.concatenate([border[2:3], border[3:4]], axis=1)
+    kind = kind_ref[...]
+    inverse = jnp.zeros(kind.shape, F32)
+    for k in range(N_KIND):
+        inverse = jnp.where(kind == k, inertia_ref[k], inverse)
+    out_ref[0:8] = border_positions(x_tile, border0, border1)
+    out_ref[8:14] = x_tile
+    out_ref[14:15] = inverse[:, :LANES]
+    out_ref[15:16] = inverse[:, LANES:]
+    out_ref[16:22] = tile_of(v_ref)
+    out_ref[22:23] = border0.astype(F32)
+    out_ref[23:24] = border1.astype(F32)
+
+    place = lax.broadcasted_iota(jnp.int32, (LANES, 2 * LANES), 0).astype(F32).astype(BF16)
+    one, none = jnp.asarray(1.0, BF16), jnp.asarray(0.0, BF16)
+
+    def group(s, carry):
+        for j in range(8):
+            lane = (index_ref[0, pl.ds(s * 8 + j, 1), :] & (LANES - 1)).astype(F32)
+            lane = jnp.broadcast_to(lane, (16, 2 * LANES)).astype(BF16)
+            lane = jnp.concatenate([lane] * (LANES // 16), axis=0)
+            cols = pl.ds(pl.multiple_of((s * 8 + j) * 2 * LANES, 2 * LANES), 2 * LANES)
+            hot_ref[:, cols] = jnp.where(place == lane, one, none)
+        return carry
+
+    lax.fori_loop(0, GROUPS, group, 0)
+    intake = intake_ref[...]
     fed = fed_columns()
     for j in range(8):
         up = jnp.where(own_columns(j, 28), 0.5 * fed, 0.0).astype(BF16)
         up_ref[j * HIDDEN : (j + 1) * HIDDEN, :] = tn_dot(intake, up).astype(BF16)
+    edge_w = edge_out_ref[...]
     weighted = intake.astype(F32) * (0.5 * edge_w)
     down_ref[...] = two_parts(weighted[0:16])
     line = jnp.sum(weighted, axis=1, keepdims=True)
@@ -153,36 +180,21 @@
     line_ref[...] = two_parts(jnp.where(own_columns(slot, 8), line, 0.0))
     wide = jnp.transpose(jnp.broadcast_to(edge_w, (LANES, HIDDEN)))
     sum_ref[...] = jnp.concatenate([wide, wide], axis=1).astype(BF16)
-    atom_ref[...] = jnp.transpose(jnp.broadcast_to(0.5 * atom_w, (LANES, HIDDEN)))
-    first_ref[...] = jnp.transpose(0.5 * opening).astype(BF16)
-    second_ref[...] = (0.5 * middle).astype(BF16)
-    back_ref[...] = jnp.transpose(middle).astype(BF16)
-    place = lax.broadcasted_iota(jnp.int32, (LANES, 2 * LANES), 0)
-
-    def group(s, carry):
-        for j in range(8):
-            lane = index_ref[0, pl.ds(s * 8 + j, 1), :] & (LANES - 1)
-            hot_ref[:, pl.ds(pl.multiple_of((s * 8 + j) * 256, 256), 256)] = (place == lane).astype(F32).astype(BF16)
-        return carry
-
-    lax.fori_loop(0, GROUPS, group, 0)
+    atom_ref[...] = jnp.transpose(jnp.broadcast_to(0.5 * atom_out_ref[...], (LANES, HIDDEN)))
+    first_ref[...] = jnp.transpose((0.5 * opening_ref[...]).astype(F32)).astype(BF16)
+    second_ref[...] = 0.5 * middle_ref[...]
+    back_ref[...] = jnp.transpose(middle_ref[...].astype(F32)).astype(BF16)
 
 
 def far_tiles(far_ref):
-    if len(far_ref.shape) == 5:
-        return far_ref[0, 0, 0], far_ref[0, 0, 1], far_ref[1, 1, 0], far_ref[1, 1, 1]
-    return far_ref[0, 0], far_ref[0, 1], far_ref[1, 0], far_ref[1, 1]
+    return far_ref[0, 0, 0], far_ref[0, 0, 1], far_ref[1, 1, 0], far_ref[1, 1, 1]
 
 
 def force_kernel(
-    core_ref,
+    where_ref,
     state_ref,
     near_ref,
     far_ref,
-    index_ref,
-    place_kind_ref,
-    total_ref,
-    kind_ref,
     up_ref,
     down_ref,
     line_ref,
@@ -193,6 +205,10 @@
     first_ref,
     second_ref,
     back_ref,
+    index_ref,
+    place_kind_ref,
+    total_ref,
+    kind_ref,
     opening_ref,
     out_ref,
     feat_ref,
@@ -204,9 +220,8 @@
     scat0_ref,
     scat1_ref,
 ):
-    core = core_ref[0]
-    first_core = core == 0
-    own = state_ref[core]
+    first_core = where_ref[0:1] == 0
+    own = jnp.where(first_core, state_ref[0], state_ref[1])
     minus2, minus1, plus2, plus3 = far_tiles(far_ref)
     near0, near1 = near_ref[0], near_ref[1]
 
@@ -297,14 +312,15 @@
         energy = line[0:8] + line[8:16]
         folded = []
 
-        def forward(j):
-            return nn_dot(up_ref[j * HIDDEN : (j + 1) * HIDDEN, :], feat).astype(BF16)
-
-        ahead = [forward(j) for j in range(AHEAD)]
+        def forward(k):
+            many = nn_dot(up_ref[k * AHEAD * HIDDEN : (k + 1) * AHEAD * HIDDEN, :], feat)
+            return [many[i * HIDDEN : (i + 1) * HIDDEN].astype(BF16) for i in range(AHEAD)]
+
+        ahead = forward(0)
         for j in range(8):
             half = ahead.pop(0)
-            if j + AHEAD < 8:
-                ahead.append(forward(j + AHEAD))
+            if j % AHEAD == 0 and j + AHEAD < 8:
+                ahead += forward(j // AHEAD + 1)
             th = jnp.tanh(half)
             rest = sum_ref[...] * (half * th)
             rest = rest[: HIDDEN // 2] + rest[HIDDEN // 2 :]
@@ -323,7 +339,7 @@
         energy_ref[s] = energy
         return g_env
 
-    g_env = lax.fori_loop(0, GROUPS, group, g_env)
+    g_env = lax.fori_loop(1, GROUPS, group, group(0, g_env))
 
     def backward(s, sums):
         sums = list(sums)
@@ -410,19 +426,25 @@
         next_ref[domain, 14:16] = state_ref[domain, 14:16]
 
 
-def last_kernel(level_ref, state_ref, near_ref, far_ref, next_ref):
+def last_kernel(where_ref, state_ref, near_ref, far_ref, next_ref):
     for domain, (place, speed, _, _) in enumerate(moved(state_ref, near_ref, far_ref)):
         next_ref[domain, 0:6] = place[0:6]
-        next_ref[domain, 6:8] = jnp.full((2, LANES), level_ref[0], F32)
+        next_ref[domain, 6:8] = jnp.broadcast_to(where_ref[4:5], (2, LANES))
         next_ref[domain, 8:16] = speed
 
 
-def swap_kernel(where_ref, level_ref, own_ref, mate_ref, x_out, v_out, x_ref, v_ref, sems):
-    core, swaps, side, position = (where_ref[k] for k in range(4))
-    mine = own_ref[core]
-    theirs = mate_ref[side, position, core]
-    chosen = jnp.where(swaps == 1, theirs, mine)
-    scale = jnp.sqrt(level_ref[0] / chosen[6:7])
+def swap_kernel(where_ref, own_ref, mate_ref, x_out, v_out, x_ref, v_ref, sems):
+    core, swaps, side, position = (where_ref[k : k + 1] == 0 for k in range(4))
+
+    def of_core(pair):
+        return jnp.where(core, pair[0], pair[1])
+
+    def of_side(s):
+        return of_core(jnp.where(position, mate_ref[s, 0], mate_ref[s, 1]))
+
+    mine = of_core(own_ref)
+    chosen = jnp.where(swaps, mine, jnp.where(side, of_side(0), of_side(1)))
+    scale = jnp.sqrt(mine[6:7] / chosen[6:7])
     put_flat(x_ref, chosen[0:6])
     put_flat(v_ref, chosen[8:14] * scale)
     bring((x_ref, v_ref), (x_out, v_out), sems)
@@ -440,17 +462,18 @@
     return jax.ShapeDtypeStruct(shape + (LANES,), F32)
 
 
-def call(kernel, scalars, arrays, out_shape, scratch=(), flops=10**6, outputs=None):
+def call(kernel, scalars, arrays, out_shape, scratch=(), flops=10**6, inputs=None, outputs=None,
+         limit=24 * 2**20):
     outputs = outputs or vmem
     out_specs = [outputs() for _ in out_shape] if isinstance(out_shape, list) else outputs()
     return pl.pallas_call(
         kernel,
         out_shape=out_shape,
-        in_specs=[smem()] * len(scalars) + [vmem()] * len(arrays),
+        in_specs=[smem()] * len(scalars) + [(inputs or vmem)()] * len(arrays),
         out_specs=out_specs,
         scratch_shapes=list(scratch),
         cost_estimate=pl.CostEstimate(flops=flops, bytes_accessed=10**6, transcendentals=0),
-        compiler_params=pltpu.CompilerParams(vmem_limit_bytes=24 * 2**20),
+        compiler_params=pltpu.CompilerParams(vmem_limit_bytes=limit),
     )(*scalars, *arrays)
 
 
@@ -477,6 +500,15 @@
     ]
 
 
+def begin_shapes(arrays):
+    through = [jax.ShapeDtypeStruct(arrays[k].shape, arrays[k].dtype) for k in (5, 6, 7, 2, 10)]
+    space = landing([arrays[k] for k in (0, 1, 3, 4, 8, 9, 11, 12)])
+    space[3] = pltpu.SMEM(arrays[4].shape, F32)
+    space[-1] = pltpu.SemaphoreType.DMA((len(arrays),))
+    made = [tiles(24)] + weight_shapes() + through
+    return made, space
+
+
 def force_scratch():
     return [
         pltpu.VMEM((GROUPS, 128, 2 * LANES), BF16),
@@ -500,21 +532,15 @@
     return lax.all_gather(value, "space", axis_index_groups=groups)
 
 
-def partner_across(value, domains):
-    pairs = []
-    for i in range(domains // 2):
-        odd, even = (2 * i - 1) % domains, 2 * i
-        pairs += [(odd, even), (even, odd)]
-    return lax.ppermute(value, "space", pairs)
-
-
 def along_ladder(value, rungs, domains):
     groups = []
     for domain in range(domains):
         shift = domain % 2
-        for low in range(shift, rungs, 2):
-            high = (low + 1) % rungs
-            groups.append([low * domains + domain, high * domains + domain])
+        for low in range(shift, rungs - shift, 2):
+            groups.append([low * domains + domain, (low + 1) * domains + domain])
+        if shift and domain // 2 % 2 == 0:
+            for end in (0, rungs - 1):
+                groups.append([end * domains + domain, end * domains + domain + 2])
     return lax.all_gather(value, ("replica", "space"), axis_index_groups=groups)
 
 
@@ -542,42 +568,41 @@
     odd = rank % 2
     side = jnp.where((mate > rank) == (odd == 0), 0, 1)
     position = jnp.where(side == 0, 1 - odd, odd)
-    where_to = jnp.stack([core, (mate != rank).astype(jnp.int32), side, position]).astype(jnp.int32)
-
-    rows = [particle_coordinates, particle_motions, particle_kinds, border_particle_numbers]
-    rows = [value.reshape(-1, LANES).astype(F32) for value in rows]
-    rows += [jnp.pad(reciprocal_kind_inertia[None], ((0, 7), (0, LANES - N_KIND)))]
-    begin = call(start_kernel, (), (jnp.concatenate(rows, axis=0),), tiles(24))
-    rows = [
+    where_to = [value.astype(F32) for value in (core, mate != rank, side, position)]
+    where_to = jnp.stack(where_to + [thermal_levels[0]])
+    where_to = jnp.broadcast_to(where_to[:, None], (5, LANES))
+
+    arrays = (
+        particle_coordinates.reshape(1, -1),
+        particle_motions.reshape(1, -1),
+        particle_kinds,
+        border_particle_numbers,
+        reciprocal_kind_inertia,
+        adjacent_particles,
+        adjacent_place_kinds,
+        filled_totals,
+        bond_intake_coefficients.T,
+        bond_output_coefficients[None],
+        particle_opening_coefficients.T,
         particle_middle_coefficients,
-        particle_opening_coefficients.T,
-        bond_output_coefficients[None],
         particle_output_coefficients[None],
-        jnp.zeros((6, HIDDEN), F32),
-        bond_intake_coefficients.T,
-    ]
-    rows = jnp.concatenate([value.astype(F32) for value in rows], axis=0)
-    weights = call(weight_kernel, (), (adjacent_particles, rows), weight_shapes(), (), 10**9)
+    )
+    arrays = tuple(pltpu.with_memory_space_constraint(a, pltpu.HBM) for a in arrays)
+    made, space = begin_shapes(arrays)
+    begin, *fixed = call(begin_kernel, (), arrays, made, space, inputs=anywhere)
     both = on_chip(begin, domains)
     send, state = both[:, 0:8], both[:, 8:24]
     for step in range(STEPS):
-        if step == 0:
-            far = on_chip(partner_across(send, domains), domains)
-        else:
-            far = on_chip(across_chips(send, domains), domains)
+        far = on_chip(across_chips(send, domains), domains)
         partial = call(
             force_kernel,
-            (where_to,),
+            (),
             (
+                where_to,
                 state,
                 send,
                 far,
-                adjacent_particles,
-                adjacent_place_kinds,
-                filled_totals,
-                particle_kinds,
-                *weights,
-                particle_opening_coefficients.T,
+                *fixed,
             ),
             tiles(16),
             force_scratch(),
@@ -587,13 +612,13 @@
         if step < STEPS - 1:
             send, state = call(step_kernel, (), (state, near, far), [tiles(2, 8), tiles(2, 16)])
         else:
-            state = call(last_kernel, (thermal_levels,), (state, near, far), tiles(2, 16))
+            state = call(last_kernel, (), (where_to, state, near, far), tiles(2, 16))
     mates = on_chip(along_ladder(state, rungs, domains), domains)
     shape = particle_coordinates.shape
     out = jax.ShapeDtypeStruct((1, particle_coordinates.size), F32)
     scratch = landing((out, out))
     new_x, new_v = call(
-        swap_kernel, (where_to, thermal_levels), (state, mates), [out, out], scratch, outputs=anywhere
+        swap_kernel, (), (where_to, state, mates), [out, out], scratch, outputs=anywhere
     )
     return new_x.reshape(shape), new_v.reshape(shape)
 

time: 77.2 us -> 65.3 us (0.85)
  the two profiles are of different devices: /device:TPU:1 before, /device:TPU:7 now
where the time goes in v4:
time: 65.3 us; the launch traced here: 65.1 us
  blocking collectives  50.7 us (78%)
  Pallas kernels  12.2 us (19%)
  between operations  1.97 us (3%)
    all_gather x8, blocking collectives, on_chip(): return lax.all_gather(value, 'space', axis_index_groups=groups)  29.3 us
    all_gather x4, blocking collectives, across_chips(): return lax.all_gather(value, 'space', axis_index_groups=groups)  15.1 us
    pallas_call x6, Pallas kernels, call(): pl.pallas_call(kernel, out_shape=out_shape, in_specs=[smem()] * len(scala...  12.2 us
    all_gather x1, blocking collectives, along_ladder(): return lax.all_gather(value, ('replica', 'space'), axis_index_groups=groups)  6.27 us

profile of v4, /device:TPU:7, one launch (start us, length us, event | category | flops | bytes accessed | tf_op | source)
XLA Modules:
  0.0 65.1 jit_solution(4285601913023583633)
XLA Ops:
  2.0 0.1 stack.23
  2.0 0.1 broadcast_in_dim.12.where_ref
  2.1 2.0 %shard_map.158 = (f32[24,128]{1,0:T(8,128)S(1)}, bf16[2048,128]{1,0:T(8,128)(2,1)S(1)}, bf16[32,256]{1,0:T(8,128)(2,1)S(1)}, bf16[16,128]{1,0:T(8,128)(2,1)S(1)}...) custom-call(f32[1,768]{1,0:T(1,128)} %bitcast.46, ...), custom_call_target="tpu_custom_call" | custom-call | flops 1000000 | bytes 1000000 | tf_op jit(solution)/shard_map/pallas_call | solution.py:469
  4.1 2.2 %all-gather = f32[48,128]{1,0:T(8,128)S(1)} all-gather(f32[24,128]{1,0:T(8,128)S(1)} %get-tuple-element.22), channel_id=2, replica_groups={{0,1},{2,3},{4,5},{6,7},{8,9},{10,11},{12,13},{14,15},{16,17},{18,19},{..., dimensions={0}, use_global_device_ids=true | all-gather | bytes 36864 | tf_op jit(solution)/shard_map/all_gather | solution.py:527
  6.3 3.8 %all-gather.1 = f32[4,8,128]{2,1,0:T(8,128)S(1)} all-gather(f32[2,8,128]{2,1,0:T(8,128)S(1)} %slice.17.near_ref), channel_id=3, replica_groups={{31,0},{1,2},{3,4},{5,6},{7,8},{9,10},{11,12},{13,14},{15,16},{17,18},{..., dimensions={0}, use_global_device_ids=true | all-gather | bytes 24576 | tf_op jit(solution)/shard_map/all_gather | solution.py:532
  10.1 9.9 %all-gather.2 = f32[4,2,8,128]{3,2,1,0:T(8,128)S(1)} all-gather(f32[2,2,8,128]{3,2,1,0:T(8,128)S(1)} %bitcast.42), channel_id=4, replica_groups={{0,1},{2,3},{4,5},{6,7},{8,9},{10,11},{12,13},{14,15},{16,17},{18,19},{..., dimensions={0}, use_global_device_ids=true | all-gather | bytes 49152 | tf_op jit(solution)/shard_map/all_gather | solution.py:527
  20.0 4.6 %shard_map.159 = f32[16,128]{1,0:T(8,128)S(1)} custom-call(f32[5,128]{1,0:T(8,128)S(1)} %broadcast_in_dim.12.where_ref, f32[2,16,128]{2,1,0:T(8,128)S(1)} %slice.16.state_ref, f32[2,8,128]{2,1,0:T(8,128)S(1)} %slice.17.near_ref, f32[2,2,2,8,128]{4,3,2,1,0:T(8,128)S(1)} %bitcast.30, bf16[2048,128]{1,0:T(8,128)(2,1)S(1)} %get-tuple-element.23.up_ref, ...), custom_call_target="tpu_custom_call" | custom-call | flops 1000000 | bytes 1000000 | tf_op jit(solution)/shard_map/pallas_call | solution.py:469
  24.6 1.8 %all-gather.3 = f32[32,128]{1,0:T(8,128)S(1)} all-gather(f32[16,128]{1,0:T(8,128)S(1)} %shard_map.159), channel_id=5, replica_groups={{0,1},{2,3},{4,5},{6,7},{8,9},{10,11},{12,13},{14,15},{16,17},{18,19},{..., dimensions={0}, use_global_device_ids=true | all-gather | bytes 24576 | tf_op jit(solution)/shard_map/all_gather | solution.py:527
  26.4 3.8 %all-gather.4 = f32[4,8,128]{2,1,0:T(8,128)S(1)} all-gather(f32[2,8,128]{2,1,0:T(8,128)S(1)} %slice.18), channel_id=6, replica_groups={{31,0},{1,2},{3,4},{5,6},{7,8},{9,10},{11,12},{13,14},{15,16},{17,18},{..., dimensions={0}, use_global_device_ids=true | all-gather | bytes 24576 | tf_op jit(solution)/shard_map/all_gather | solution.py:532
  30.2 3.9 %all-gather.5 = f32[4,2,8,128]{3,2,1,0:T(8,128)S(1)} all-gather(f32[2,2,8,128]{3,2,1,0:T(8,128)S(1)} %bitcast.40), channel_id=7, replica_groups={{0,1},{2,3},{4,5},{6,7},{8,9},{10,11},{12,13},{14,15},{16,17},{18,19},{..., dimensions={0}, use_global_device_ids=true | all-gather | bytes 49152 | tf_op jit(solution)/shard_map/all_gather | solution.py:527
  34.1 0.2 shard_map.160
  34.3 3.8 %all-gather.6 = f32[4,8,128]{2,1,0:T(8,128)S(1)} all-gather(f32[2,8,128]{2,1,0:T(8,128)S(1)} %get-tuple-element.39.near_ref), channel_id=8, replica_groups={{31,0},{1,2},{3,4},{5,6},{7,8},{9,10},{11,12},{13,14},{15,16},{17,18},{..., dimensions={0}, use_global_device_ids=true | all-gather | bytes 24576 | tf_op jit(solution)/shard_map/all_gather | solution.py:532
  38.1 3.9 %all-gather.7 = f32[4,2,8,128]{3,2,1,0:T(8,128)S(1)} all-gather(f32[2,2,8,128]{3,2,1,0:T(8,128)S(1)} %bitcast.43), channel_id=9, replica_groups={{0,1},{2,3},{4,5},{6,7},{8,9},{10,11},{12,13},{14,15},{16,17},{18,19},{..., dimensions={0}, use_global_device_ids=true | all-gather | bytes 49152 | tf_op jit(solution)/shard_map/all_gather | solution.py:527
  42.1 4.6 %shard_map.161 = f32[16,128]{1,0:T(8,128)S(1)} custom-call(f32[5,128]{1,0:T(8,128)S(1)} %broadcast_in_dim.12.where_ref, f32[2,16,128]{2,1,0:T(8,128)S(1)} %get-tuple-element.38.state_ref, f32[2,8,128]{2,1,0:T(8,128)S(1)} %get-tuple-element.39.near_ref, f32[2,2,2,8,128]{4,3,2,1,0:T(8,128)S(1)} %bitcast.29, bf16[2048,128]{1,0:T(8,128)(2,1)S(1)} %get-tuple-element.23.up_ref, ...), custom_call_target="tpu_custom_call" | custom-call | flops 1000000 | bytes 1000000 | tf_op jit(solution)/shard_map/pallas_call | solution.py:469
  46.6 1.8 %all-gather.8 = f32[32,128]{1,0:T(8,128)S(1)} all-gather(f32[16,128]{1,0:T(8,128)S(1)} %shard_map.161), channel_id=10, replica_groups={{0,1},{2,3},{4,5},{6,7},{8,9},{10,11},{12,13},{14,15},{16,17},{18,19},{..., dimensions={0}, use_global_device_ids=true | all-gather | bytes 24576 | tf_op jit(solution)/shard_map/all_gather | solution.py:527
  48.5 3.8 %all-gather.9 = f32[4,8,128]{2,1,0:T(8,128)S(1)} all-gather(f32[2,8,128]{2,1,0:T(8,128)S(1)} %slice.19), channel_id=11, replica_groups={{31,0},{1,2},{3,4},{5,6},{7,8},{9,10},{11,12},{13,14},{15,16},{17,18},{..., dimensions={0}, use_global_device_ids=true | all-gather | bytes 24576 | tf_op jit(solution)/shard_map/all_gather | solution.py:532
  52.2 3.9 %all-gather.10 = f32[4,2,8,128]{3,2,1,0:T(8,128)S(1)} all-gather(f32[2,2,8,128]{3,2,1,0:T(8,128)S(1)} %bitcast.41), channel_id=12, replica_groups={{0,1},{2,3},{4,5},{6,7},{8,9},{10,11},{12,13},{14,15},{16,17},{18,19},{..., dimensions={0}, use_global_device_ids=true | all-gather | bytes 49152 | tf_op jit(solution)/shard_map/all_gather | solution.py:527
  56.2 0.2 shard_map.162.own_ref
  56.3 6.3 %all-gather.11 = f32[4,16,128]{2,1,0:T(8,128)S(1)} all-gather(f32[2,16,128]{2,1,0:T(8,128)S(1)} %shard_map.162.own_ref), channel_id=13, replica_groups={{0,32},{64,96},{128,160},{192,224},{256,288},{320,352},{384,416},{448,4..., dimensions={0}, use_global_device_ids=true | all-gather | bytes 49152 | tf_op jit(solution)/shard_map/all_gather | solution.py:544
  62.6 1.8 %all-gather.12 = f32[4,2,16,128]{3,2,1,0:T(8,128)S(1)} all-gather(f32[2,2,16,128]{3,2,1,0:T(8,128)S(1)} %bitcast.37), channel_id=14, replica_groups={{0,1},{2,3},{4,5},{6,7},{8,9},{10,11},{12,13},{14,15},{16,17},{18,19},{..., dimensions={0}, use_global_device_ids=true | all-gather | bytes 98304 | tf_op jit(solution)/shard_map/all_gather | solution.py:527
  64.4 0.6 shard_map.163
  (4 shorter events, 0.0 us)

commit v5 on v4

--- a/solution.py
+++ b/solution.py
@@ -113,7 +113,7 @@
 
 def own_columns(slot, rows):
     col = lax.broadcasted_iota(jnp.int32, (rows, LANES), 1)
-    return (col // 8 == 8) | (col // 8 == 9) | (col % 8 == slot)
+    return ((col // 8 == 8) | (col // 8 == 9) | (col % 8 == slot)).astype(F32)
 
 
 def two_parts(value):
@@ -168,7 +168,7 @@
     intake = intake_ref[...]
     fed = fed_columns()
     for j in range(8):
-        up = jnp.where(own_columns(j, 28), 0.5 * fed, 0.0).astype(BF16)
+        up = (0.5 * fed * own_columns(j, 1)).astype(BF16)
         up_ref[j * HIDDEN : (j + 1) * HIDDEN, :] = tn_dot(intake, up).astype(BF16)
     edge_w = edge_out_ref[...]
     weighted = intake.astype(F32) * (0.5 * edge_w)
@@ -177,9 +177,8 @@
     flat_ref[...] = jnp.broadcast_to(line[0:16], (16, LANES))
     line = jnp.sum(fed * line, axis=0, keepdims=True)
     slot = lax.broadcasted_iota(jnp.int32, (8, LANES), 0)
-    line_ref[...] = two_parts(jnp.where(own_columns(slot, 8), line, 0.0))
-    wide = jnp.transpose(jnp.broadcast_to(edge_w, (LANES, HIDDEN)))
-    sum_ref[...] = jnp.concatenate([wide, wide], axis=1).astype(BF16)
+    line_ref[...] = two_parts(own_columns(slot, 8) * line)
+    sum_ref[...] = jnp.transpose(jnp.broadcast_to(edge_w, (LANES, HIDDEN)))
     atom_ref[...] = jnp.transpose(jnp.broadcast_to(0.5 * atom_out_ref[...], (LANES, HIDDEN)))
     first_ref[...] = jnp.transpose((0.5 * opening_ref[...]).astype(F32)).astype(BF16)
     second_ref[...] = 0.5 * middle_ref[...]
@@ -217,9 +216,9 @@
     energy_ref,
     gin0_ref,
     gin1_ref,
-    scat0_ref,
-    scat1_ref,
+    *scratch,
 ):
+    scat, ahead_ref = (scratch[:GROUPS], scratch[GROUPS : 2 * GROUPS]), scratch[2 * GROUPS]
     first_core = where_ref[0:1] == 0
     own = jnp.where(first_core, state_ref[0], state_ref[1])
     minus2, minus1, plus2, plus3 = far_tiles(far_ref)
@@ -306,23 +305,29 @@
     quarter = lax.broadcasted_iota(jnp.int32, (16, HIDDEN), 1) // (HIDDEN // 4)
     members = [(slot == quarter + 4 * k).astype(F32).astype(BF16) for k in range(2)]
 
+    def first_forward(s):
+        ahead_ref[...] = nn_dot(up_ref[: AHEAD * HIDDEN, :], feat_ref[s])
+
     def group(s, g_env):
         feat = feat_ref[s]
         line = nn_dot(line_ref[...], feat)
         energy = line[0:8] + line[8:16]
         folded = []
+        edge_w = sum_ref[...].astype(BF16)
+        edge_w = jnp.concatenate([edge_w, edge_w], axis=1)
 
         def forward(k):
             many = nn_dot(up_ref[k * AHEAD * HIDDEN : (k + 1) * AHEAD * HIDDEN, :], feat)
             return [many[i * HIDDEN : (i + 1) * HIDDEN].astype(BF16) for i in range(AHEAD)]
 
-        ahead = forward(0)
+        ahead = [ahead_ref[i * HIDDEN : (i + 1) * HIDDEN].astype(BF16) for i in range(AHEAD)]
+        ahead += forward(1)
         for j in range(8):
             half = ahead.pop(0)
-            if j % AHEAD == 0 and j + AHEAD < 8:
-                ahead += forward(j // AHEAD + 1)
+            if j == AHEAD:
+                first_forward(jnp.minimum(s + 1, GROUPS - 1))
             th = jnp.tanh(half)
-            rest = sum_ref[...] * (half * th)
+            rest = edge_w * (half * th)
             rest = rest[: HIDDEN // 2] + rest[HIDDEN // 2 :]
             folded.append(rest[: HIDDEN // 4] + rest[HIDDEN // 4 :])
             slope = th + half * (jnp.asarray(1.0, BF16) - th * th)
@@ -339,6 +344,7 @@
         energy_ref[s] = energy
         return g_env
 
+    first_forward(0)
     g_env = lax.fori_loop(1, GROUPS, group, group(0, g_env))
 
     def backward(s, sums):
@@ -359,25 +365,28 @@
                 g_gap = moment if g_gap is None else g_gap + moment
             g_dist = (-4.0 * SHARP) * (cutoff * g_gap) + 2.0 * (g_cut * slope)
             chunk = index_ref[0, slots, cols] // LANES
-            scat = (scat0_ref, scat1_ref)[h]
+            target = scat[h][s]
             for comp in range(3):
                 g_vec = g_dist * geo_ref[comp, s, :, cols]
                 sums[h * 3 + comp] = sums[h * 3 + comp] + g_vec
                 for part, value in enumerate(split_parts(g_vec, 2)):
                     for which in range(4):
-                        row = s * 8 * 24 + part * 12 + which * 3 + comp
-                        scat[pl.ds(row, 8, stride=24), :] = jnp.where(chunk == which, value, 0.0)
+                        row = part * 12 + which * 3 + comp
+                        target[pl.ds(row, 8, stride=24), :] = jnp.where(chunk == which, value, 0.0)
         return tuple(sums)
 
-    sums = (nothing,) * 6
+    def scatter(s):
+        lhs = []
+        for j in range(8):
+            rows = slice(j * 24, j * 24 + 24)
+            lhs.append(jnp.concatenate([half[s][rows, :] for half in scat], axis=1).astype(BF16))
+        return nt_dot(jnp.concatenate(lhs, axis=1), hot_ref[:, s * 16 * LANES : (s + 1) * 16 * LANES])
+
+    sums, total = (nothing,) * 6, None
     for s in range(GROUPS):
         sums = backward(s, sums)
-
-    lhs = []
-    for slot in range(SLOTS):
-        rows = slice(slot * 24, slot * 24 + 24)
-        lhs.append(jnp.concatenate([scat0_ref[rows, :], scat1_ref[rows, :]], axis=1).astype(BF16))
-    total = nt_dot(jnp.concatenate(lhs, axis=1), hot_ref[...])
+        part = scatter(s)
+        total = part if total is None else total + part
     total = total[0:12] + total[12:24]
     centre = jnp.concatenate([jnp.sum(value, axis=0, keepdims=True) for value in sums], axis=0)
     pad = jnp.zeros((2, LANES), F32)
@@ -491,7 +500,7 @@
         jax.ShapeDtypeStruct((32, HIDDEN), BF16),
         jax.ShapeDtypeStruct((16, LANES), BF16),
         tiles(16),
-        jax.ShapeDtypeStruct((HIDDEN, 2 * LANES), BF16),
+        tiles(HIDDEN),
         jax.ShapeDtypeStruct((LANES, SLOTS * 2 * LANES), BF16),
         tiles(HIDDEN),
         jax.ShapeDtypeStruct((HIDDEN, N_BASIS), BF16),
@@ -517,9 +526,7 @@
         pltpu.VMEM((GROUPS, 8, 2 * LANES), F32),
         pltpu.VMEM((GROUPS * 64, LANES), F32),
         pltpu.VMEM((GROUPS * 64, LANES), F32),
-        pltpu.VMEM((SLOTS * 24, LANES), F32),
-        pltpu.VMEM((SLOTS * 24, LANES), F32),
-    ]
+    ] + [pltpu.VMEM((8 * 24, LANES), F32)] * (2 * GROUPS) + [pltpu.VMEM((AHEAD * HIDDEN, 2 * LANES), F32)]
 
 
 def on_chip(value, domains):

time: 65.3 us -> 64.8 us (level)
  no operation moved by 1% of the time
where the time goes in v5:
time: 64.8 us; the launch traced here: 64.5 us
  blocking collectives  50.7 us (78%)
  Pallas kernels  11.6 us (18%)
  between operations  1.98 us (3%)
    all_gather x8, blocking collectives, on_chip(): return lax.all_gather(value, 'space', axis_index_groups=groups)  29.3 us
    all_gather x4, blocking collectives, across_chips(): return lax.all_gather(value, 'space', axis_index_groups=groups)  15.1 us
    pallas_call x6, Pallas kernels, call(): pl.pallas_call(kernel, out_shape=out_shape, in_specs=[smem()] * len(scala...  11.6 us
    all_gather x1, blocking collectives, along_ladder(): return lax.all_gather(value, ('replica', 'space'), axis_index_groups=groups)  6.27 us

profile of v5, /device:TPU:7, one launch (start us, length us, event | category | flops | bytes accessed | tf_op | source)
XLA Modules:
  0.0 64.5 jit_solution(4740533249788261390)
XLA Ops:
  2.0 0.1 stack.23
  2.0 0.1 broadcast_in_dim.12.where_ref
  2.1 2.0 %shard_map.158 = (f32[24,128]{1,0:T(8,128)S(1)}, bf16[2048,128]{1,0:T(8,128)(2,1)S(1)}, bf16[32,256]{1,0:T(8,128)(2,1)S(1)}, bf16[16,128]{1,0:T(8,128)(2,1)S(1)}...) custom-call(f32[1,768]{1,0:T(1,128)} %bitcast.46, ...), custom_call_target="tpu_custom_call" | custom-call | flops 1000000 | bytes 1000000 | tf_op jit(solution)/shard_map/pallas_call | solution.py:478
  4.1 2.2 %all-gather = f32[48,128]{1,0:T(8,128)S(1)} all-gather(f32[24,128]{1,0:T(8,128)S(1)} %get-tuple-element.22), channel_id=2, replica_groups={{0,1},{2,3},{4,5},{6,7},{8,9},{10,11},{12,13},{14,15},{16,17},{18,19},{..., dimensions={0}, use_global_device_ids=true | all-gather | bytes 36864 | tf_op jit(solution)/shard_map/all_gather | solution.py:534
  6.3 3.8 %all-gather.1 = f32[4,8,128]{2,1,0:T(8,128)S(1)} all-gather(f32[2,8,128]{2,1,0:T(8,128)S(1)} %slice.17.near_ref), channel_id=3, replica_groups={{31,0},{1,2},{3,4},{5,6},{7,8},{9,10},{11,12},{13,14},{15,16},{17,18},{..., dimensions={0}, use_global_device_ids=true | all-gather | bytes 24576 | tf_op jit(solution)/shard_map/all_gather | solution.py:539
  10.1 9.9 %all-gather.2 = f32[4,2,8,128]{3,2,1,0:T(8,128)S(1)} all-gather(f32[2,2,8,128]{3,2,1,0:T(8,128)S(1)} %bitcast.42), channel_id=4, replica_groups={{0,1},{2,3},{4,5},{6,7},{8,9},{10,11},{12,13},{14,15},{16,17},{18,19},{..., dimensions={0}, use_global_device_ids=true | all-gather | bytes 49152 | tf_op jit(solution)/shard_map/all_gather | solution.py:534
  20.0 4.3 %shard_map.159 = f32[16,128]{1,0:T(8,128)S(1)} custom-call(f32[5,128]{1,0:T(8,128)S(1)} %broadcast_in_dim.12.where_ref, f32[2,16,128]{2,1,0:T(8,128)S(1)} %slice.16.state_ref, f32[2,8,128]{2,1,0:T(8,128)S(1)} %slice.17.near_ref, f32[2,2,2,8,128]{4,3,2,1,0:T(8,128)S(1)} %bitcast.30, bf16[2048,128]{1,0:T(8,128)(2,1)S(1)} %get-tuple-element.23.up_ref, ...), custom_call_target="tpu_custom_call" | custom-call | flops 1000000 | bytes 1000000 | tf_op jit(solution)/shard_map/pallas_call | solution.py:478
  24.3 1.8 %all-gather.3 = f32[32,128]{1,0:T(8,128)S(1)} all-gather(f32[16,128]{1,0:T(8,128)S(1)} %shard_map.159), channel_id=5, replica_groups={{0,1},{2,3},{4,5},{6,7},{8,9},{10,11},{12,13},{14,15},{16,17},{18,19},{..., dimensions={0}, use_global_device_ids=true | all-gather | bytes 24576 | tf_op jit(solution)/shard_map/all_gather | solution.py:534
  26.1 3.8 %all-gather.4 = f32[4,8,128]{2,1,0:T(8,128)S(1)} all-gather(f32[2,8,128]{2,1,0:T(8,128)S(1)} %slice.18), channel_id=6, replica_groups={{31,0},{1,2},{3,4},{5,6},{7,8},{9,10},{11,12},{13,14},{15,16},{17,18},{..., dimensions={0}, use_global_device_ids=true | all-gather | bytes 24576 | tf_op jit(solution)/shard_map/all_gather | solution.py:539
  29.9 3.9 %all-gather.5 = f32[4,2,8,128]{3,2,1,0:T(8,128)S(1)} all-gather(f32[2,2,8,128]{3,2,1,0:T(8,128)S(1)} %bitcast.40), channel_id=7, replica_groups={{0,1},{2,3},{4,5},{6,7},{8,9},{10,11},{12,13},{14,15},{16,17},{18,19},{..., dimensions={0}, use_global_device_ids=true | all-gather | bytes 49152 | tf_op jit(solution)/shard_map/all_gather | solution.py:534
  33.8 0.2 shard_map.160
  34.1 3.8 %all-gather.6 = f32[4,8,128]{2,1,0:T(8,128)S(1)} all-gather(f32[2,8,128]{2,1,0:T(8,128)S(1)} %get-tuple-element.39.near_ref), channel_id=8, replica_groups={{31,0},{1,2},{3,4},{5,6},{7,8},{9,10},{11,12},{13,14},{15,16},{17,18},{..., dimensions={0}, use_global_device_ids=true | all-gather | bytes 24576 | tf_op jit(solution)/shard_map/all_gather | solution.py:539
  37.8 3.9 %all-gather.7 = f32[4,2,8,128]{3,2,1,0:T(8,128)S(1)} all-gather(f32[2,2,8,128]{3,2,1,0:T(8,128)S(1)} %bitcast.43), channel_id=9, replica_groups={{0,1},{2,3},{4,5},{6,7},{8,9},{10,11},{12,13},{14,15},{16,17},{18,19},{..., dimensions={0}, use_global_device_ids=true | all-gather | bytes 49152 | tf_op jit(solution)/shard_map/all_gather | solution.py:534
  41.8 4.3 %shard_map.161 = f32[16,128]{1,0:T(8,128)S(1)} custom-call(f32[5,128]{1,0:T(8,128)S(1)} %broadcast_in_dim.12.where_ref, f32[2,16,128]{2,1,0:T(8,128)S(1)} %get-tuple-element.38.state_ref, f32[2,8,128]{2,1,0:T(8,128)S(1)} %get-tuple-element.39.near_ref, f32[2,2,2,8,128]{4,3,2,1,0:T(8,128)S(1)} %bitcast.29, bf16[2048,128]{1,0:T(8,128)(2,1)S(1)} %get-tuple-element.23.up_ref, ...), custom_call_target="tpu_custom_call" | custom-call | flops 1000000 | bytes 1000000 | tf_op jit(solution)/shard_map/pallas_call | solution.py:478
  46.1 1.8 %all-gather.8 = f32[32,128]{1,0:T(8,128)S(1)} all-gather(f32[16,128]{1,0:T(8,128)S(1)} %shard_map.161), channel_id=10, replica_groups={{0,1},{2,3},{4,5},{6,7},{8,9},{10,11},{12,13},{14,15},{16,17},{18,19},{..., dimensions={0}, use_global_device_ids=true | all-gather | bytes 24576 | tf_op jit(solution)/shard_map/all_gather | solution.py:534
  47.9 3.8 %all-gather.9 = f32[4,8,128]{2,1,0:T(8,128)S(1)} all-gather(f32[2,8,128]{2,1,0:T(8,128)S(1)} %slice.19), channel_id=11, replica_groups={{31,0},{1,2},{3,4},{5,6},{7,8},{9,10},{11,12},{13,14},{15,16},{17,18},{..., dimensions={0}, use_global_device_ids=true | all-gather | bytes 24576 | tf_op jit(solution)/shard_map/all_gather | solution.py:539
  51.7 3.9 %all-gather.10 = f32[4,2,8,128]{3,2,1,0:T(8,128)S(1)} all-gather(f32[2,2,8,128]{3,2,1,0:T(8,128)S(1)} %bitcast.41), channel_id=12, replica_groups={{0,1},{2,3},{4,5},{6,7},{8,9},{10,11},{12,13},{14,15},{16,17},{18,19},{..., dimensions={0}, use_global_device_ids=true | all-gather | bytes 49152 | tf_op jit(solution)/shard_map/all_gather | solution.py:534
  55.6 0.2 shard_map.162.own_ref
  55.8 6.3 %all-gather.11 = f32[4,16,128]{2,1,0:T(8,128)S(1)} all-gather(f32[2,16,128]{2,1,0:T(8,128)S(1)} %shard_map.162.own_ref), channel_id=13, replica_groups={{0,32},{64,96},{128,160},{192,224},{256,288},{320,352},{384,416},{448,4..., dimensions={0}, use_global_device_ids=true | all-gather | bytes 49152 | tf_op jit(solution)/shard_map/all_gather | solution.py:551
  62.0 1.8 %all-gather.12 = f32[4,2,16,128]{3,2,1,0:T(8,128)S(1)} all-gather(f32[2,2,16,128]{3,2,1,0:T(8,128)S(1)} %bitcast.37), channel_id=14, replica_groups={{0,1},{2,3},{4,5},{6,7},{8,9},{10,11},{12,13},{14,15},{16,17},{18,19},{..., dimensions={0}, use_global_device_ids=true | all-gather | bytes 98304 | tf_op jit(solution)/shard_map/all_gather | solution.py:534
  63.9 0.6 shard_map.163
  (4 shorter events, 0.0 us)

commit v6 on v5

--- a/solution.py
+++ b/solution.py
@@ -121,21 +121,9 @@
     return jnp.concatenate([high, low], axis=0).astype(BF16)
 
 
-def begin_kernel(*refs):
-    inputs, refs = refs[:13], refs[13:]
-    (out_ref, up_ref, down_ref, line_ref, flat_ref, sum_ref, hot_ref, atom_ref, first_ref,
-     second_ref, back_ref, index_ref, place_ref, total_ref, kind_ref, opening_ref), refs = (
-        refs[:16], refs[16:]
-    )
-    x_ref, v_ref, border_ref, inertia_ref, intake_ref, edge_out_ref, middle_ref, atom_out_ref = (
-        refs[:8]
-    )
-    landed = (
-        x_ref, v_ref, kind_ref, border_ref, inertia_ref, index_ref, place_ref, total_ref,
-        intake_ref, edge_out_ref, opening_ref, middle_ref, atom_out_ref,
-    )
-    bring(inputs, landed, refs[8])
-
+def start_kernel(x_in, v_in, kind_in, border_in, inertia_in, out_ref, *scratch):
+    x_ref, v_ref, kind_ref, border_ref, inertia_ref, sems = scratch
+    bring((x_in, v_in, kind_in, border_in, inertia_in), scratch[:-1], sems)
     x_tile = tile_of(x_ref)
     border = border_ref[0]
     border0 = jnp.concatenate([border[0:1], border[1:2]], axis=1)
@@ -152,6 +140,19 @@
     out_ref[22:23] = border0.astype(F32)
     out_ref[23:24] = border1.astype(F32)
 
+
+def weight_kernel(*refs):
+    inputs, refs = refs[:9], refs[9:]
+    (up_ref, down_ref, line_ref, flat_ref, sum_ref, hot_ref, atom_ref, first_ref,
+     second_ref, back_ref, index_ref, place_ref, total_ref, kind_ref, opening_ref), refs = (
+        refs[:15], refs[15:]
+    )
+    intake_ref, edge_out_ref, middle_ref, atom_out_ref, sems = refs
+    landed = (
+        index_ref, place_ref, total_ref, kind_ref, opening_ref, intake_ref, edge_out_ref,
+        middle_ref, atom_out_ref,
+    )
+    bring(inputs, landed, sems)
     place = lax.broadcasted_iota(jnp.int32, (LANES, 2 * LANES), 0).astype(F32).astype(BF16)
     one, none = jnp.asarray(1.0, BF16), jnp.asarray(0.0, BF16)
 
@@ -186,6 +187,8 @@
 
 
 def far_tiles(far_ref):
+    if len(far_ref.shape) == 4:
+        return far_ref[0, 0], far_ref[0, 1], far_ref[1, 0], far_ref[1, 1]
     return far_ref[0, 0, 0], far_ref[0, 0, 1], far_ref[1, 1, 0], far_ref[1, 1, 1]
 
 
@@ -490,6 +493,10 @@
     return pl.BlockSpec(memory_space=pltpu.HBM)
 
 
+def pinned(*arrays):
+    return tuple(pltpu.with_memory_space_constraint(a, pltpu.HBM) for a in arrays)
+
+
 def landing(arrays):
     return [pltpu.VMEM(a.shape, a.dtype) for a in arrays] + [pltpu.SemaphoreType.DMA((len(arrays),))]
 
@@ -509,13 +516,11 @@
     ]
 
 
-def begin_shapes(arrays):
-    through = [jax.ShapeDtypeStruct(arrays[k].shape, arrays[k].dtype) for k in (5, 6, 7, 2, 10)]
-    space = landing([arrays[k] for k in (0, 1, 3, 4, 8, 9, 11, 12)])
-    space[3] = pltpu.SMEM(arrays[4].shape, F32)
+def weight_parts(arrays):
+    through = [jax.ShapeDtypeStruct(a.shape, a.dtype) for a in arrays[:5]]
+    space = landing(arrays[5:])
     space[-1] = pltpu.SemaphoreType.DMA((len(arrays),))
-    made = [tiles(24)] + weight_shapes() + through
-    return made, space
+    return weight_shapes() + through, space
 
 
 def force_scratch():
@@ -537,6 +542,14 @@
 def across_chips(value, domains):
     groups = [[(2 * i - 1) % domains, 2 * i] for i in range(domains // 2)]
     return lax.all_gather(value, "space", axis_index_groups=groups)
+
+
+def partner_across(value, domains):
+    pairs = []
+    for i in range(domains // 2):
+        odd, even = (2 * i - 1) % domains, 2 * i
+        pairs += [(odd, even), (even, odd)]
+    return lax.ppermute(value, "space", pairs)
 
 
 def along_ladder(value, rungs, domains):
@@ -579,28 +592,34 @@
     where_to = jnp.stack(where_to + [thermal_levels[0]])
     where_to = jnp.broadcast_to(where_to[:, None], (5, LANES))
 
-    arrays = (
+    arrays = pinned(
         particle_coordinates.reshape(1, -1),
         particle_motions.reshape(1, -1),
         particle_kinds,
         border_particle_numbers,
         reciprocal_kind_inertia,
+    )
+    space = landing(arrays)
+    space[4] = pltpu.SMEM(reciprocal_kind_inertia.shape, F32)
+    begin = call(start_kernel, (), arrays, tiles(24), space, inputs=anywhere)
+    arrays = pinned(
         adjacent_particles,
         adjacent_place_kinds,
         filled_totals,
+        particle_kinds,
+        particle_opening_coefficients.T,
         bond_intake_coefficients.T,
         bond_output_coefficients[None],
-        particle_opening_coefficients.T,
         particle_middle_coefficients,
         particle_output_coefficients[None],
     )
-    arrays = tuple(pltpu.with_memory_space_constraint(a, pltpu.HBM) for a in arrays)
-    made, space = begin_shapes(arrays)
-    begin, *fixed = call(begin_kernel, (), arrays, made, space, inputs=anywhere)
+    made, space = weight_parts(arrays)
+    fixed = call(weight_kernel, (), arrays, made, space, 10**9, inputs=anywhere)
     both = on_chip(begin, domains)
     send, state = both[:, 0:8], both[:, 8:24]
     for step in range(STEPS):
-        far = on_chip(across_chips(send, domains), domains)
+        across = partner_across if step == 0 else across_chips
+        far = on_chip(across(send, domains), domains)
         partial = call(
             force_kernel,
             (),

time: 64.8 us -> 65.4 us (level)
  blocking collectives: 50.7 us -> 47.1 us
  starting transfers between devices: 0 us -> 3.41 us
  Pallas kernels: 11.6 us -> 12.3 us
    all_gather x4 -> x3, blocking collectives: 15.1 us -> 11.3 us  [across_chips(): return lax.all_gather(value, 'space', axis_index_groups=groups)]
    ppermute x0 -> x1, starting transfers between devices: none -> 3.41 us  [partner_across(): return lax.ppermute(value, 'space', pairs)]
    pallas_call x6 -> x7, Pallas kernels: 11.6 us -> 12.3 us  [call(): pl.pallas_call(kernel, out_shape=out_shape, in_specs=[smem()] * len(scala...]
  transfers between devices with their start and end apart: 0 -> 1, of which waited for: 0 -> 0; matrix products, arithmetic and copies ran while one was open for 0% -> 0% of each run, Pallas kernels for 0% -> 3%
where the time goes in v6:
time: 65.4 us; the launch traced here: 65.1 us
  blocking collectives  47.1 us (72%)
  Pallas kernels  12.3 us (19%)
  starting transfers between devices  3.41 us (5%)
  between operations  2.02 us (3%)
    all_gather x8, blocking collectives, on_chip(): return lax.all_gather(value, 'space', axis_index_groups=groups)  29.5 us
    pallas_call x7, Pallas kernels, call(): pl.pallas_call(kernel, out_shape=out_shape, in_specs=[smem()] * len(scala...  12.3 us
    all_gather x3, blocking collectives, across_chips(): return lax.all_gather(value, 'space', axis_index_groups=groups)  11.3 us
    all_gather x1, blocking collectives, along_ladder(): return lax.all_gather(value, ('replica', 'space'), axis_index_groups=groups)  6.27 us
    ppermute x1, starting transfers between devices, partner_across(): return lax.ppermute(value, 'space', pairs)  3.41 us
  transfers between devices with their start and end apart: 1, of which 0 were waited for; matrix products, arithmetic and copies ran while one was open for 0% of the time, Pallas kernels for 3%

profile of v6, /device:TPU:7, one launch (start us, length us, event | category | flops | bytes accessed | tf_op | source)
XLA Modules:
  0.0 65.1 jit_solution(9038429449643279443)
XLA Ops:
  0.6 1.0 %shard_map.158 = f32[24,128]{1,0:T(8,128)S(1)} custom-call(f32[1,768]{1,0:T(1,128)} %bitcast.42, f32[1,768]{1,0:T(1,128)} %bitcast.43, s32[1,256]{1,0:T(1,128)} %refs_3_.1, s32[1,4,64]{2,1,0:T(4,128)} %border_in.1, f32[6]{0:T(128)} %inertia_in.1), custom_call_target="tpu_custom_call" | custom-call | flops 1000000 | bytes 1000000 | tf_op jit(solution)/shard_map/pallas_call | solution.py:481
  1.6 2.2 %all-gather = f32[48,128]{1,0:T(8,128)S(1)} all-gather(f32[24,128]{1,0:T(8,128)S(1)} %shard_map.158), channel_id=2, replica_groups={{0,1},{2,3},{4,5},{6,7},{8,9},{10,11},{12,13},{14,15},{16,17},{18,19},{..., dimensions={0}, use_global_device_ids=true | all-gather | bytes 36864 | tf_op jit(solution)/shard_map/all_gather | solution.py:539
  3.8 3.4 %collective-permute-start = (f32[2,8,128]{2,1,0:T(8,128)S(1)}, f32[2,8,128]{2,1,0:T(8,128)S(1)}, u32[]{:S(2)}, u32[]{:S(2)}) collective-permute-start(f32[2,8,128]{2,1,0:T(8,128)S(1)} %slice.17.near_ref), channel_id=1, source_target_pairs={{31,0},{0,31},{1,2},{2,1},{3,4},{4,3},{5,6},{6,5},{7,8},{8,7},{9,1... | collective-permute-start | bytes 24584 | tf_op jit(solution)/shard_map/ppermute | solution.py:552
  7.2 1.8 %shard_map.159 = (bf16[2048,128]{1,0:T(8,128)(2,1)S(1)}, bf16[32,256]{1,0:T(8,128)(2,1)S(1)}, bf16[16,128]{1,0:T(8,128)(2,1)S(1)}, f32[16,128]{1,0:T(8,128)S(1)}...) custom-call(s32[1,32,256]{2,1,0:T(8,128)} %refs_0_.1, ...), custom_call_target="tpu_custom_call" | custom-call | flops 1000000000 | bytes 1000000 | tf_op jit(solution)/shard_map/pallas_call | solution.py:481
  10.4 0.1 stack.23
  10.5 0.0 collective-permute-done
  10.5 10.1 %all-gather.1 = f32[4,8,128]{2,1,0:T(8,128)S(1)} all-gather(f32[2,8,128]{2,1,0:T(8,128)S(1)} %collective-permute-done), channel_id=3, replica_groups={{0,1},{2,3},{4,5},{6,7},{8,9},{10,11},{12,13},{14,15},{16,17},{18,19},{..., dimensions={0}, use_global_device_ids=true | all-gather | bytes 24576 | tf_op jit(solution)/shard_map/all_gather | solution.py:539
  20.6 0.1 broadcast_in_dim.12.where_ref
  20.7 4.2 %shard_map.160 = f32[16,128]{1,0:T(8,128)S(1)} custom-call(f32[5,128]{1,0:T(8,128)S(1)} %broadcast_in_dim.12.where_ref, f32[2,16,128]{2,1,0:T(8,128)S(1)} %slice.16.state_ref, f32[2,8,128]{2,1,0:T(8,128)S(1)} %slice.17.near_ref, f32[2,2,8,128]{3,2,1,0:T(8,128)S(1)} %bitcast.35, bf16[2048,128]{1,0:T(8,128)(2,1)S(1)} %get-tuple-element.21.up_ref, ...), custom_call_target="tpu_custom_call" | custom-call | flops 1000000 | bytes 1000000 | tf_op jit(solution)/shard_map/pallas_call | solution.py:481
  24.9 1.8 %all-gather.2 = f32[32,128]{1,0:T(8,128)S(1)} all-gather(f32[16,128]{1,0:T(8,128)S(1)} %shard_map.160), channel_id=4, replica_groups={{0,1},{2,3},{4,5},{6,7},{8,9},{10,11},{12,13},{14,15},{16,17},{18,19},{..., dimensions={0}, use_global_device_ids=true | all-gather | bytes 24576 | tf_op jit(solution)/shard_map/all_gather | solution.py:539
  26.8 3.8 %all-gather.3 = f32[4,8,128]{2,1,0:T(8,128)S(1)} all-gather(f32[2,8,128]{2,1,0:T(8,128)S(1)} %slice.18), channel_id=5, replica_groups={{31,0},{1,2},{3,4},{5,6},{7,8},{9,10},{11,12},{13,14},{15,16},{17,18},{..., dimensions={0}, use_global_device_ids=true | all-gather | bytes 24576 | tf_op jit(solution)/shard_map/all_gather | solution.py:544
  30.5 3.9 %all-gather.4 = f32[4,2,8,128]{3,2,1,0:T(8,128)S(1)} all-gather(f32[2,2,8,128]{3,2,1,0:T(8,128)S(1)} %bitcast.39), channel_id=6, replica_groups={{0,1},{2,3},{4,5},{6,7},{8,9},{10,11},{12,13},{14,15},{16,17},{18,19},{..., dimensions={0}, use_global_device_ids=true | all-gather | bytes 49152 | tf_op jit(solution)/shard_map/all_gather | solution.py:539
  34.5 0.2 shard_map.161
  34.7 3.8 %all-gather.5 = f32[4,8,128]{2,1,0:T(8,128)S(1)} all-gather(f32[2,8,128]{2,1,0:T(8,128)S(1)} %get-tuple-element.37.near_ref), channel_id=7, replica_groups={{31,0},{1,2},{3,4},{5,6},{7,8},{9,10},{11,12},{13,14},{15,16},{17,18},{..., dimensions={0}, use_global_device_ids=true | all-gather | bytes 24576 | tf_op jit(solution)/shard_map/all_gather | solution.py:544
  38.5 3.9 %all-gather.6 = f32[4,2,8,128]{3,2,1,0:T(8,128)S(1)} all-gather(f32[2,2,8,128]{3,2,1,0:T(8,128)S(1)} %bitcast.41), channel_id=8, replica_groups={{0,1},{2,3},{4,5},{6,7},{8,9},{10,11},{12,13},{14,15},{16,17},{18,19},{..., dimensions={0}, use_global_device_ids=true | all-gather | bytes 49152 | tf_op jit(solution)/shard_map/all_gather | solution.py:539
  42.4 4.2 %shard_map.162 = f32[16,128]{1,0:T(8,128)S(1)} custom-call(f32[5,128]{1,0:T(8,128)S(1)} %broadcast_in_dim.12.where_ref, f32[2,16,128]{2,1,0:T(8,128)S(1)} %get-tuple-element.36.state_ref, f32[2,8,128]{2,1,0:T(8,128)S(1)} %get-tuple-element.37.near_ref, f32[2,2,2,8,128]{4,3,2,1,0:T(8,128)S(1)} %bitcast.28, bf16[2048,128]{1,0:T(8,128)(2,1)S(1)} %get-tuple-element.21.up_ref, ...), custom_call_target="tpu_custom_call" | custom-call | flops 1000000 | bytes 1000000 | tf_op jit(solution)/shard_map/pallas_call | solution.py:481
  46.7 1.8 %all-gather.7 = f32[32,128]{1,0:T(8,128)S(1)} all-gather(f32[16,128]{1,0:T(8,128)S(1)} %shard_map.162), channel_id=9, replica_groups={{0,1},{2,3},{4,5},{6,7},{8,9},{10,11},{12,13},{14,15},{16,17},{18,19},{..., dimensions={0}, use_global_device_ids=true | all-gather | bytes 24576 | tf_op jit(solution)/shard_map/all_gather | solution.py:539
  48.5 3.8 %all-gather.8 = f32[4,8,128]{2,1,0:T(8,128)S(1)} all-gather(f32[2,8,128]{2,1,0:T(8,128)S(1)} %slice.19), channel_id=10, replica_groups={{31,0},{1,2},{3,4},{5,6},{7,8},{9,10},{11,12},{13,14},{15,16},{17,18},{..., dimensions={0}, use_global_device_ids=true | all-gather | bytes 24576 | tf_op jit(solution)/shard_map/all_gather | solution.py:544
  52.3 3.9 %all-gather.9 = f32[4,2,8,128]{3,2,1,0:T(8,128)S(1)} all-gather(f32[2,2,8,128]{3,2,1,0:T(8,128)S(1)} %bitcast.40), channel_id=11, replica_groups={{0,1},{2,3},{4,5},{6,7},{8,9},{10,11},{12,13},{14,15},{16,17},{18,19},{..., dimensions={0}, use_global_device_ids=true | all-gather | bytes 49152 | tf_op jit(solution)/shard_map/all_gather | solution.py:539
  56.2 0.2 shard_map.163.own_ref
  56.3 6.3 %all-gather.10 = f32[4,16,128]{2,1,0:T(8,128)S(1)} all-gather(f32[2,16,128]{2,1,0:T(8,128)S(1)} %shard_map.163.own_ref), channel_id=12, replica_groups={{0,32},{64,96},{128,160},{192,224},{256,288},{320,352},{384,416},{448,4..., dimensions={0}, use_global_device_ids=true | all-gather | bytes 49152 | tf_op jit(solution)/shard_map/all_gather | solution.py:564
  62.6 1.8 %all-gather.11 = f32[4,2,16,128]{3,2,1,0:T(8,128)S(1)} all-gather(f32[2,2,16,128]{3,2,1,0:T(8,128)S(1)} %bitcast.36), channel_id=13, replica_groups={{0,1},{2,3},{4,5},{6,7},{8,9},{10,11},{12,13},{14,15},{16,17},{18,19},{..., dimensions={0}, use_global_device_ids=true | all-gather | bytes 98304 | tf_op jit(solution)/shard_map/all_gather | solution.py:539
  64.5 0.6 shard_map.164
  (4 shorter events, 0.0 us)
Async XLA Ops:
  3.8 6.7 %collective-permute-start = (f32[2,8,128]{2,1,0:T(8,128)S(1)}, f32[2,8,128]{2,1,0:T(8,128)S(1)}, u32[]{:S(2)}, u32[]{:S(2)}) collective-permute-start(f32[2,8,128]{2,1,0:T(8,128)S(1)} %slice.17.near_ref), channel_id=1, source_target_pairs={{31,0},{0,31},{1,2},{2,1},{3,4},{4,3},{5,6},{6,5},{7,8},{8,7},{9,1... | collective-permute-start | bytes 24584 | tf_op jit(solution)/shard_map/ppermute | solution.py:552

commit v7 on v5

--- a/solution.py
+++ b/solution.py
@@ -17,6 +17,8 @@
 GROUPS = SLOTS // 8
 HIDDEN = 256
 AHEAD = 4
+SENT, STATE = slice(0, 8), slice(8, 24)
+GHOSTS, OWN = slice(0, 8), slice(8, 16)
 SHARP = (N_BASIS / CUT_SQ) ** 2
 CENTRES = [CUT_SQ * c / (N_BASIS - 1) for c in range(N_BASIS)]
 F32 = jnp.float32
@@ -185,14 +187,15 @@
     back_ref[...] = jnp.transpose(middle_ref[...].astype(F32)).astype(BF16)
 
 
-def far_tiles(far_ref):
-    return far_ref[0, 0, 0], far_ref[0, 0, 1], far_ref[1, 1, 0], far_ref[1, 1, 1]
+def around(far_ref, rows):
+    if len(far_ref.shape) == 3:
+        return [far_ref[k, rows] for k in range(4)]
+    return [far_ref[0, 0, 0, rows], far_ref[0, 0, 1, rows], far_ref[1, 1, 0, rows], far_ref[1, 1, 1, rows]]
 
 
 def force_kernel(
     where_ref,
-    state_ref,
-    near_ref,
+    home_ref,
     far_ref,
     up_ref,
     down_ref,
@@ -220,9 +223,9 @@
 ):
     scat, ahead_ref = (scratch[:GROUPS], scratch[GROUPS : 2 * GROUPS]), scratch[2 * GROUPS]
     first_core = where_ref[0:1] == 0
-    own = jnp.where(first_core, state_ref[0], state_ref[1])
-    minus2, minus1, plus2, plus3 = far_tiles(far_ref)
-    near0, near1 = near_ref[0], near_ref[1]
+    own = jnp.where(first_core, home_ref[0, STATE], home_ref[1, STATE])
+    minus2, minus1, plus2, plus3 = around(far_ref, SENT)
+    near0, near1 = home_ref[0, SENT], home_ref[1, SENT]
 
     def pick(a, b):
         return jnp.where(first_core, a, b)
@@ -409,34 +412,43 @@
     return total[0:8] + total[8:16] + total[16:24]
 
 
-def moved(state_ref, near_ref, far_ref):
-    minus2, minus1, plus2, plus3 = far_tiles(far_ref)
-    near0, near1 = near_ref[0, 0:8], near_ref[1, 0:8]
-    sets = ((near1, minus1, plus2, minus2), (plus2, near0, plus3, minus1))
-    result = []
+def moved(state, own_grad, ghosts, domain):
+    border0 = state[14:15].astype(jnp.int32)
+    border1 = state[15:16].astype(jnp.int32)
+    inverse = rows_of_two(state[6:7], state[7:8])
+    returned = four_sets(*(ghosts[domain + offset] for offset in (1, -1, 2, -2)))
+    grad = own_grad + returned_sum(returned, border0, border1)
+    speed = state[8:16] - TIME_STEP * grad * inverse
+    return state[0:8] + TIME_STEP * speed, speed, border0, border1
+
+
+def step_kernel(home_ref, far_ref, near_ref, wide_ref, next_ref, around_ref):
+    below, above = wide_ref.at[0, 0], wide_ref.at[1, 1]
+    states = dict(zip((-2, -1, 2, 3), around(far_ref, STATE)))
+    ghosts, owns = {}, {}
+    for k in range(2):
+        states[k] = home_ref[k, STATE]
+        for domain, block in ((k, near_ref.at[k]), (k - 2, below.at[k]), (k + 2, above.at[k])):
+            ghosts[domain], owns[domain] = block[GHOSTS], block[OWN]
+        ghosts[k - 4], ghosts[k + 4] = below[k, 16:24], above[k, 16:24]
+    for domain, state in states.items():
+        place, speed, border0, border1 = moved(state, owns[domain], ghosts, domain)
+        sent = border_positions(place, border0, border1)
+        if domain in (0, 1):
+            next_ref[domain, SENT] = sent
+            next_ref[domain, 8:14] = place[0:6]
+            next_ref[domain, 14:16] = state[6:8]
+            next_ref[domain, 16:22] = speed[0:6]
+            next_ref[domain, 22:24] = state[14:16]
+        else:
+            around_ref[domain + 2 if domain < 0 else domain] = sent
+
+
+def last_kernel(where_ref, home_ref, near_ref, far_ref, next_ref):
+    ghosts = dict(zip((-2, -1, 2, 3), around(far_ref, GHOSTS)))
+    ghosts[0], ghosts[1] = near_ref[0, GHOSTS], near_ref[1, GHOSTS]
     for domain in range(2):
-        state = state_ref[domain]
-        border0 = state[14:15].astype(jnp.int32)
-        border1 = state[15:16].astype(jnp.int32)
-        inverse = rows_of_two(state[6:7], state[7:8])
-        grad = near_ref[domain, 8:16] + returned_sum(four_sets(*sets[domain]), border0, border1)
-        speed = state[8:16] - TIME_STEP * grad * inverse
-        place = state[0:8] + TIME_STEP * speed
-        result.append((place, speed, border0, border1))
-    return result
-
-
-def step_kernel(state_ref, near_ref, far_ref, send_ref, next_ref):
-    for domain, (place, speed, border0, border1) in enumerate(moved(state_ref, near_ref, far_ref)):
-        send_ref[domain] = border_positions(place, border0, border1)
-        next_ref[domain, 0:6] = place[0:6]
-        next_ref[domain, 6:8] = state_ref[domain, 6:8]
-        next_ref[domain, 8:14] = speed[0:6]
-        next_ref[domain, 14:16] = state_ref[domain, 14:16]
-
-
-def last_kernel(where_ref, state_ref, near_ref, far_ref, next_ref):
-    for domain, (place, speed, _, _) in enumerate(moved(state_ref, near_ref, far_ref)):
+        place, speed, _, _ = moved(home_ref[domain, STATE], near_ref[domain, OWN], ghosts, domain)
         next_ref[domain, 0:6] = place[0:6]
         next_ref[domain, 6:8] = jnp.broadcast_to(where_ref[4:5], (2, LANES))
         next_ref[domain, 8:16] = speed
@@ -534,8 +546,8 @@
     return lax.all_gather(value, "space", axis_index_groups=groups)
 
 
-def across_chips(value, domains):
-    groups = [[(2 * i - 1) % domains, 2 * i] for i in range(domains // 2)]
+def across_chips(value, domains, chips=1):
+    groups = [[(2 * (i - chips) + 1) % domains, 2 * i] for i in range(domains // 2)]
     return lax.all_gather(value, "space", axis_index_groups=groups)
 
 
@@ -597,29 +609,20 @@
     arrays = tuple(pltpu.with_memory_space_constraint(a, pltpu.HBM) for a in arrays)
     made, space = begin_shapes(arrays)
     begin, *fixed = call(begin_kernel, (), arrays, made, space, inputs=anywhere)
-    both = on_chip(begin, domains)
-    send, state = both[:, 0:8], both[:, 8:24]
+    home = on_chip(begin, domains)
+    far = on_chip(across_chips(home, domains), domains)
     for step in range(STEPS):
-        far = on_chip(across_chips(send, domains), domains)
-        partial = call(
-            force_kernel,
-            (),
-            (
-                where_to,
-                state,
-                send,
-                far,
-                *fixed,
-            ),
-            tiles(16),
-            force_scratch(),
-        )
+        partial = call(force_kernel, (), (where_to, home, far, *fixed), tiles(16), force_scratch())
         near = on_chip(partial, domains)
-        far = on_chip(across_chips(near[:, 0:8], domains), domains)
         if step < STEPS - 1:
-            send, state = call(step_kernel, (), (state, near, far), [tiles(2, 8), tiles(2, 16)])
+            one = across_chips(near, domains)
+            two = across_chips(near[:, GHOSTS], domains, 2)
+            wide = on_chip(jnp.concatenate([one, two], axis=2), domains)
+            shapes = [tiles(2, 24), tiles(4, 8)]
+            home, far = call(step_kernel, (), (home, far, near, wide), shapes)
         else:
-            state = call(last_kernel, (), (where_to, state, near, far), tiles(2, 16))
+            far = on_chip(across_chips(near[:, GHOSTS], domains), domains)
+            state = call(last_kernel, (), (where_to, home, near, far), tiles(2, 16))
     mates = on_chip(along_ladder(state, rungs, domains), domains)
     shape = particle_coordinates.shape
     out = jax.ShapeDtypeStruct((1, particle_coordinates.size), F32)

time: 64.8 us -> 62.4 us (0.963)
  blocking collectives: 50.7 us -> 48.3 us
    all_gather x8 -> x7, blocking collectives: 29.3 us -> 25.9 us  [on_chip(): return lax.all_gather(value, 'space', axis_index_groups=groups)]
    all_gather x4, blocking collectives: 15.1 us -> 16.1 us  [across_chips(): return lax.all_gather(value, 'space', axis_index_groups=groups)]
where the time goes in v7:
time: 62.4 us; the launch traced here: 62.2 us
  blocking collectives  48.3 us (77%)
  Pallas kernels  11.7 us (19%)
  between operations  1.98 us (3%)
    all_gather x7, blocking collectives, on_chip(): return lax.all_gather(value, 'space', axis_index_groups=groups)  25.9 us
    all_gather x4, blocking collectives, across_chips(): return lax.all_gather(value, 'space', axis_index_groups=groups)  16.1 us
    pallas_call x6, Pallas kernels, call(): pl.pallas_call(kernel, out_shape=out_shape, in_specs=[smem()] * len(scala...  11.7 us
    all_gather x1, blocking collectives, along_ladder(): return lax.all_gather(value, ('replica', 'space'), axis_index_groups=groups)  6.27 us

profile of v7, /device:TPU:7, one launch (start us, length us, event | category | flops | bytes accessed | tf_op | source)
XLA Modules:
  0.0 62.2 jit_solution(15903092610338488259)
XLA Ops:
  2.0 0.1 stack.23
  2.0 0.1 broadcast_in_dim.12.where_ref
  2.1 2.0 %shard_map.158 = (f32[24,128]{1,0:T(8,128)S(1)}, bf16[2048,128]{1,0:T(8,128)(2,1)S(1)}, bf16[32,256]{1,0:T(8,128)(2,1)S(1)}, bf16[16,128]{1,0:T(8,128)(2,1)S(1)}...) custom-call(f32[1,768]{1,0:T(1,128)} %bitcast.47, ...), custom_call_target="tpu_custom_call" | custom-call | flops 1000000 | bytes 1000000 | tf_op jit(solution)/shard_map/pallas_call | solution.py:490
  4.1 2.2 %all-gather = f32[48,128]{1,0:T(8,128)S(1)} all-gather(f32[24,128]{1,0:T(8,128)S(1)} %get-tuple-element.22), channel_id=2, replica_groups={{0,1},{2,3},{4,5},{6,7},{8,9},{10,11},{12,13},{14,15},{16,17},{18,19},{..., dimensions={0}, use_global_device_ids=true | all-gather | bytes 36864 | tf_op jit(solution)/shard_map/all_gather | solution.py:546
  6.3 3.9 %all-gather.1 = f32[4,24,128]{2,1,0:T(8,128)S(1)} all-gather(f32[2,24,128]{2,1,0:T(8,128)S(1)} %bitcast.29), channel_id=3, replica_groups={{31,0},{1,2},{3,4},{5,6},{7,8},{9,10},{11,12},{13,14},{15,16},{17,18},{..., dimensions={0}, use_global_device_ids=true | all-gather | bytes 73728 | tf_op jit(solution)/shard_map/all_gather | solution.py:551
  10.2 9.9 %all-gather.2 = f32[4,2,24,128]{3,2,1,0:T(8,128)S(1)} all-gather(f32[2,2,24,128]{3,2,1,0:T(8,128)S(1)} %bitcast.40), channel_id=4, replica_groups={{0,1},{2,3},{4,5},{6,7},{8,9},{10,11},{12,13},{14,15},{16,17},{18,19},{..., dimensions={0}, use_global_device_ids=true | all-gather | bytes 147456 | tf_op jit(solution)/shard_map/all_gather | solution.py:546
  20.2 4.3 %shard_map.159 = f32[16,128]{1,0:T(8,128)S(1)} custom-call(f32[5,128]{1,0:T(8,128)S(1)} %broadcast_in_dim.12.where_ref, f32[2,24,128]{2,1,0:T(8,128)S(1)} %bitcast.30, f32[2,2,2,24,128]{4,3,2,1,0:T(8,128)S(1)} %bitcast.27, bf16[2048,128]{1,0:T(8,128)(2,1)S(1)} %get-tuple-element.23.up_ref, bf16[32,256]{1,0:T(8,128)(2,1)S(1)} %get-tuple-element.24.down_ref, ...), custom_call_target="tpu_custom_call" | custom-call | flops 1000000 | bytes 1000000 | tf_op jit(solution)/shard_map/pallas_call | solution.py:490
  24.5 1.8 %all-gather.3 = f32[32,128]{1,0:T(8,128)S(1)} all-gather(f32[16,128]{1,0:T(8,128)S(1)} %shard_map.159), channel_id=5, replica_groups={{0,1},{2,3},{4,5},{6,7},{8,9},{10,11},{12,13},{14,15},{16,17},{18,19},{..., dimensions={0}, use_global_device_ids=true | all-gather | bytes 24576 | tf_op jit(solution)/shard_map/all_gather | solution.py:546
  26.3 3.8 %all-gather.5 = f32[4,8,128]{2,1,0:T(8,128)S(1)} all-gather(f32[2,8,128]{2,1,0:T(8,128)S(1)} %slice.8), channel_id=7, replica_groups={{29,0},{31,2},{1,4},{3,6},{5,8},{7,10},{9,12},{11,14},{13,16},{15,18},{..., dimensions={0}, use_global_device_ids=true | all-gather | bytes 24576 | tf_op jit(solution)/shard_map/all_gather | solution.py:551
  30.1 4.7 %all-gather.4 = f32[4,16,128]{2,1,0:T(8,128)S(1)} all-gather(f32[2,16,128]{2,1,0:T(8,128)S(1)} %bitcast.35), channel_id=6, replica_groups={{31,0},{1,2},{3,4},{5,6},{7,8},{9,10},{11,12},{13,14},{15,16},{17,18},{..., dimensions={0}, use_global_device_ids=true | all-gather | bytes 49152 | tf_op jit(solution)/shard_map/all_gather | solution.py:551
  34.8 4.3 %all-gather.6 = f32[4,2,24,128]{3,2,1,0:T(8,128)S(1)} all-gather(f32[2,2,24,128]{3,2,1,0:T(8,128)S(1)} %pad_maximum_fusion), channel_id=8, replica_groups={{0,1},{2,3},{4,5},{6,7},{8,9},{10,11},{12,13},{14,15},{16,17},{18,19},{..., dimensions={0}, use_global_device_ids=true | all-gather | bytes 147456 | tf_op jit(solution)/shard_map/all_gather | solution.py:546
  39.1 0.3 shard_map.160
  39.4 4.3 %shard_map.161 = f32[16,128]{1,0:T(8,128)S(1)} custom-call(f32[5,128]{1,0:T(8,128)S(1)} %broadcast_in_dim.12.where_ref, f32[2,24,128]{2,1,0:T(8,128)S(1)} %get-tuple-element.38.home_ref, f32[4,8,128]{2,1,0:T(8,128)S(1)} %get-tuple-element.39.far_ref, bf16[2048,128]{1,0:T(8,128)(2,1)S(1)} %get-tuple-element.23.up_ref, ...), custom_call_target="tpu_custom_call" | custom-call | flops 1000000 | bytes 1000000 | tf_op jit(solution)/shard_map/pallas_call | solution.py:490
  43.7 1.8 %all-gather.7 = f32[32,128]{1,0:T(8,128)S(1)} all-gather(f32[16,128]{1,0:T(8,128)S(1)} %shard_map.161), channel_id=9, replica_groups={{0,1},{2,3},{4,5},{6,7},{8,9},{10,11},{12,13},{14,15},{16,17},{18,19},{..., dimensions={0}, use_global_device_ids=true | all-gather | bytes 24576 | tf_op jit(solution)/shard_map/all_gather | solution.py:546
  45.6 3.8 %all-gather.8 = f32[4,8,128]{2,1,0:T(8,128)S(1)} all-gather(f32[2,8,128]{2,1,0:T(8,128)S(1)} %slice.9), channel_id=10, replica_groups={{31,0},{1,2},{3,4},{5,6},{7,8},{9,10},{11,12},{13,14},{15,16},{17,18},{..., dimensions={0}, use_global_device_ids=true | all-gather | bytes 24576 | tf_op jit(solution)/shard_map/all_gather | solution.py:551
  49.3 3.9 %all-gather.9 = f32[4,2,8,128]{3,2,1,0:T(8,128)S(1)} all-gather(f32[2,2,8,128]{3,2,1,0:T(8,128)S(1)} %bitcast.43), channel_id=11, replica_groups={{0,1},{2,3},{4,5},{6,7},{8,9},{10,11},{12,13},{14,15},{16,17},{18,19},{..., dimensions={0}, use_global_device_ids=true | all-gather | bytes 49152 | tf_op jit(solution)/shard_map/all_gather | solution.py:546
  53.3 0.2 shard_map.162.own_ref
  53.4 6.3 %all-gather.10 = f32[4,16,128]{2,1,0:T(8,128)S(1)} all-gather(f32[2,16,128]{2,1,0:T(8,128)S(1)} %shard_map.162.own_ref), channel_id=12, replica_groups={{0,32},{64,96},{128,160},{192,224},{256,288},{320,352},{384,416},{448,4..., dimensions={0}, use_global_device_ids=true | all-gather | bytes 49152 | tf_op jit(solution)/shard_map/all_gather | solution.py:563
  59.7 1.8 %all-gather.11 = f32[4,2,16,128]{3,2,1,0:T(8,128)S(1)} all-gather(f32[2,2,16,128]{3,2,1,0:T(8,128)S(1)} %bitcast.42), channel_id=13, replica_groups={{0,1},{2,3},{4,5},{6,7},{8,9},{10,11},{12,13},{14,15},{16,17},{18,19},{..., dimensions={0}, use_global_device_ids=true | all-gather | bytes 98304 | tf_op jit(solution)/shard_map/all_gather | solution.py:546
  61.5 0.6 %shard_map.163 = (f32[1,768]{1,0:T(1,128)}, f32[1,768]{1,0:T(1,128)}) custom-call(f32[5,128]{1,0:T(8,128)S(1)} %broadcast_in_dim.12.where_ref, f32[2,16,128]{2,1,0:T(8,128)S(1)} %shard_map.162.own_ref, f32[2,2,2,16,128]{4,3,2,1,0:T(8,128)S(1)} %bitcast.33), custom_call_target="tpu_custom_call" | custom-call | flops 1000000 | bytes 1000000 | tf_op jit(solution)/shard_map/pallas_call | solution.py:490
  (3 shorter events, 0.0 us)

commit v8 on v7

--- a/solution.py
+++ b/solution.py
@@ -422,17 +422,19 @@
     return state[0:8] + TIME_STEP * speed, speed, border0, border1
 
 
-def step_kernel(home_ref, far_ref, near_ref, wide_ref, next_ref, around_ref):
-    below, above = wide_ref.at[0, 0], wide_ref.at[1, 1]
+def step_kernel(where_ref, home_ref, far_ref, wide_ref, next_ref, around_ref):
+    blocks = [wide_ref.at[0, 0], wide_ref.at[0, 1], wide_ref.at[1, 1]]
+    first_chip = where_ref[5:6] == 0
+
+    def forces(domain, rows):
+        one, other = (blocks[k // 4][k % 4 // 2, k % 2, rows] for k in (domain + 4, domain + 6))
+        return jnp.where(first_chip, one, other)
+
     states = dict(zip((-2, -1, 2, 3), around(far_ref, STATE)))
-    ghosts, owns = {}, {}
-    for k in range(2):
-        states[k] = home_ref[k, STATE]
-        for domain, block in ((k, near_ref.at[k]), (k - 2, below.at[k]), (k + 2, above.at[k])):
-            ghosts[domain], owns[domain] = block[GHOSTS], block[OWN]
-        ghosts[k - 4], ghosts[k + 4] = below[k, 16:24], above[k, 16:24]
+    states[0], states[1] = home_ref[0, STATE], home_ref[1, STATE]
+    ghosts = {domain: forces(domain, GHOSTS) for domain in range(-4, 6)}
     for domain, state in states.items():
-        place, speed, border0, border1 = moved(state, owns[domain], ghosts, domain)
+        place, speed, border0, border1 = moved(state, forces(domain, OWN), ghosts, domain)
         sent = border_positions(place, border0, border1)
         if domain in (0, 1):
             next_ref[domain, SENT] = sent
@@ -548,6 +550,11 @@
 
 def across_chips(value, domains, chips=1):
     groups = [[(2 * (i - chips) + 1) % domains, 2 * i] for i in range(domains // 2)]
+    return lax.all_gather(value, "space", axis_index_groups=groups)
+
+
+def across_pair(value, domains):
+    groups = [[4 * i + core, 4 * i + 2 + core] for i in range(domains // 4) for core in range(2)]
     return lax.all_gather(value, "space", axis_index_groups=groups)
 
 
@@ -588,8 +595,9 @@
     side = jnp.where((mate > rank) == (odd == 0), 0, 1)
     position = jnp.where(side == 0, 1 - odd, odd)
     where_to = [value.astype(F32) for value in (core, mate != rank, side, position)]
-    where_to = jnp.stack(where_to + [thermal_levels[0]])
-    where_to = jnp.broadcast_to(where_to[:, None], (5, LANES))
+    chip = lax.axis_index("space") // 2 % 2
+    where_to = jnp.stack(where_to + [thermal_levels[0], chip.astype(F32)])
+    where_to = jnp.broadcast_to(where_to[:, None], (6, LANES))
 
     arrays = (
         particle_coordinates.reshape(1, -1),
@@ -615,11 +623,10 @@
         partial = call(force_kernel, (), (where_to, home, far, *fixed), tiles(16), force_scratch())
         near = on_chip(partial, domains)
         if step < STEPS - 1:
-            one = across_chips(near, domains)
-            two = across_chips(near[:, GHOSTS], domains, 2)
-            wide = on_chip(jnp.concatenate([one, two], axis=2), domains)
+            pair = across_pair(near, domains)
+            wide = on_chip(across_chips(pair, domains, 2), domains)
             shapes = [tiles(2, 24), tiles(4, 8)]
-            home, far = call(step_kernel, (), (home, far, near, wide), shapes)
+            home, far = call(step_kernel, (), (where_to, home, far, wide), shapes)
         else:
             far = on_chip(across_chips(near[:, GHOSTS], domains), domains)
             state = call(last_kernel, (), (where_to, home, near, far), tiles(2, 16))

time: 62.4 us -> 61.2 us (0.981)
  blocking collectives: 48.3 us -> 47 us
    all_gather x4 -> x3, blocking collectives: 16.1 us -> 11.7 us  [across_chips(): return lax.all_gather(value, 'space', axis_index_groups=groups)]
    all_gather x0 -> x1, blocking collectives: none -> 3.25 us  [across_pair(): return lax.all_gather(value, 'space', axis_index_groups=groups)]
where the time goes in v8:
time: 61.2 us; the launch traced here: 60.9 us
  blocking collectives  47 us (77%)
  Pallas kernels  11.7 us (19%)
  between operations  2.01 us (3%)
    all_gather x7, blocking collectives, on_chip(): return lax.all_gather(value, 'space', axis_index_groups=groups)  25.8 us
    pallas_call x6, Pallas kernels, call(): pl.pallas_call(kernel, out_shape=out_shape, in_specs=[smem()] * len(scala...  11.7 us
    all_gather x3, blocking collectives, across_chips(): return lax.all_gather(value, 'space', axis_index_groups=groups)  11.7 us
    all_gather x1, blocking collectives, along_ladder(): return lax.all_gather(value, ('replica', 'space'), axis_index_groups=groups)  6.27 us
    all_gather x1, blocking collectives, across_pair(): return lax.all_gather(value, 'space', axis_index_groups=groups)  3.25 us

profile of v8, /device:TPU:7, one launch (start us, length us, event | category | flops | bytes accessed | tf_op | source)
XLA Modules:
  0.0 60.9 jit_solution(3096272898913398533)
XLA Ops:
  2.0 0.1 stack.27
  2.1 0.1 broadcast_in_dim.12.where_ref
  2.1 2.0 %shard_map.158 = (f32[24,128]{1,0:T(8,128)S(1)}, bf16[2048,128]{1,0:T(8,128)(2,1)S(1)}, bf16[32,256]{1,0:T(8,128)(2,1)S(1)}, bf16[16,128]{1,0:T(8,128)(2,1)S(1)}...) custom-call(f32[1,768]{1,0:T(1,128)} %bitcast.46, ...), custom_call_target="tpu_custom_call" | custom-call | flops 1000000 | bytes 1000000 | tf_op jit(solution)/shard_map/pallas_call | solution.py:492
  4.2 2.2 %all-gather = f32[48,128]{1,0:T(8,128)S(1)} all-gather(f32[24,128]{1,0:T(8,128)S(1)} %get-tuple-element.22), channel_id=2, replica_groups={{0,1},{2,3},{4,5},{6,7},{8,9},{10,11},{12,13},{14,15},{16,17},{18,19},{..., dimensions={0}, use_global_device_ids=true | all-gather | bytes 36864 | tf_op jit(solution)/shard_map/all_gather | solution.py:548
  6.3 3.9 %all-gather.1 = f32[4,24,128]{2,1,0:T(8,128)S(1)} all-gather(f32[2,24,128]{2,1,0:T(8,128)S(1)} %bitcast.31), channel_id=3, replica_groups={{31,0},{1,2},{3,4},{5,6},{7,8},{9,10},{11,12},{13,14},{15,16},{17,18},{..., dimensions={0}, use_global_device_ids=true | all-gather | bytes 73728 | tf_op jit(solution)/shard_map/all_gather | solution.py:553
  10.2 10.0 %all-gather.2 = f32[4,2,24,128]{3,2,1,0:T(8,128)S(1)} all-gather(f32[2,2,24,128]{3,2,1,0:T(8,128)S(1)} %bitcast.39), channel_id=4, replica_groups={{0,1},{2,3},{4,5},{6,7},{8,9},{10,11},{12,13},{14,15},{16,17},{18,19},{..., dimensions={0}, use_global_device_ids=true | all-gather | bytes 147456 | tf_op jit(solution)/shard_map/all_gather | solution.py:548
  20.2 4.3 %shard_map.159 = f32[16,128]{1,0:T(8,128)S(1)} custom-call(f32[6,128]{1,0:T(8,128)S(1)} %broadcast_in_dim.12.where_ref, f32[2,24,128]{2,1,0:T(8,128)S(1)} %bitcast.32, f32[2,2,2,24,128]{4,3,2,1,0:T(8,128)S(1)} %bitcast.28, bf16[2048,128]{1,0:T(8,128)(2,1)S(1)} %get-tuple-element.23.up_ref, bf16[32,256]{1,0:T(8,128)(2,1)S(1)} %get-tuple-element.24.down_ref, ...), custom_call_target="tpu_custom_call" | custom-call | flops 1000000 | bytes 1000000 | tf_op jit(solution)/shard_map/pallas_call | solution.py:492
  24.5 1.8 %all-gather.3 = f32[32,128]{1,0:T(8,128)S(1)} all-gather(f32[16,128]{1,0:T(8,128)S(1)} %shard_map.159), channel_id=5, replica_groups={{0,1},{2,3},{4,5},{6,7},{8,9},{10,11},{12,13},{14,15},{16,17},{18,19},{..., dimensions={0}, use_global_device_ids=true | all-gather | bytes 24576 | tf_op jit(solution)/shard_map/all_gather | solution.py:548
  26.3 3.3 %all-gather.4 = f32[4,16,128]{2,1,0:T(8,128)S(1)} all-gather(f32[2,16,128]{2,1,0:T(8,128)S(1)} %bitcast.42), channel_id=6, replica_groups={{0,2},{1,3},{4,6},{5,7},{8,10},{9,11},{12,14},{13,15},{16,18},{17,19},{..., dimensions={0}, use_global_device_ids=true | all-gather | bytes 49152 | tf_op jit(solution)/shard_map/all_gather | solution.py:558
  29.6 4.0 %all-gather.5 = f32[4,2,16,128]{3,2,1,0:T(8,128)S(1)} all-gather(f32[2,2,16,128]{3,2,1,0:T(8,128)S(1)} %bitcast.40), channel_id=7, replica_groups={{29,0},{31,2},{1,4},{3,6},{5,8},{7,10},{9,12},{11,14},{13,16},{15,18},{..., dimensions={0}, use_global_device_ids=true | all-gather | bytes 98304 | tf_op jit(solution)/shard_map/all_gather | solution.py:553
  33.6 4.2 %all-gather.6 = f32[4,2,2,16,128]{4,3,2,1,0:T(8,128)S(1)} all-gather(f32[2,2,2,16,128]{4,3,2,1,0:T(8,128)S(1)} %bitcast.38), channel_id=8, replica_groups={{0,1},{2,3},{4,5},{6,7},{8,9},{10,11},{12,13},{14,15},{16,17},{18,19},{..., dimensions={0}, use_global_device_ids=true | all-gather | bytes 196608 | tf_op jit(solution)/shard_map/all_gather | solution.py:548
  37.8 0.3 shard_map.160
  38.1 4.3 %shard_map.161 = f32[16,128]{1,0:T(8,128)S(1)} custom-call(f32[6,128]{1,0:T(8,128)S(1)} %broadcast_in_dim.12.where_ref, f32[2,24,128]{2,1,0:T(8,128)S(1)} %get-tuple-element.38.home_ref, f32[4,8,128]{2,1,0:T(8,128)S(1)} %get-tuple-element.39.far_ref, bf16[2048,128]{1,0:T(8,128)(2,1)S(1)} %get-tuple-element.23.up_ref, ...), custom_call_target="tpu_custom_call" | custom-call | flops 1000000 | bytes 1000000 | tf_op jit(solution)/shard_map/pallas_call | solution.py:492
  42.5 1.8 %all-gather.7 = f32[32,128]{1,0:T(8,128)S(1)} all-gather(f32[16,128]{1,0:T(8,128)S(1)} %shard_map.161), channel_id=9, replica_groups={{0,1},{2,3},{4,5},{6,7},{8,9},{10,11},{12,13},{14,15},{16,17},{18,19},{..., dimensions={0}, use_global_device_ids=true | all-gather | bytes 24576 | tf_op jit(solution)/shard_map/all_gather | solution.py:548
  44.3 3.8 %all-gather.8 = f32[4,8,128]{2,1,0:T(8,128)S(1)} all-gather(f32[2,8,128]{2,1,0:T(8,128)S(1)} %slice.4), channel_id=10, replica_groups={{31,0},{1,2},{3,4},{5,6},{7,8},{9,10},{11,12},{13,14},{15,16},{17,18},{..., dimensions={0}, use_global_device_ids=true | all-gather | bytes 24576 | tf_op jit(solution)/shard_map/all_gather | solution.py:553
  48.1 3.9 %all-gather.9 = f32[4,2,8,128]{3,2,1,0:T(8,128)S(1)} all-gather(f32[2,2,8,128]{3,2,1,0:T(8,128)S(1)} %bitcast.43), channel_id=11, replica_groups={{0,1},{2,3},{4,5},{6,7},{8,9},{10,11},{12,13},{14,15},{16,17},{18,19},{..., dimensions={0}, use_global_device_ids=true | all-gather | bytes 49152 | tf_op jit(solution)/shard_map/all_gather | solution.py:548
  52.0 0.2 shard_map.162.own_ref
  52.2 6.3 %all-gather.10 = f32[4,16,128]{2,1,0:T(8,128)S(1)} all-gather(f32[2,16,128]{2,1,0:T(8,128)S(1)} %shard_map.162.own_ref), channel_id=12, replica_groups={{0,32},{64,96},{128,160},{192,224},{256,288},{320,352},{384,416},{448,4..., dimensions={0}, use_global_device_ids=true | all-gather | bytes 49152 | tf_op jit(solution)/shard_map/all_gather | solution.py:570
  58.4 1.8 %all-gather.11 = f32[4,2,16,128]{3,2,1,0:T(8,128)S(1)} all-gather(f32[2,2,16,128]{3,2,1,0:T(8,128)S(1)} %bitcast.41), channel_id=13, replica_groups={{0,1},{2,3},{4,5},{6,7},{8,9},{10,11},{12,13},{14,15},{16,17},{18,19},{..., dimensions={0}, use_global_device_ids=true | all-gather | bytes 98304 | tf_op jit(solution)/shard_map/all_gather | solution.py:548
  60.3 0.6 %shard_map.163 = (f32[1,768]{1,0:T(1,128)}, f32[1,768]{1,0:T(1,128)}) custom-call(f32[6,128]{1,0:T(8,128)S(1)} %broadcast_in_dim.12.where_ref, f32[2,16,128]{2,1,0:T(8,128)S(1)} %shard_map.162.own_ref, f32[2,2,2,16,128]{4,3,2,1,0:T(8,128)S(1)} %bitcast.34), custom_call_target="tpu_custom_call" | custom-call | flops 1000000 | bytes 1000000 | tf_op jit(solution)/shard_map/pallas_call | solution.py:492
  (1 shorter events, 0.0 us)

commit v9 on v8

--- a/solution.py
+++ b/solution.py
@@ -184,13 +184,16 @@
     atom_ref[...] = jnp.transpose(jnp.broadcast_to(0.5 * atom_out_ref[...], (LANES, HIDDEN)))
     first_ref[...] = jnp.transpose((0.5 * opening_ref[...]).astype(F32)).astype(BF16)
     second_ref[...] = 0.5 * middle_ref[...]
-    back_ref[...] = jnp.transpose(middle_ref[...].astype(F32)).astype(BF16)
-
-
-def around(far_ref, rows):
+    back_ref[...] = middle_ref[...]
+
+
+def around(where_ref, far_ref, rows):
     if len(far_ref.shape) == 3:
         return [far_ref[k, rows] for k in range(4)]
-    return [far_ref[0, 0, 0, rows], far_ref[0, 0, 1, rows], far_ref[1, 1, 0, rows], far_ref[1, 1, 1, rows]]
+    first_chip = where_ref[5:6] == 0
+    before = [jnp.where(first_chip, far_ref[1, 0, k, rows], far_ref[0, 0, k, rows]) for k in range(2)]
+    after = [jnp.where(first_chip, far_ref[0, 1, k, rows], far_ref[1, 1, k, rows]) for k in range(2)]
+    return before + after
 
 
 def force_kernel(
@@ -224,7 +227,7 @@
     scat, ahead_ref = (scratch[:GROUPS], scratch[GROUPS : 2 * GROUPS]), scratch[2 * GROUPS]
     first_core = where_ref[0:1] == 0
     own = jnp.where(first_core, home_ref[0, STATE], home_ref[1, STATE])
-    minus2, minus1, plus2, plus3 = around(far_ref, SENT)
+    minus2, minus1, plus2, plus3 = around(where_ref, far_ref, SENT)
     near0, near1 = home_ref[0, SENT], home_ref[1, SENT]
 
     def pick(a, b):
@@ -299,7 +302,7 @@
     half = nn_dot(second_ref[...], hidden_one)
     th = jnp.tanh(half)
     g_second = (atom_w * (1.0 + th + half * (1.0 - th * th))).astype(BF16)
-    g_hidden = nn_dot(back_ref[...], g_second)
+    g_hidden = tn_dot(back_ref[...], g_second)
     g_first = (g_hidden * slope_one).astype(BF16)
     g_env = nn_dot(opening_ref[...], g_first)
 
@@ -423,14 +426,21 @@
 
 
 def step_kernel(where_ref, home_ref, far_ref, wide_ref, next_ref, around_ref):
-    blocks = [wide_ref.at[0, 0], wide_ref.at[0, 1], wide_ref.at[1, 1]]
-    first_chip = where_ref[5:6] == 0
+    first_chip, even_pair = where_ref[5:6] == 0, where_ref[6:7] == 0
+    blocks = (
+        (wide_ref.at[1, 0], wide_ref.at[0, 0]),
+        (wide_ref.at[0, 0], wide_ref.at[0, 1]),
+        (wide_ref.at[0, 1], wide_ref.at[1, 1]),
+    )
+
+    def on_line(k, rows):
+        even, odd = (block[k % 4 // 2, k % 2, rows] for block in blocks[k // 4])
+        return jnp.where(even_pair, even, odd)
 
     def forces(domain, rows):
-        one, other = (blocks[k // 4][k % 4 // 2, k % 2, rows] for k in (domain + 4, domain + 6))
-        return jnp.where(first_chip, one, other)
-
-    states = dict(zip((-2, -1, 2, 3), around(far_ref, STATE)))
+        return jnp.where(first_chip, on_line(domain + 4, rows), on_line(domain + 6, rows))
+
+    states = dict(zip((-2, -1, 2, 3), around(where_ref, far_ref, STATE)))
     states[0], states[1] = home_ref[0, STATE], home_ref[1, STATE]
     ghosts = {domain: forces(domain, GHOSTS) for domain in range(-4, 6)}
     for domain, state in states.items():
@@ -447,7 +457,7 @@
 
 
 def last_kernel(where_ref, home_ref, near_ref, far_ref, next_ref):
-    ghosts = dict(zip((-2, -1, 2, 3), around(far_ref, GHOSTS)))
+    ghosts = dict(zip((-2, -1, 2, 3), around(where_ref, far_ref, GHOSTS)))
     ghosts[0], ghosts[1] = near_ref[0, GHOSTS], near_ref[1, GHOSTS]
     for domain in range(2):
         place, speed, _, _ = moved(home_ref[domain, STATE], near_ref[domain, OWN], ghosts, domain)
@@ -548,25 +558,46 @@
     return lax.all_gather(value, "space", axis_index_groups=groups)
 
 
-def across_chips(value, domains, chips=1):
-    groups = [[(2 * (i - chips) + 1) % domains, 2 * i] for i in range(domains // 2)]
+def across_chips(value, domains):
+    groups = []
+    for i in range(domains // 4):
+        groups += [[4 * i, 4 * i + 2], [4 * i + 3, (4 * i + 5) % domains]]
     return lax.all_gather(value, "space", axis_index_groups=groups)
 
 
 def across_pair(value, domains):
-    groups = [[4 * i + core, 4 * i + 2 + core] for i in range(domains // 4) for core in range(2)]
+    groups = []
+    for i in range(domains // 4):
+        groups += [[4 * i, 4 * i + 3], [4 * i + 1, 4 * i + 2]]
     return lax.all_gather(value, "space", axis_index_groups=groups)
+
+
+def between_pairs(value, domains):
+    groups = []
+    for i in range(0, domains // 4, 2):
+        for chip in range(2):
+            first = 4 * i + 2 * chip
+            groups += [[first, first + 4], [first + 5, (first + 9) % domains]]
+    return lax.all_gather(value, "space", axis_index_groups=groups)
+
+
+def even_odd_core(rank, rungs):
+    far = (rank % 4 == 0) | (rank % 4 == 3)
+    return 1 - (far & (rank > 0) & (rank < rungs - 1))
 
 
 def along_ladder(value, rungs, domains):
     groups = []
-    for domain in range(domains):
-        shift = domain % 2
-        for low in range(shift, rungs - shift, 2):
-            groups.append([low * domains + domain, (low + 1) * domains + domain])
-        if shift and domain // 2 % 2 == 0:
+    for chip in range(0, domains, 2):
+        for low in range(rungs - 1):
+            pair = []
+            for rank in (low, low + 1):
+                core = even_odd_core(rank, rungs)
+                pair.append(rank * domains + chip + (core if low % 2 == 0 else 1 - core))
+            groups.append(pair)
+        if chip % 4 == 0:
             for end in (0, rungs - 1):
-                groups.append([end * domains + domain, end * domains + domain + 2])
+                groups.append([end * domains + chip, end * domains + chip + 2])
     return lax.all_gather(value, ("replica", "space"), axis_index_groups=groups)
 
 
@@ -592,12 +623,15 @@
     rank = lax.axis_index("replica")
     mate = swap_mates[0]
     odd = rank % 2
-    side = jnp.where((mate > rank) == (odd == 0), 0, 1)
-    position = jnp.where(side == 0, 1 - odd, odd)
+    even_odd = (mate > rank) == (odd == 0)
+    side = even_odd_core(rank, rungs)
+    side = jnp.where(even_odd, side, 1 - side)
+    position = jnp.where(even_odd, 1 - odd, odd)
     where_to = [value.astype(F32) for value in (core, mate != rank, side, position)]
-    chip = lax.axis_index("space") // 2 % 2
-    where_to = jnp.stack(where_to + [thermal_levels[0], chip.astype(F32)])
-    where_to = jnp.broadcast_to(where_to[:, None], (6, LANES))
+    here = lax.axis_index("space")
+    chip, pair = (here // 2 % 2).astype(F32), (here // 4 % 2).astype(F32)
+    where_to = jnp.stack(where_to + [thermal_levels[0], chip, pair])
+    where_to = jnp.broadcast_to(where_to[:, None], (7, LANES))
 
     arrays = (
         particle_coordinates.reshape(1, -1),
@@ -624,7 +658,7 @@
         near = on_chip(partial, domains)
         if step < STEPS - 1:
             pair = across_pair(near, domains)
-            wide = on_chip(across_chips(pair, domains, 2), domains)
+            wide = on_chip(between_pairs(pair, domains), domains)
             shapes = [tiles(2, 24), tiles(4, 8)]
             home, far = call(step_kernel, (), (where_to, home, far, wide), shapes)
         else:

time: 61.2 us -> 59.3 us (0.969)
  blocking collectives: 47 us -> 45.1 us
    all_gather x7, blocking collectives: 25.8 us -> 13.2 us  [on_chip(): return lax.all_gather(value, 'space', axis_index_groups=groups)]
    all_gather x3 -> x2, blocking collectives: 11.7 us -> 16.9 us  [across_chips(): return lax.all_gather(value, 'space', axis_index_groups=groups)]
    all_gather x0 -> x1, blocking collectives: none -> 4.64 us  [between_pairs(): return lax.all_gather(value, 'space', axis_index_groups=groups)]
where the time goes in v9:
time: 59.3 us; the launch traced here: 59 us
  blocking collectives  45.1 us (76%)
  Pallas kernels  11.7 us (20%)
  between operations  2.05 us (3%)
    all_gather x2, blocking collectives, across_chips(): return lax.all_gather(value, 'space', axis_index_groups=groups)  16.9 us
    all_gather x7, blocking collectives, on_chip(): return lax.all_gather(value, 'space', axis_index_groups=groups)  13.2 us
    pallas_call x6, Pallas kernels, call(): pl.pallas_call(kernel, out_shape=out_shape, in_specs=[smem()] * len(scala...  11.7 us
    all_gather x1, blocking collectives, along_ladder(): return lax.all_gather(value, ('replica', 'space'), axis_index_groups=groups)  6.45 us
    all_gather x1, blocking collectives, between_pairs(): return lax.all_gather(value, 'space', axis_index_groups=groups)  4.64 us
    all_gather x1, blocking collectives, across_pair(): return lax.all_gather(value, 'space', axis_index_groups=groups)  3.83 us

profile of v9, /device:TPU:7, one launch (start us, length us, event | category | flops | bytes accessed | tf_op | source)
XLA Modules:
  0.0 59.0 jit_solution(12384628575066367660)
XLA Ops:
  2.0 0.1 stack.31
  2.1 0.1 broadcast_in_dim.12.where_ref
  2.2 2.0 %shard_map.158 = (f32[24,128]{1,0:T(8,128)S(1)}, bf16[2048,128]{1,0:T(8,128)(2,1)S(1)}, bf16[32,256]{1,0:T(8,128)(2,1)S(1)}, bf16[16,128]{1,0:T(8,128)(2,1)S(1)}...) custom-call(f32[1,768]{1,0:T(1,128)} %bitcast.47, ...), custom_call_target="tpu_custom_call" | custom-call | flops 1000000 | bytes 1000000 | tf_op jit(solution)/shard_map/pallas_call | solution.py:502
  4.2 2.2 %all-gather = f32[48,128]{1,0:T(8,128)S(1)} all-gather(f32[24,128]{1,0:T(8,128)S(1)} %get-tuple-element.22), channel_id=2, replica_groups={{0,1},{2,3},{4,5},{6,7},{8,9},{10,11},{12,13},{14,15},{16,17},{18,19},{..., dimensions={0}, use_global_device_ids=true | all-gather | bytes 36864 | tf_op jit(solution)/shard_map/all_gather | solution.py:558
  6.4 11.6 %all-gather.1 = f32[4,24,128]{2,1,0:T(8,128)S(1)} all-gather(f32[2,24,128]{2,1,0:T(8,128)S(1)} %bitcast.32), channel_id=3, replica_groups={{0,2},{3,5},{4,6},{7,9},{8,10},{11,13},{12,14},{15,17},{16,18},{19,21},..., dimensions={0}, use_global_device_ids=true | all-gather | bytes 73728 | tf_op jit(solution)/shard_map/all_gather | solution.py:565
  18.0 1.9 %all-gather.2 = f32[4,2,24,128]{3,2,1,0:T(8,128)S(1)} all-gather(f32[2,2,24,128]{3,2,1,0:T(8,128)S(1)} %bitcast.40), channel_id=4, replica_groups={{0,1},{2,3},{4,5},{6,7},{8,9},{10,11},{12,13},{14,15},{16,17},{18,19},{..., dimensions={0}, use_global_device_ids=true | all-gather | bytes 147456 | tf_op jit(solution)/shard_map/all_gather | solution.py:558
  19.9 4.3 %shard_map.159 = f32[16,128]{1,0:T(8,128)S(1)} custom-call(f32[7,128]{1,0:T(8,128)S(1)} %broadcast_in_dim.12.where_ref, f32[2,24,128]{2,1,0:T(8,128)S(1)} %bitcast.33, f32[2,2,2,24,128]{4,3,2,1,0:T(8,128)S(1)} %bitcast.29, bf16[2048,128]{1,0:T(8,128)(2,1)S(1)} %get-tuple-element.23.up_ref, bf16[32,256]{1,0:T(8,128)(2,1)S(1)} %get-tuple-element.24.down_ref, ...), custom_call_target="tpu_custom_call" | custom-call | flops 1000000 | bytes 1000000 | tf_op jit(solution)/shard_map/pallas_call | solution.py:502
  24.2 1.8 %all-gather.3 = f32[32,128]{1,0:T(8,128)S(1)} all-gather(f32[16,128]{1,0:T(8,128)S(1)} %shard_map.159), channel_id=5, replica_groups={{0,1},{2,3},{4,5},{6,7},{8,9},{10,11},{12,13},{14,15},{16,17},{18,19},{..., dimensions={0}, use_global_device_ids=true | all-gather | bytes 24576 | tf_op jit(solution)/shard_map/all_gather | solution.py:558
  26.0 3.8 %all-gather.4 = f32[4,16,128]{2,1,0:T(8,128)S(1)} all-gather(f32[2,16,128]{2,1,0:T(8,128)S(1)} %bitcast.43), channel_id=6, replica_groups={{0,3},{1,2},{4,7},{5,6},{8,11},{9,10},{12,15},{13,14},{16,19},{17,18},{..., dimensions={0}, use_global_device_ids=true | all-gather | bytes 49152 | tf_op jit(solution)/shard_map/all_gather | solution.py:572
  29.8 4.6 %all-gather.5 = f32[4,2,16,128]{3,2,1,0:T(8,128)S(1)} all-gather(f32[2,2,16,128]{3,2,1,0:T(8,128)S(1)} %bitcast.41), channel_id=7, replica_groups={{0,4},{5,9},{2,6},{7,11},{8,12},{13,17},{10,14},{15,19},{16,20},{21,25}..., dimensions={0}, use_global_device_ids=true | all-gather | bytes 98304 | tf_op jit(solution)/shard_map/all_gather | solution.py:581
  34.4 1.9 %all-gather.6 = f32[4,2,2,16,128]{4,3,2,1,0:T(8,128)S(1)} all-gather(f32[2,2,2,16,128]{4,3,2,1,0:T(8,128)S(1)} %bitcast.39), channel_id=8, replica_groups={{0,1},{2,3},{4,5},{6,7},{8,9},{10,11},{12,13},{14,15},{16,17},{18,19},{..., dimensions={0}, use_global_device_ids=true | all-gather | bytes 196608 | tf_op jit(solution)/shard_map/all_gather | solution.py:558
  36.3 0.3 shard_map.160
  36.7 4.3 %shard_map.161 = f32[16,128]{1,0:T(8,128)S(1)} custom-call(f32[7,128]{1,0:T(8,128)S(1)} %broadcast_in_dim.12.where_ref, f32[2,24,128]{2,1,0:T(8,128)S(1)} %get-tuple-element.38.home_ref, f32[4,8,128]{2,1,0:T(8,128)S(1)} %get-tuple-element.39.far_ref, bf16[2048,128]{1,0:T(8,128)(2,1)S(1)} %get-tuple-element.23.up_ref, ...), custom_call_target="tpu_custom_call" | custom-call | flops 1000000 | bytes 1000000 | tf_op jit(solution)/shard_map/pallas_call | solution.py:502
  41.0 1.8 %all-gather.7 = f32[32,128]{1,0:T(8,128)S(1)} all-gather(f32[16,128]{1,0:T(8,128)S(1)} %shard_map.161), channel_id=9, replica_groups={{0,1},{2,3},{4,5},{6,7},{8,9},{10,11},{12,13},{14,15},{16,17},{18,19},{..., dimensions={0}, use_global_device_ids=true | all-gather | bytes 24576 | tf_op jit(solution)/shard_map/all_gather | solution.py:558
  42.8 5.3 %all-gather.8 = f32[4,8,128]{2,1,0:T(8,128)S(1)} all-gather(f32[2,8,128]{2,1,0:T(8,128)S(1)} %slice.4), channel_id=10, replica_groups={{0,2},{3,5},{4,6},{7,9},{8,10},{11,13},{12,14},{15,17},{16,18},{19,21},..., dimensions={0}, use_global_device_ids=true | all-gather | bytes 24576 | tf_op jit(solution)/shard_map/all_gather | solution.py:565
  48.1 1.8 %all-gather.9 = f32[4,2,8,128]{3,2,1,0:T(8,128)S(1)} all-gather(f32[2,2,8,128]{3,2,1,0:T(8,128)S(1)} %bitcast.44), channel_id=11, replica_groups={{0,1},{2,3},{4,5},{6,7},{8,9},{10,11},{12,13},{14,15},{16,17},{18,19},{..., dimensions={0}, use_global_device_ids=true | all-gather | bytes 49152 | tf_op jit(solution)/shard_map/all_gather | solution.py:558
  49.9 0.2 shard_map.162.own_ref
  50.1 6.4 %all-gather.10 = f32[4,16,128]{2,1,0:T(8,128)S(1)} all-gather(f32[2,16,128]{2,1,0:T(8,128)S(1)} %shard_map.162.own_ref), channel_id=12, replica_groups={{1,33},{32,64},{65,96},{97,129},{128,161},{160,192},{193,224},{225,257}..., dimensions={0}, use_global_device_ids=true | all-gather | bytes 49152 | tf_op jit(solution)/shard_map/all_gather | solution.py:601
  56.5 1.8 %all-gather.11 = f32[4,2,16,128]{3,2,1,0:T(8,128)S(1)} all-gather(f32[2,2,16,128]{3,2,1,0:T(8,128)S(1)} %bitcast.42), channel_id=13, replica_groups={{0,1},{2,3},{4,5},{6,7},{8,9},{10,11},{12,13},{14,15},{16,17},{18,19},{..., dimensions={0}, use_global_device_ids=true | all-gather | bytes 98304 | tf_op jit(solution)/shard_map/all_gather | solution.py:558
  58.4 0.6 %shard_map.163 = (f32[1,768]{1,0:T(1,128)}, f32[1,768]{1,0:T(1,128)}) custom-call(f32[7,128]{1,0:T(8,128)S(1)} %broadcast_in_dim.12.where_ref, f32[2,16,128]{2,1,0:T(8,128)S(1)} %shard_map.162.own_ref, f32[2,2,2,16,128]{4,3,2,1,0:T(8,128)S(1)} %bitcast.35), custom_call_target="tpu_custom_call" | custom-call | flops 1000000 | bytes 1000000 | tf_op jit(solution)/shard_map/pallas_call | solution.py:502
  (1 shorter events, 0.0 us)

commit v10 on v9

--- a/solution.py
+++ b/solution.py
@@ -565,11 +565,10 @@
     return lax.all_gather(value, "space", axis_index_groups=groups)
 
 
-def across_pair(value, domains):
-    groups = []
-    for i in range(domains // 4):
-        groups += [[4 * i, 4 * i + 3], [4 * i + 1, 4 * i + 2]]
-    return lax.all_gather(value, "space", axis_index_groups=groups)
+def in_pair(value, domains):
+    groups = [[4 * i + k for k in range(4)] for i in range(domains // 4)]
+    whole = lax.all_gather(value, "space", axis_index_groups=groups)
+    return whole.reshape((2, 2) + value.shape)
 
 
 def between_pairs(value, domains):
@@ -655,13 +654,13 @@
     far = on_chip(across_chips(home, domains), domains)
     for step in range(STEPS):
         partial = call(force_kernel, (), (where_to, home, far, *fixed), tiles(16), force_scratch())
-        near = on_chip(partial, domains)
         if step < STEPS - 1:
-            pair = across_pair(near, domains)
+            pair = in_pair(partial, domains)
             wide = on_chip(between_pairs(pair, domains), domains)
             shapes = [tiles(2, 24), tiles(4, 8)]
             home, far = call(step_kernel, (), (where_to, home, far, wide), shapes)
         else:
+            near = on_chip(partial, domains)
             far = on_chip(across_chips(near[:, GHOSTS], domains), domains)
             state = call(last_kernel, (), (where_to, home, near, far), tiles(2, 16))
     mates = on_chip(along_ladder(state, rungs, domains), domains)

time: 59.3 us -> 58.8 us (level)
    all_gather x7 -> x6, blocking collectives: 13.2 us -> 11.4 us  [on_chip(): return lax.all_gather(value, 'space', axis_index_groups=groups)]
    all_gather x1, blocking collectives: 3.83 us -> 5.16 us  [in_pair(): whole = lax.all_gather(value, 'space', axis_index_groups=groups)]
where the time goes in v10:
time: 58.8 us; the launch traced here: 58.5 us
  blocking collectives  44.6 us (76%)
  Pallas kernels  11.7 us (20%)
  between operations  2.05 us (3%)
    all_gather x2, blocking collectives, across_chips(): return lax.all_gather(value, 'space', axis_index_groups=groups)  16.9 us
    pallas_call x6, Pallas kernels, call(): pl.pallas_call(kernel, out_shape=out_shape, in_specs=[smem()] * len(scala...  11.7 us
    all_gather x6, blocking collectives, on_chip(): return lax.all_gather(value, 'space', axis_index_groups=groups)  11.4 us
    all_gather x1, blocking collectives, along_ladder(): return lax.all_gather(value, ('replica', 'space'), axis_index_groups=groups)  6.45 us
    all_gather x1, blocking collectives, in_pair(): whole = lax.all_gather(value, 'space', axis_index_groups=groups)  5.16 us
    all_gather x1, blocking collectives, between_pairs(): return lax.all_gather(value, 'space', axis_index_groups=groups)  4.64 us

profile of v10, /device:TPU:7, one launch (start us, length us, event | category | flops | bytes accessed | tf_op | source)
XLA Modules:
  0.0 58.5 jit_solution(5137537823308873337)
XLA Ops:
  2.0 0.1 stack.31
  2.1 0.1 broadcast_in_dim.12.where_ref
  2.2 2.0 %shard_map.158 = (f32[24,128]{1,0:T(8,128)S(1)}, bf16[2048,128]{1,0:T(8,128)(2,1)S(1)}, bf16[32,256]{1,0:T(8,128)(2,1)S(1)}, bf16[16,128]{1,0:T(8,128)(2,1)S(1)}...) custom-call(f32[1,768]{1,0:T(1,128)} %bitcast.43, ...), custom_call_target="tpu_custom_call" | custom-call | flops 1000000 | bytes 1000000 | tf_op jit(solution)/shard_map/pallas_call | solution.py:502
  4.2 2.2 %all-gather = f32[48,128]{1,0:T(8,128)S(1)} all-gather(f32[24,128]{1,0:T(8,128)S(1)} %get-tuple-element.22), channel_id=2, replica_groups={{0,1},{2,3},{4,5},{6,7},{8,9},{10,11},{12,13},{14,15},{16,17},{18,19},{..., dimensions={0}, use_global_device_ids=true | all-gather | bytes 36864 | tf_op jit(solution)/shard_map/all_gather | solution.py:558
  6.4 11.6 %all-gather.1 = f32[4,24,128]{2,1,0:T(8,128)S(1)} all-gather(f32[2,24,128]{2,1,0:T(8,128)S(1)} %bitcast.30), channel_id=3, replica_groups={{0,2},{3,5},{4,6},{7,9},{8,10},{11,13},{12,14},{15,17},{16,18},{19,21},..., dimensions={0}, use_global_device_ids=true | all-gather | bytes 73728 | tf_op jit(solution)/shard_map/all_gather | solution.py:565
  18.0 1.9 %all-gather.2 = f32[4,2,24,128]{3,2,1,0:T(8,128)S(1)} all-gather(f32[2,2,24,128]{3,2,1,0:T(8,128)S(1)} %bitcast.37), channel_id=4, replica_groups={{0,1},{2,3},{4,5},{6,7},{8,9},{10,11},{12,13},{14,15},{16,17},{18,19},{..., dimensions={0}, use_global_device_ids=true | all-gather | bytes 147456 | tf_op jit(solution)/shard_map/all_gather | solution.py:558
  19.9 4.3 %shard_map.159 = f32[16,128]{1,0:T(8,128)S(1)} custom-call(f32[7,128]{1,0:T(8,128)S(1)} %broadcast_in_dim.12.where_ref, f32[2,24,128]{2,1,0:T(8,128)S(1)} %bitcast.31, f32[2,2,2,24,128]{4,3,2,1,0:T(8,128)S(1)} %bitcast.27, bf16[2048,128]{1,0:T(8,128)(2,1)S(1)} %get-tuple-element.23.up_ref, bf16[32,256]{1,0:T(8,128)(2,1)S(1)} %get-tuple-element.24.down_ref, ...), custom_call_target="tpu_custom_call" | custom-call | flops 1000000 | bytes 1000000 | tf_op jit(solution)/shard_map/pallas_call | solution.py:502
  24.2 5.2 %all-gather.3 = f32[64,128]{1,0:T(8,128)S(1)} all-gather(f32[16,128]{1,0:T(8,128)S(1)} %shard_map.159), channel_id=5, replica_groups={{0,1,2,3},{4,5,6,7},{8,9,10,11},{12,13,14,15},{16,17,18,19},{20,21,22,2..., dimensions={0}, use_global_device_ids=true | all-gather | bytes 40960 | tf_op jit(solution)/shard_map/all_gather | solution.py:570
  29.3 4.6 %all_gather.71 = f32[2,2,2,16,128]{4,3,2,1,0:T(8,128)S(1)} all-gather(f32[1,2,2,16,128]{4,3,2,1,0:T(8,128)S(1)} %bitcast.38), channel_id=1, replica_groups={{0,4},{5,9},{2,6},{7,11},{8,12},{13,17},{10,14},{15,19},{16,20},{21,25}..., dimensions={0}, use_global_device_ids=true | all-gather | bytes 98304 | tf_op jit(solution)/shard_map/all_gather | solution.py:580
  34.0 1.9 %all-gather.4 = f32[4,2,2,16,128]{4,3,2,1,0:T(8,128)S(1)} all-gather(f32[2,2,2,16,128]{4,3,2,1,0:T(8,128)S(1)} %all_gather.71), channel_id=6, replica_groups={{0,1},{2,3},{4,5},{6,7},{8,9},{10,11},{12,13},{14,15},{16,17},{18,19},{..., dimensions={0}, use_global_device_ids=true | all-gather | bytes 196608 | tf_op jit(solution)/shard_map/all_gather | solution.py:558
  35.9 0.3 shard_map.160
  36.2 4.3 %shard_map.161 = f32[16,128]{1,0:T(8,128)S(1)} custom-call(f32[7,128]{1,0:T(8,128)S(1)} %broadcast_in_dim.12.where_ref, f32[2,24,128]{2,1,0:T(8,128)S(1)} %get-tuple-element.38.home_ref, f32[4,8,128]{2,1,0:T(8,128)S(1)} %get-tuple-element.39.far_ref, bf16[2048,128]{1,0:T(8,128)(2,1)S(1)} %get-tuple-element.23.up_ref, ...), custom_call_target="tpu_custom_call" | custom-call | flops 1000000 | bytes 1000000 | tf_op jit(solution)/shard_map/pallas_call | solution.py:502
  40.5 1.8 %all-gather.5 = f32[32,128]{1,0:T(8,128)S(1)} all-gather(f32[16,128]{1,0:T(8,128)S(1)} %shard_map.161), channel_id=7, replica_groups={{0,1},{2,3},{4,5},{6,7},{8,9},{10,11},{12,13},{14,15},{16,17},{18,19},{..., dimensions={0}, use_global_device_ids=true | all-gather | bytes 24576 | tf_op jit(solution)/shard_map/all_gather | solution.py:558
  42.3 5.3 %all-gather.6 = f32[4,8,128]{2,1,0:T(8,128)S(1)} all-gather(f32[2,8,128]{2,1,0:T(8,128)S(1)} %slice.4), channel_id=8, replica_groups={{0,2},{3,5},{4,6},{7,9},{8,10},{11,13},{12,14},{15,17},{16,18},{19,21},..., dimensions={0}, use_global_device_ids=true | all-gather | bytes 24576 | tf_op jit(solution)/shard_map/all_gather | solution.py:565
  47.6 1.8 %all-gather.7 = f32[4,2,8,128]{3,2,1,0:T(8,128)S(1)} all-gather(f32[2,2,8,128]{3,2,1,0:T(8,128)S(1)} %bitcast.40), channel_id=9, replica_groups={{0,1},{2,3},{4,5},{6,7},{8,9},{10,11},{12,13},{14,15},{16,17},{18,19},{..., dimensions={0}, use_global_device_ids=true | all-gather | bytes 49152 | tf_op jit(solution)/shard_map/all_gather | solution.py:558
  49.5 0.2 shard_map.162.own_ref
  49.6 6.4 %all-gather.8 = f32[4,16,128]{2,1,0:T(8,128)S(1)} all-gather(f32[2,16,128]{2,1,0:T(8,128)S(1)} %shard_map.162.own_ref), channel_id=10, replica_groups={{1,33},{32,64},{65,96},{97,129},{128,161},{160,192},{193,224},{225,257}..., dimensions={0}, use_global_device_ids=true | all-gather | bytes 49152 | tf_op jit(solution)/shard_map/all_gather | solution.py:600
  56.1 1.8 %all-gather.9 = f32[4,2,16,128]{3,2,1,0:T(8,128)S(1)} all-gather(f32[2,2,16,128]{3,2,1,0:T(8,128)S(1)} %bitcast.39), channel_id=11, replica_groups={{0,1},{2,3},{4,5},{6,7},{8,9},{10,11},{12,13},{14,15},{16,17},{18,19},{..., dimensions={0}, use_global_device_ids=true | all-gather | bytes 98304 | tf_op jit(solution)/shard_map/all_gather | solution.py:558
  57.9 0.6 %shard_map.163 = (f32[1,768]{1,0:T(1,128)}, f32[1,768]{1,0:T(1,128)}) custom-call(f32[7,128]{1,0:T(8,128)S(1)} %broadcast_in_dim.12.where_ref, f32[2,16,128]{2,1,0:T(8,128)S(1)} %shard_map.162.own_ref, f32[2,2,2,16,128]{4,3,2,1,0:T(8,128)S(1)} %bitcast.33), custom_call_target="tpu_custom_call" | custom-call | flops 1000000 | bytes 1000000 | tf_op jit(solution)/shard_map/pallas_call | solution.py:502
  (1 shorter events, 0.0 us)

commit v11 on v10

--- a/solution.py
+++ b/solution.py
@@ -91,17 +91,6 @@
     return parts
 
 
-def bring(sources, targets, sems):
-    copies = [
-        pltpu.make_async_copy(source, target, sems.at[k])
-        for k, (source, target) in enumerate(zip(sources, targets))
-    ]
-    for copy in copies:
-        copy.start()
-    for copy in copies:
-        copy.wait()
-
-
 def fed_columns():
     feature = lax.broadcasted_iota(jnp.int32, (28, LANES), 0)
     col = lax.broadcasted_iota(jnp.int32, (28, LANES), 1)
@@ -136,7 +125,30 @@
         x_ref, v_ref, kind_ref, border_ref, inertia_ref, index_ref, place_ref, total_ref,
         intake_ref, edge_out_ref, opening_ref, middle_ref, atom_out_ref,
     )
-    bring(inputs, landed, refs[8])
+    copies = [
+        pltpu.make_async_copy(source, target, refs[8].at[k])
+        for k, (source, target) in enumerate(zip(inputs, landed))
+    ]
+    indices = copies.pop(5)
+    indices.start()
+    for copy in copies:
+        copy.start()
+    indices.wait()
+    place = lax.broadcasted_iota(jnp.int32, (LANES, 2 * LANES), 0).astype(F32).astype(BF16)
+    one, none = jnp.asarray(1.0, BF16), jnp.asarray(0.0, BF16)
+
+    def group(s, carry):
+        for j in range(8):
+            lane = (index_ref[0, pl.ds(s * 8 + j, 1), :] & (LANES - 1)).astype(F32)
+            lane = jnp.broadcast_to(lane, (16, 2 * LANES)).astype(BF16)
+            lane = jnp.concatenate([lane] * (LANES // 16), axis=0)
+            cols = pl.ds(pl.multiple_of((s * 8 + j) * 2 * LANES, 2 * LANES), 2 * LANES)
+            hot_ref[:, cols] = jnp.where(place == lane, one, none)
+        return carry
+
+    lax.fori_loop(0, GROUPS, group, 0)
+    for copy in copies:
+        copy.wait()
 
     x_tile = tile_of(x_ref)
     border = border_ref[0]
@@ -154,19 +166,6 @@
     out_ref[22:23] = border0.astype(F32)
     out_ref[23:24] = border1.astype(F32)
 
-    place = lax.broadcasted_iota(jnp.int32, (LANES, 2 * LANES), 0).astype(F32).astype(BF16)
-    one, none = jnp.asarray(1.0, BF16), jnp.asarray(0.0, BF16)
-
-    def group(s, carry):
-        for j in range(8):
-            lane = (index_ref[0, pl.ds(s * 8 + j, 1), :] & (LANES - 1)).astype(F32)
-            lane = jnp.broadcast_to(lane, (16, 2 * LANES)).astype(BF16)
-            lane = jnp.concatenate([lane] * (LANES // 16), axis=0)
-            cols = pl.ds(pl.multiple_of((s * 8 + j) * 2 * LANES, 2 * LANES), 2 * LANES)
-            hot_ref[:, cols] = jnp.where(place == lane, one, none)
-        return carry
-
-    lax.fori_loop(0, GROUPS, group, 0)
     intake = intake_ref[...]
     fed = fed_columns()
     for j in range(8):
@@ -477,10 +476,15 @@
 
     mine = of_core(own_ref)
     chosen = jnp.where(swaps, mine, jnp.where(side, of_side(0), of_side(1)))
+    put_flat(x_ref, chosen[0:6])
+    x_copy = pltpu.make_async_copy(x_ref, x_out, sems.at[0])
+    x_copy.start()
     scale = jnp.sqrt(mine[6:7] / chosen[6:7])
-    put_flat(x_ref, chosen[0:6])
     put_flat(v_ref, chosen[8:14] * scale)
-    bring((x_ref, v_ref), (x_out, v_out), sems)
+    v_copy = pltpu.make_async_copy(v_ref, v_out, sems.at[1])
+    v_copy.start()
+    x_copy.wait()
+    v_copy.wait()
 
 
 def vmem():

time: 58.8 us -> 58.4 us (level)
  no operation moved by 1% of the time
where the time goes in v11:
time: 58.4 us; the launch traced here: 58.2 us
  blocking collectives  44.6 us (76%)
  Pallas kernels  11.4 us (20%)
  between operations  2.05 us (4%)
    all_gather x2, blocking collectives, across_chips(): return lax.all_gather(value, 'space', axis_index_groups=groups)  16.9 us
    all_gather x6, blocking collectives, on_chip(): return lax.all_gather(value, 'space', axis_index_groups=groups)  11.4 us
    pallas_call x6, Pallas kernels, call(): pl.pallas_call(kernel, out_shape=out_shape, in_specs=[smem()] * len(scala...  11.4 us
    all_gather x1, blocking collectives, along_ladder(): return lax.all_gather(value, ('replica', 'space'), axis_index_groups=groups)  6.45 us
    all_gather x1, blocking collectives, in_pair(): whole = lax.all_gather(value, 'space', axis_index_groups=groups)  5.16 us
    all_gather x1, blocking collectives, between_pairs(): return lax.all_gather(value, 'space', axis_index_groups=groups)  4.64 us

profile of v11, /device:TPU:7, one launch (start us, length us, event | category | flops | bytes accessed | tf_op | source)
XLA Modules:
  0.0 58.2 jit_solution(6562497542702491480)
XLA Ops:
  2.0 0.1 stack.31
  2.1 0.1 broadcast_in_dim.12.where_ref
  2.2 1.6 %shard_map.158 = (f32[24,128]{1,0:T(8,128)S(1)}, bf16[2048,128]{1,0:T(8,128)(2,1)S(1)}, bf16[32,256]{1,0:T(8,128)(2,1)S(1)}, bf16[16,128]{1,0:T(8,128)(2,1)S(1)}...) custom-call(f32[1,768]{1,0:T(1,128)} %bitcast.43, ...), custom_call_target="tpu_custom_call" | custom-call | flops 1000000 | bytes 1000000 | tf_op jit(solution)/shard_map/pallas_call | solution.py:506
  3.8 2.2 %all-gather = f32[48,128]{1,0:T(8,128)S(1)} all-gather(f32[24,128]{1,0:T(8,128)S(1)} %get-tuple-element.22), channel_id=2, replica_groups={{0,1},{2,3},{4,5},{6,7},{8,9},{10,11},{12,13},{14,15},{16,17},{18,19},{..., dimensions={0}, use_global_device_ids=true | all-gather | bytes 36864 | tf_op jit(solution)/shard_map/all_gather | solution.py:562
  6.0 11.6 %all-gather.1 = f32[4,24,128]{2,1,0:T(8,128)S(1)} all-gather(f32[2,24,128]{2,1,0:T(8,128)S(1)} %bitcast.30), channel_id=3, replica_groups={{0,2},{3,5},{4,6},{7,9},{8,10},{11,13},{12,14},{15,17},{16,18},{19,21},..., dimensions={0}, use_global_device_ids=true | all-gather | bytes 73728 | tf_op jit(solution)/shard_map/all_gather | solution.py:569
  17.6 1.9 %all-gather.2 = f32[4,2,24,128]{3,2,1,0:T(8,128)S(1)} all-gather(f32[2,2,24,128]{3,2,1,0:T(8,128)S(1)} %bitcast.37), channel_id=4, replica_groups={{0,1},{2,3},{4,5},{6,7},{8,9},{10,11},{12,13},{14,15},{16,17},{18,19},{..., dimensions={0}, use_global_device_ids=true | all-gather | bytes 147456 | tf_op jit(solution)/shard_map/all_gather | solution.py:562
  19.5 4.3 %shard_map.159 = f32[16,128]{1,0:T(8,128)S(1)} custom-call(f32[7,128]{1,0:T(8,128)S(1)} %broadcast_in_dim.12.where_ref, f32[2,24,128]{2,1,0:T(8,128)S(1)} %bitcast.31, f32[2,2,2,24,128]{4,3,2,1,0:T(8,128)S(1)} %bitcast.27, bf16[2048,128]{1,0:T(8,128)(2,1)S(1)} %get-tuple-element.23.up_ref, bf16[32,256]{1,0:T(8,128)(2,1)S(1)} %get-tuple-element.24.down_ref, ...), custom_call_target="tpu_custom_call" | custom-call | flops 1000000 | bytes 1000000 | tf_op jit(solution)/shard_map/pallas_call | solution.py:506
  23.8 5.2 %all-gather.3 = f32[64,128]{1,0:T(8,128)S(1)} all-gather(f32[16,128]{1,0:T(8,128)S(1)} %shard_map.159), channel_id=5, replica_groups={{0,1,2,3},{4,5,6,7},{8,9,10,11},{12,13,14,15},{16,17,18,19},{20,21,22,2..., dimensions={0}, use_global_device_ids=true | all-gather | bytes 40960 | tf_op jit(solution)/shard_map/all_gather | solution.py:574
  29.0 4.6 %all_gather.71 = f32[2,2,2,16,128]{4,3,2,1,0:T(8,128)S(1)} all-gather(f32[1,2,2,16,128]{4,3,2,1,0:T(8,128)S(1)} %bitcast.38), channel_id=1, replica_groups={{0,4},{5,9},{2,6},{7,11},{8,12},{13,17},{10,14},{15,19},{16,20},{21,25}..., dimensions={0}, use_global_device_ids=true | all-gather | bytes 98304 | tf_op jit(solution)/shard_map/all_gather | solution.py:584
  33.6 1.9 %all-gather.4 = f32[4,2,2,16,128]{4,3,2,1,0:T(8,128)S(1)} all-gather(f32[2,2,2,16,128]{4,3,2,1,0:T(8,128)S(1)} %all_gather.71), channel_id=6, replica_groups={{0,1},{2,3},{4,5},{6,7},{8,9},{10,11},{12,13},{14,15},{16,17},{18,19},{..., dimensions={0}, use_global_device_ids=true | all-gather | bytes 196608 | tf_op jit(solution)/shard_map/all_gather | solution.py:562
  35.5 0.3 shard_map.160
  35.8 4.3 %shard_map.161 = f32[16,128]{1,0:T(8,128)S(1)} custom-call(f32[7,128]{1,0:T(8,128)S(1)} %broadcast_in_dim.12.where_ref, f32[2,24,128]{2,1,0:T(8,128)S(1)} %get-tuple-element.38.home_ref, f32[4,8,128]{2,1,0:T(8,128)S(1)} %get-tuple-element.39.far_ref, bf16[2048,128]{1,0:T(8,128)(2,1)S(1)} %get-tuple-element.23.up_ref, ...), custom_call_target="tpu_custom_call" | custom-call | flops 1000000 | bytes 1000000 | tf_op jit(solution)/shard_map/pallas_call | solution.py:506
  40.1 1.8 %all-gather.5 = f32[32,128]{1,0:T(8,128)S(1)} all-gather(f32[16,128]{1,0:T(8,128)S(1)} %shard_map.161), channel_id=7, replica_groups={{0,1},{2,3},{4,5},{6,7},{8,9},{10,11},{12,13},{14,15},{16,17},{18,19},{..., dimensions={0}, use_global_device_ids=true | all-gather | bytes 24576 | tf_op jit(solution)/shard_map/all_gather | solution.py:562
  42.0 5.3 %all-gather.6 = f32[4,8,128]{2,1,0:T(8,128)S(1)} all-gather(f32[2,8,128]{2,1,0:T(8,128)S(1)} %slice.4), channel_id=8, replica_groups={{0,2},{3,5},{4,6},{7,9},{8,10},{11,13},{12,14},{15,17},{16,18},{19,21},..., dimensions={0}, use_global_device_ids=true | all-gather | bytes 24576 | tf_op jit(solution)/shard_map/all_gather | solution.py:569
  47.3 1.8 %all-gather.7 = f32[4,2,8,128]{3,2,1,0:T(8,128)S(1)} all-gather(f32[2,2,8,128]{3,2,1,0:T(8,128)S(1)} %bitcast.40), channel_id=9, replica_groups={{0,1},{2,3},{4,5},{6,7},{8,9},{10,11},{12,13},{14,15},{16,17},{18,19},{..., dimensions={0}, use_global_device_ids=true | all-gather | bytes 49152 | tf_op jit(solution)/shard_map/all_gather | solution.py:562
  49.1 0.2 shard_map.162.own_ref
  49.3 6.4 %all-gather.8 = f32[4,16,128]{2,1,0:T(8,128)S(1)} all-gather(f32[2,16,128]{2,1,0:T(8,128)S(1)} %shard_map.162.own_ref), channel_id=10, replica_groups={{1,33},{32,64},{65,96},{97,129},{128,161},{160,192},{193,224},{225,257}..., dimensions={0}, use_global_device_ids=true | all-gather | bytes 49152 | tf_op jit(solution)/shard_map/all_gather | solution.py:604
  55.7 1.8 %all-gather.9 = f32[4,2,16,128]{3,2,1,0:T(8,128)S(1)} all-gather(f32[2,2,16,128]{3,2,1,0:T(8,128)S(1)} %bitcast.39), channel_id=11, replica_groups={{0,1},{2,3},{4,5},{6,7},{8,9},{10,11},{12,13},{14,15},{16,17},{18,19},{..., dimensions={0}, use_global_device_ids=true | all-gather | bytes 98304 | tf_op jit(solution)/shard_map/all_gather | solution.py:562
  57.5 0.6 %shard_map.163 = (f32[1,768]{1,0:T(1,128)}, f32[1,768]{1,0:T(1,128)}) custom-call(f32[7,128]{1,0:T(8,128)S(1)} %broadcast_in_dim.12.where_ref, f32[2,16,128]{2,1,0:T(8,128)S(1)} %shard_map.162.own_ref, f32[2,2,2,16,128]{4,3,2,1,0:T(8,128)S(1)} %bitcast.33), custom_call_target="tpu_custom_call" | custom-call | flops 1000000 | bytes 1000000 | tf_op jit(solution)/shard_map/pallas_call | solution.py:506
  (1 shorter events, 0.0 us)
